TPU v7x, 32 devices: a whole 2x2x4 slice. The times are simulated.
32 devices in a mesh: dp: 4 (over z), expert: 8 (over y, x, core).
Axes of the slice: x: 2, y: 2, z: 4, core: 2. Of those that a mesh axis runs over, the one named last changes fastest.
Arguments:
- cotangent: bfloat16 [4096, 2048], P(('dp', 'expert')), may hold values from -6 to 6
- saved_gate_up: bfloat16 [4096, 8, 1536], P(('dp', 'expert')), may hold values from -6 to 6
- route_ids: int32 [4096, 8], P(('dp', 'expert')), may hold values from 0 to 15, all different within a row; in each aligned block of 128 rows (0 to 127, 128 to 255, ...) at most 128 rows name the same one
- route_weights: float32 [4096, 8], P(('dp', 'expert')), may hold values from 0.05 to 1
- w_down: bfloat16 [16, 768, 2048], P('expert', 'dp'), may hold values from -0.21875 to 0.21875
Outputs:
- grad_gate_up: bfloat16 [4096, 8, 1536], P(('dp', 'expert'))
- route_grad: float32 [4096, 8], P(('dp', 'expert'))
- grad_down: float32 [16, 768, 2048], P('expert', 'dp')
Inputs may be any that keep to these rules, and one draw needn't show every extreme that they name: `route_ids`: within the rows of one device (aligned blocks of 128 tokens), no expert is named by more than 128 routes, and in every draw some expert is named by exactly 128; the 8 experts of a token are distinct.
All inputs are finite; a program needn't handle non-finite values.
Results may differ from a plain program's by a relative error of at most 0.02.
Values may be sent and summed in bfloat16 or wider, within the bound.
No kernel may reach another device: no remote copies, remote signals or barrier semaphores. Data moves between devices by JAX's collectives and lax.ppermute only.
A program may use at most 128 MiB of HBM per device.

v0:
```python
import jax
import jax.numpy as jnp
from jax import lax
from jax.sharding import PartitionSpec as P


def slot_positions(flat_ids, experts, capacity):
    onehot = (flat_ids[:, None] == jnp.arange(experts, dtype=jnp.int32)[None, :]).astype(jnp.int32)
    before = jnp.cumsum(onehot, axis=0) - onehot
    slot = jnp.sum(before * onehot, axis=1)
    return flat_ids * capacity + slot


def local(cotangent, saved_gate_up, route_ids, route_weights, w_down):
    tokens, top = route_ids.shape
    width = cotangent.shape[1]
    hidden_units = saved_gate_up.shape[2] // 2
    owners = lax.axis_size("expert")
    local_experts = w_down.shape[0]
    experts = local_experts * owners
    capacity = min(tokens, 2 * tokens * top // experts)
    routes = tokens * top
    gate = saved_gate_up[:, :, :hidden_units].astype(jnp.float32)
    up = saved_gate_up[:, :, hidden_units:].astype(jnp.float32)
    sig = jax.nn.sigmoid(gate)
    act = gate * sig
    hidden = (act * up).astype(jnp.bfloat16)
    weights = route_weights[:, :, None]
    scaled = (weights * hidden.astype(jnp.float32)).astype(jnp.bfloat16)
    flat_ids = route_ids.reshape(routes)
    position = slot_positions(flat_ids, experts, capacity)
    source = (
        jnp.full((experts * capacity,), routes, jnp.int32)
        .at[position]
        .set(jnp.arange(routes, dtype=jnp.int32))
    )
    dy_rows = jnp.concatenate([cotangent, jnp.zeros((1, width), cotangent.dtype)], 0)[source // top]
    h_rows = jnp.concatenate(
        [scaled.reshape(routes, hidden_units), jnp.zeros((1, hidden_units), jnp.bfloat16)], 0
    )[source]
    dy_send = dy_rows.reshape(owners, local_experts, capacity, width)
    h_send = h_rows.reshape(owners, local_experts, capacity, hidden_units)
    full_down = lax.all_gather(w_down, "dp", axis=1, tiled=True)
    dy_recv, h_recv = (
        lax.all_to_all(dy_send, "expert", split_axis=0, concat_axis=2, tiled=True),
        lax.all_to_all(h_send, "expert", split_axis=0, concat_axis=2, tiled=True),
    )
    dy_recv = dy_recv[0]
    h_recv = h_recv[0]
    grads = jnp.einsum(
        "jsd,jfd->jsf", dy_recv, full_down, preferred_element_type=jnp.float32
    ).astype(jnp.bfloat16)
    back = lax.all_to_all(
        grads.reshape(1, local_experts, owners * capacity, hidden_units),
        "expert",
        split_axis=2,
        concat_axis=0,
        tiled=True,
    )
    summed = lax.psum_scatter(
        jnp.einsum("jsn,jsd->njd", h_recv, dy_recv, preferred_element_type=jnp.float32).astype(
            jnp.bfloat16
        ),
        "dp",
        scatter_dimension=0,
        tiled=True,
    ).astype(jnp.float32)
    grad_down = jnp.transpose(summed, (1, 0, 2))
    returned_rows = back.reshape(experts * capacity, hidden_units)[position]
    qf = returned_rows.reshape(tokens, top, hidden_units).astype(jnp.float32)
    route_grad = jnp.sum(qf * hidden.astype(jnp.float32), -1)
    d_hidden = weights * qf
    d_gate = d_hidden * up * sig * (1.0 + gate * (1.0 - sig))
    d_up = d_hidden * act
    grad_gate_up = jnp.concatenate([d_gate, d_up], -1).astype(jnp.bfloat16)
    return (grad_gate_up, route_grad, grad_down)


def solution(mesh):
    return jax.shard_map(
        local,
        mesh=mesh,
        in_specs=(
            P(("dp", "expert"), None),
            P(("dp", "expert"), None, None),
            P(("dp", "expert"), None),
            P(("dp", "expert"), None),
            P("expert", "dp", None),
        ),
        out_specs=(
            P(("dp", "expert"), None, None),
            P(("dp", "expert"), None),
            P("expert", "dp", None),
        ),
        check_vma=False,
    )
```

profile of v0, /device:TPU:0, one launch (start us, length us, event | category | flops | bytes accessed | tf_op | source)
XLA Modules:
  0.0 531.2 jit_solution(17813649203675663712)
XLA Ops:
  7.2 0.0 all-gather.2.cloned.1.call-start
  7.2 0.7 all-gather.2.cloned.1.call-update
  7.9 0.8 copy.29
  8.7 0.1 eq.29
  8.8 0.1 eq.25
  8.9 0.7 broadcast_multiply_fusion
  9.6 0.1 copy.28
  9.7 0.1 mul.60
  9.8 4.5 reduce-window.6
  14.3 0.1 slice.22
  14.4 0.1 copy.31
  14.5 0.1 copy.32
  14.6 1.1 concatenate.10
  15.7 0.1 broadcast_add_fusion
  15.9 4.3 scatter_custom_fusion
  20.2 11.0 %gather_fusion = bf16[2048,2048]{1,0:T(8,128)(2,1)} fusion(bf16[129,2048]{1,0:T(8,128)(2,1)S(1)} %concatenate.10, s32[2048]{0:T(1024)S(1)} %get-tuple-element.19), kind=kCustom, calls=%fused_computation | custom fusion | bytes 16785408 | tf_op jit(solution)/shard_map/gather | solution.py:37
  31.2 100.4 %all_to_all.45 = bf16[8,2,128,2048]{3,2,1,0:T(8,128)(2,1)} all-to-all(bf16[8,2,128,2048]{3,2,1,0:T(8,128)(2,1)} %bitcast.53), channel_id=1, replica_groups=mesh['dp'=4,'expert'=8] {'expert'}, dimensions={0} | all-to-all | bytes 16777216 | tf_op jit(solution)/shard_map/all_to_all | solution.py:45
  131.6 8.3 %copy.33 = bf16[1,2,8,128,2048]{4,3,2,1,0:T(8,128)(2,1)} copy(bf16[1,2,8,128,2048]{4,3,1,2,0:T(8,128)(2,1)} %bitcast.54) | data formatting | bytes 16777216 | tf_op jit(solution)/shard_map/all_to_all | solution.py:45
  139.9 0.0 all-gather.2.cloned.1.call-done
  139.9 11.0 %convert_bitcast_fusion.2 = bf16[1,2,1024,768]{3,2,1,0:T(8,128)(2,1)S(1)} fusion(bf16[2,1024,2048]{2,1,0:T(8,128)(2,1)} %bitcast.58, bf16[2,768,2048]{2,1,0:T(8,128)(2,1)} %all-gather.2.cloned.1.call-done), kind=kOutput, calls=%fused_computation.27 | convolution fusion | flops 6444023808 | bytes 17825792 | tf_op jit(solution)/shard_map/jsd,jfd->jsf/dot_general | solution.py:50
  150.9 4.9 copy.34
  155.8 0.0 copy-start.2
  155.8 3.8 all-to-all-start.1
  159.6 0.2 all-reduce.5.cloned.1.call-start
  159.8 0.0 copy-done.2
  159.8 0.1 copy.27
  159.9 37.5 %all-to-all-done.1 = bf16[1,2,1024,768]{3,1,0,2:T(2,128)(2,1)S(1)} async-done(((bf16[1,2,1024,768]{3,1,0,2:T(2,128)(2,1)}), bf16[1,2,1024,768]{3,1,0,2:T(2,128)(2,1)S(1)}, u32[]{:S(2)}, u32[]{:S(2)}) %all-to-all-start.1) | async-done | bytes 3145760 | tf_op jit(solution)/shard_map/all_to_all | solution.py:53
  197.4 0.0 copy-start.1
  197.4 1.7 copy-done.1
  199.0 2.4 copy.35
  201.5 5.2 gather_fusion.1
  206.7 5.0 fusion.12
  211.7 0.1 concatenate.12
  211.8 9.4 %gather_fusion.2 = bf16[2048,768]{1,0:T(8,128)(2,1)} fusion(bf16[1025,768]{1,0:T(8,128)(2,1)S(1)} %concatenate.12, s32[2048]{0:T(1024)S(1)} %get-tuple-element.18), kind=kCustom, calls=%fused_computation.2 | custom fusion | bytes 6299648 | tf_op jit(solution)/shard_map/gather | solution.py:38
  221.2 41.4 %all_to_all.46 = bf16[8,2,128,768]{3,2,1,0:T(8,128)(2,1)S(1)} all-to-all(bf16[8,2,128,768]{3,2,1,0:T(8,128)(2,1)} %bitcast.57), channel_id=1, replica_groups=mesh['dp'=4,'expert'=8] {'expert'}, dimensions={0} | all-to-all | bytes 6291456 | tf_op jit(solution)/shard_map/all_to_all | solution.py:46
  262.6 0.2 copy.36
  262.8 15.2 %convert_bitcast_fusion = bf16[768,2,2048]{0,2,1:T(8,128)(2,1)} fusion(bf16[2,1024,2048]{2,1,0:T(8,128)(2,1)} %bitcast.59, bf16[2,1024,768]{2,1,0:T(8,128)(2,1)S(1)} %bitcast.60), kind=kOutput, calls=%fused_computation.4 | convolution fusion | flops 6445596672 | bytes 17825792 | tf_op jit(solution)/shard_map/jsn,jsd->njd/dot_general | solution.py:61
  278.0 16.4 %copy.38 = bf16[768,2,2048]{2,1,0:T(2,128)(2,1)} copy(bf16[768,2,2048]{0,2,1:T(8,128)(2,1)} %convert_bitcast_fusion) | data formatting | bytes 12582912 | tf_op jit(solution)/shard_map/convert_element_type | solution.py:61
  294.4 0.0 all-reduce.5.cloned.1.call-update
  294.4 0.6 copy-done.3
  295.0 0.6 dynamic-slice
  296.3 0.0 copy-done
  296.3 0.5 fusion.7
  296.8 0.7 copy.39
  297.4 4.1 pad_maximum_fusion
  301.5 216.1 %all-reduce.5.cloned.1.call-done = bf16[768,2,2048]{2,1,0:T(2,128)(2,1)} async-done(((bf16[768,2,2048]{2,1,0:T(2,128)(2,1)}), bf16[768,2,2048]{2,1,0:T(2,128)(2,1)}) %all-reduce.5.cloned.1.call-update) | async-done | bytes 6291472
  517.6 3.2 convert_bitcast_fusion.1
  520.9 3.5 copy.40
  (10 shorter events, 0.1 us)
Async XLA Ops:
  7.2 132.7 %all-gather.2.cloned.1.call-start = ((), (), s32[]{:S(2)}) async-start(), calls=%async_computation.3 | async-start | bytes 7864320 | tf_op jit(solution)/shard_map/all_gather | solution.py:43
  155.8 4.0 copy-start.2
  155.8 41.6 %all-to-all-start.1 = ((bf16[1,2,1024,768]{3,1,0,2:T(2,128)(2,1)}), bf16[1,2,1024,768]{3,1,0,2:T(2,128)(2,1)S(1)}, u32[]{:S(2)}, u32[]{:S(2)}) async-start(bf16[1,2,1024,768]{3,1,0,2:T(2,128)(2,1)} %copy.34), calls=%async_computation.1 | async-start | bytes 6291456 | tf_op jit(solution)/shard_map/all_to_all | solution.py:53
  159.6 358.0 %all-reduce.5.cloned.1.call-start = ((), (), s32[]{:S(2)}) async-start(), calls=%async_computation.4 | async-start | bytes 12582912
  197.4 1.7 copy-start.1
  294.4 0.7 copy-start.3
  294.4 1.9 copy-start
Sparse Core Ops, SparseCore 0:
  9.6 118.0 all-gather.1
  294.5 223.0 all-reduce.4
where the time goes:
time: 532 us; the launch traced here: 531 us
  waiting for transfers between devices  254 us (48%)
  blocking collectives  142 us (27%)
  local copies, waits for them, and re-layouts  71.9 us (14%)
  matrix products  26.2 us (5%)
  other arithmetic  18.1 us (3%)
  between operations  14.8 us (3%)
    unnamed x3, waiting for transfers between devices  217 us
    all_to_all x1, blocking collectives, local(): lax.all_to_all(dy_send, 'expert', split_axis=0, concat_axis=2, tiled=True)  100 us
    all_to_all x1, blocking collectives, local(): lax.all_to_all(h_send, 'expert', split_axis=0, concat_axis=2, tiled=True)  41.4 us
    all_to_all x1, waiting for transfers between devices, local(): lax.all_to_all(grads.reshape(1, local_experts, owners * capacity, hidden_...  37.5 us
    convert_element_type x1, local copies, waits for them, and re-layouts, local(): jnp.einsum('jsn,jsd->njd', h_recv, dy_recv, preferred_element_type=jnp.fl...  16.4 us
    dot_general x1, matrix products, local(): jnp.einsum('jsn,jsd->njd', h_recv, dy_recv, preferred_element_type=jnp.fl...  15.2 us
    gather x1, local copies, waits for them, and re-layouts, local(): jnp.concatenate([cotangent, jnp.zeros((1, width), cotangent.dtype)], 0)  11 us
    dot_general x1, matrix products, local(): jnp.einsum('jsd,jfd->jsf', dy_recv, full_down, preferred_element_type=jnp...  11 us
  transfers between devices with their start and end apart: 3, of which 2 were waited for; matrix products, arithmetic and copies ran while one was open for 7% of the time, Pallas kernels for 0%

commit v1 on v0

v1 whole, which is shorter than its diff:
```python
import functools

import jax
import jax.numpy as jnp
from jax import lax
from jax.experimental import pallas as pl
from jax.experimental.pallas import tpu as pltpu
from jax.sharding import PartitionSpec as P

BF16 = jnp.bfloat16
F32 = jnp.float32
ANY = pl.BlockSpec(memory_space=pl.ANY)
SMEM = pl.BlockSpec(memory_space=pltpu.SMEM)
LIMIT = 56 * 1024 * 1024
ROWS = 16


def call(kernel, flops, moved, **kw):
    return pl.pallas_call(
        kernel,
        compiler_params=pltpu.CompilerParams(vmem_limit_bytes=LIMIT),
        cost_estimate=pl.CostEstimate(flops=int(flops), bytes_accessed=int(moved), transcendentals=0),
        **kw,
    )


def hidden_body(nd, top, chunks, pos, gu, wt, idt, *rest):
    outs, keep, rows, packed = rest[: nd * chunks], rest[nd * chunks], rest[-2], rest[-1]
    step = pl.program_id(0)
    block, units = gu.shape[0], gu.shape[1] // 2
    g = gu[:, :units].astype(F32)
    u = gu[:, units:].astype(F32)
    h = g * jax.nn.sigmoid(g) * u
    for c in range(units // 128):
        rows[c, pl.ds(pl.multiple_of(step * block, block), block), :] = h[:, c * 128 : (c + 1) * 128]

    @pl.when(step == pl.num_programs(0) - 1)
    def _():
        tokens = wt.shape[1]
        slice_units = packed.shape[1]
        for k in range(top):
            for c in range(units // 128):
                part = rows[c, pl.ds(k, tokens, stride=top), :]
                part = part.T.astype(BF16)
                keep[c * 128 : (c + 1) * 128, k * tokens : (k + 1) * tokens] = part
        for z in range(nd):
            for k in range(top):
                w = wt[k : k + 1, :]
                part = keep[z * slice_units : (z + 1) * slice_units, k * tokens : (k + 1) * tokens]
                packed[z, :, k * tokens : (k + 1) * tokens] = (part.astype(F32) * w).astype(BF16)
        size = slice_units // chunks
        for s in range(nd):
            z = lax.rem(pos[0] + s, nd)
            for c in range(chunks):
                outs[s * chunks + c][:size, :] = packed[z, c * size : (c + 1) * size, :]
            for k in range(top):
                outs[s * chunks][size:, k * tokens : (k + 1) * tokens] = jnp.broadcast_to(
                    idt[k : k + 1, :], (ROWS, tokens)
                ).astype(BF16)


def back_body(nw, nd, top, eids, *refs):
    ws, cots, ids = refs[:nw], refs[nw : nw + nd], refs[nw + nd : nw + 2 * nd]
    outs = refs[nw + 2 * nd : nw + 3 * nd]
    wv, cv, idv, grads, sem = refs[nw + 3 * nd :]
    names = [eids[e] for e in range(eids.shape[0])]
    tokens = cots[0].shape[0]
    units = wv.shape[1]
    copies = []
    for s in range(nd):
        copies.append(pltpu.make_async_copy(cots[s], cv.at[pl.ds(s * tokens, tokens), :], sem.at[s]))
        first = ids[s].shape[0] - ROWS
        copies.append(pltpu.make_async_copy(ids[s].at[pl.ds(first, ROWS), :], idv.at[s], sem.at[nd + s]))
    at, places = 0, []
    for i, w in enumerate(ws):
        places.append((at, w.shape[0]))
        copies.append(pltpu.make_async_copy(w, wv.at[pl.ds(at, w.shape[0])], sem.at[2 * nd + i]))
        at += w.shape[0]
    for c in copies:
        c.start()
    for c in copies[: 2 * nd]:
        c.wait()
    for i, (start, n) in enumerate(places):
        copies[2 * nd + i].wait()
        w = wv[start : start + n].reshape(n * units, wv.shape[2])
        got = lax.dot_general(w, cv[...], (((1,), (1,)), ((), ())), preferred_element_type=F32)
        grads[start : start + n] = got.reshape(n, units, cv.shape[0])
    for s in range(nd):
        cols = slice(s * tokens, (s + 1) * tokens)

        def body(j, _, s=s, cols=cols):
            f = pl.multiple_of(j * ROWS, ROWS)
            held = [grads[e, pl.ds(f, ROWS), cols] for e in range(at)]
            for k in range(top):
                span = slice(k * tokens, (k + 1) * tokens)
                row = idv[s, :, span].astype(F32)
                acc = jnp.zeros((ROWS, tokens), F32)
                for e in range(at):
                    acc = jnp.where(row == names[e], held[e], acc)
                outs[s][pl.ds(f, ROWS), span] = acc.astype(BF16)
            return 0

        lax.fori_loop(0, units // ROWS, body, 0)


def down_body(nb, top, plan, columns, eids, *refs):
    cots, hs, ids = refs[:nb], refs[nb : 2 * nb], refs[2 * nb : 3 * nb]
    outs = refs[3 * nb : 3 * nb + len(plan)]
    cv, hv, idv, dense, sem = refs[3 * nb + len(plan) :]
    experts = eids.shape[0]
    tokens = cots[0].shape[0]
    units = hv.shape[1]
    copies = []
    for b in range(nb):
        first = ids[b].shape[0] - ROWS
        copies.append(pltpu.make_async_copy(hs[b].at[pl.ds(0, units), :], hv.at[b], sem.at[b]))
        copies.append(pltpu.make_async_copy(ids[b].at[pl.ds(first, ROWS), :], idv.at[b], sem.at[nb + b]))
    for b in range(nb):
        copies.append(pltpu.make_async_copy(cots[b], cv.at[pl.ds(b * tokens, tokens), :], sem.at[2 * nb + b]))
    for c in copies:
        c.start()
    names = [eids[e] for e in range(experts)]
    for b in range(nb):
        copies[2 * b].wait()
        copies[2 * b + 1].wait()
        cols = slice(b * tokens, (b + 1) * tokens)

        def body(j, _, b=b, cols=cols):
            f = pl.multiple_of(j * ROWS, ROWS)
            spans = [slice(k * tokens, (k + 1) * tokens) for k in range(top)]
            held = [hv[b, pl.ds(f, ROWS), span].astype(F32) for span in spans]
            for e in range(experts):
                acc = jnp.zeros((ROWS, tokens), F32)
                for k in range(top):
                    acc = jnp.where(idv[b, :, spans[k]].astype(F32) == names[e], held[k], acc)
                dense[e, pl.ds(f, ROWS), cols] = acc.astype(BF16)
            return 0

        lax.fori_loop(0, units // ROWS, body, 0)
    for c in copies[2 * nb :]:
        c.wait()
    width = cv.shape[1]
    lhs = dense[...].reshape(experts * units, nb * tokens)
    for start in range(0, width, columns):
        got = jnp.dot(lhs, cv[:, start : start + columns], preferred_element_type=F32)
        got = got.astype(BF16).reshape(experts, units, columns)
        for out, (groups, low, high) in zip(outs, plan):
            if low <= start < high:
                per = out.shape[1]
                for i, r in enumerate(groups):
                    out[i, :, :, start - low : start - low + columns] = got[r * per : (r + 1) * per]


def final_body(nd, top, pos, *refs):
    backs, (gu, wt, keep, out, route, turned, rows) = refs[:nd], refs[nd:]
    step = pl.program_id(0)
    block, units = gu.shape[0], gu.shape[1] // 2
    tokens = wt.shape[1]

    @pl.when(step == 0)
    def _():
        size = backs[0].shape[0]
        for k in range(top):
            span = slice(k * tokens, (k + 1) * tokens)
            w = wt[k : k + 1, :]
            total = jnp.zeros((1, tokens), F32)
            for s in range(nd):
                at = pl.multiple_of(lax.rem(pos[0] + s, nd) * size, ROWS)
                q = backs[s][:, span].astype(F32)
                total = total + jnp.sum(q * keep[pl.ds(at, size), span].astype(F32), axis=0, keepdims=True)
                turned[pl.ds(at, size), :] = q * w
            route[k : k + 1, :] = total
            for c in range(units // 128):
                rows[c, pl.ds(k, tokens, stride=top), :] = turned[c * 128 : (c + 1) * 128, :].T

    g = gu[:, :units].astype(F32)
    u = gu[:, units:].astype(F32)
    at = pl.multiple_of(step * block, block)
    d = jnp.concatenate([rows[c, pl.ds(at, block), :] for c in range(units // 128)], axis=1)
    sig = jax.nn.sigmoid(g)
    out[:, :units] = (d * u * sig * (1.0 + g * (1.0 - sig))).astype(BF16)
    out[:, units:] = (d * (g * sig)).astype(BF16)


def total_body(chunks, halves, parts, *refs):
    ins, out = refs[:-1], refs[-1]
    units = out.shape[1] // chunks
    width = out.shape[2] // halves
    at = 0
    for c in range(chunks):
        for h in range(halves):
            acc = ins[at][...].astype(F32)
            for i in range(1, parts):
                acc = acc + ins[at + i][...].astype(F32)
            at += parts
            out[:, c * units : (c + 1) * units, h * width : (h + 1) * width] = acc


def local(cotangent, saved_gate_up, route_ids, route_weights, w_down):
    tokens, top = route_ids.shape
    width = cotangent.shape[1]
    units = saved_gate_up.shape[2] // 2
    nd, ne = lax.axis_size("dp"), lax.axis_size("expert")
    per, size = w_down.shape[0], w_down.shape[1]
    routes = tokens * top
    chunks = 2 if (size // 2) % ROWS == 0 else 1
    part = size // chunks
    bits = ne.bit_length() - 1
    groups = ne // 2
    held = groups * per
    p = lax.axis_index("dp").astype(jnp.int32)
    q = lax.axis_index("expert").astype(jnp.int32)
    pos = p.reshape(1)

    def owner_of(r):
        return ((q // 2) ^ r) * 2 + q % 2

    def swap(a, mask):
        return lax.ppermute(a, "expert", [(i, i ^ mask) for i in range(ne)])

    def shift(a, s):
        return lax.ppermute(a, "dp", [(i, (i + s) % nd) for i in range(nd)])

    eids = jnp.stack([owner_of(r) * per + e for r in range(groups) for e in range(per)]).astype(F32)

    gu = saved_gate_up.reshape(routes, 2 * units)
    wt = route_weights.T
    idt = route_ids.T.astype(F32)

    cots = [cotangent] + [shift(cotangent, s) for s in range(1, nd)]
    if bits == 3:
        w_x, w_y = swap(w_down, 2), swap(w_down, 4)
        w_d = [swap(w_x[: per // 2], 4), swap(w_y[per // 2 :], 2)]
        weights = [w_down, w_x, w_y] + w_d
    else:
        weights = w_down
        for b in range(1, bits):
            weights = jnp.concatenate([weights, swap(weights, 1 << b)], 0)
        weights = [weights]

    block = routes // 8
    shapes = []
    for s in range(nd):
        for c in range(chunks):
            shapes.append(jax.ShapeDtypeStruct((part + (ROWS if c == 0 else 0), routes), BF16))
    whole = lambda shape: pl.BlockSpec(shape, lambda i: (0,) * len(shape))
    made = call(
        functools.partial(hidden_body, nd, top, chunks),
        0,
        6 * units * routes * 4,
        grid=(8,),
        in_specs=[SMEM, pl.BlockSpec((block, 2 * units), lambda i: (i, 0)), whole((top, tokens)), whole((top, tokens))],
        out_specs=[whole(o.shape) for o in shapes] + [whole((units, routes))],
        out_shape=shapes + [jax.ShapeDtypeStruct((units, routes), BF16)],
        scratch_shapes=[pltpu.VMEM((units // 128, routes, 128), F32), pltpu.VMEM((nd, size, routes), BF16)],
    )(pos, gu, wt, idt)
    keep = made[-1]
    hs = [[made[s * chunks + c] for c in range(chunks)] for s in range(nd)]
    for c in range(chunks):
        for s in range(1, nd):
            hs[s][c] = shift(hs[s][c], s)

    cots_b = [swap(a, 1) for a in cots]
    hs_b = [[None] * chunks for _ in range(nd)]
    for c in range(chunks):
        for s in range(nd):
            hs_b[s][c] = swap(hs[s][c], 1)

    def back(cots, ids):
        nw = len(weights)
        n = nd * tokens
        return call(
            functools.partial(back_body, nw, nd, top),
            2 * held * size * width * n,
            2 * (held * size * width + n * width + n * top * size),
            in_specs=[SMEM] + [ANY] * (nw + 2 * nd),
            out_specs=[pl.BlockSpec(memory_space=pltpu.VMEM)] * nd,
            out_shape=[jax.ShapeDtypeStruct((size, routes), BF16)] * nd,
            scratch_shapes=[
                pltpu.VMEM((held, size, width), BF16),
                pltpu.VMEM((n, width), BF16),
                pltpu.VMEM((nd, ROWS, routes), BF16),
                pltpu.VMEM((held, size, n), F32),
                pltpu.SemaphoreType.DMA((2 * nd + nw,)),
            ],
        )(eids, *weights, *cots, *ids)

    other = back(cots_b, [h[0] for h in hs_b])
    own = back(cots, [h[0] for h in hs])
    backs = []
    for s in range(nd):
        mine = own[s] + swap(other[s], 1)
        backs.append(mine if s == 0 else shift(mine, nd - s))

    half = width // 2
    if bits == 3:
        plan = [((1, 3), 0, half), ((0, 2), 0, half), ((2, 3), half, width), ((0, 1), half, width)]
    else:
        plan = [(tuple(range(groups)), 0, width)]
    nb = 2 * nd
    cots_all = [a for s in range(nd) for a in (cots[s], cots_b[s])]
    first = [a for s in range(nd) for a in (hs[s][0], hs_b[s][0])]
    terms = []
    for c in range(chunks):
        parts = call(
            functools.partial(down_body, nb, top, plan, 512),
            2 * held * part * width * nb * tokens,
            2 * (held * part * width + nb * tokens * width + nb * routes * part),
            in_specs=[SMEM] + [ANY] * (3 * nb),
            out_specs=[pl.BlockSpec(memory_space=pltpu.VMEM)] * len(plan),
            out_shape=[jax.ShapeDtypeStruct((len(g), per, part, b - a), BF16) for g, a, b in plan],
            scratch_shapes=[
                pltpu.VMEM((nb * tokens, width), BF16),
                pltpu.VMEM((nb, part, routes), BF16),
                pltpu.VMEM((nb, ROWS, routes), BF16),
                pltpu.VMEM((held, part, nb * tokens), BF16),
                pltpu.SemaphoreType.DMA((3 * nb,)),
            ],
        )(eids, *cots_all, *[a for s in range(nd) for a in (hs[s][c], hs_b[s][c])], *first)
        if bits == 3:
            for (send, kept), (one, two) in (((parts[0], parts[1]), (2, 4)), ((parts[2], parts[3]), (4, 2))):
                got = swap(send, one)
                mid = (kept[1].astype(F32) + got[1].astype(F32)).astype(BF16)
                terms += [kept[0], got[0], swap(mid, two)]
        else:
            acc = parts[0]
            for b in reversed(range(1, bits)):
                n = acc.shape[0] // 2
                acc = (acc[:n].astype(F32) + swap(acc[n:], 1 << b).astype(F32)).astype(BF16)
            terms.append(acc[0])
    halves, parts = (2, 3) if bits == 3 else (1, 1)
    grad_down = call(
        functools.partial(total_body, chunks, halves, parts),
        0,
        2 * 5 * per * size * width,
        out_shape=jax.ShapeDtypeStruct((per, size, width), F32),
    )(*terms)

    out, route = call(
        functools.partial(final_body, nd, top),
        0,
        8 * units * routes * 4,
        grid=(8,),
        in_specs=[SMEM]
        + [whole((size, routes))] * nd
        + [pl.BlockSpec((block, 2 * units), lambda i: (i, 0)), whole((top, tokens)), whole((units, routes))],
        out_specs=[pl.BlockSpec((block, 2 * units), lambda i: (i, 0)), whole((top, tokens))],
        out_shape=[
            jax.ShapeDtypeStruct((routes, 2 * units), BF16),
            jax.ShapeDtypeStruct((top, tokens), F32),
        ],
        scratch_shapes=[pltpu.VMEM((units, tokens), F32), pltpu.VMEM((units // 128, routes, 128), F32)],
    )(pos, *backs, gu, wt, keep)
    return out.reshape(tokens, top, 2 * units), route.T, grad_down


def solution(mesh):
    return jax.shard_map(
        local,
        mesh=mesh,
        in_specs=(
            P(("dp", "expert"), None),
            P(("dp", "expert"), None, None),
            P(("dp", "expert"), None),
            P(("dp", "expert"), None),
            P("expert", "dp", None),
        ),
        out_specs=(
            P(("dp", "expert"), None, None),
            P(("dp", "expert"), None),
            P("expert", "dp", None),
        ),
        check_vma=False,
    )
```

time: 532 us -> 243 us (0.46)
  waiting for transfers between devices: 254 us -> 92.2 us
  blocking collectives: 142 us -> 0 us
  starting transfers between devices: 4.04 us -> 71.7 us
  local copies, waits for them, and re-layouts: 71.9 us -> 10.9 us
  Pallas kernels: 0 us -> 60.7 us
  matrix products: 26.2 us -> 0 us
  between operations: 14.8 us -> 1.03 us
  other arithmetic: 18.1 us -> 5.66 us
    unnamed x3 -> x0, waiting for transfers between devices: 217 us -> none
    all_to_all x2 -> x0, blocking collectives: 142 us -> none  [the longest x1 100 us: local(): lax.all_to_all(dy_send, 'expert', split_axis=0, concat_axis=2, tiled=True)]
    ppermute x0 -> x40, waiting for transfers between devices: none -> 92.2 us  [the longest x12 57.2 us: shift(): return lax.ppermute(a, 'dp', [(i, (i + s) % nd) for i in range(nd)])]
    ppermute x0 -> x40, starting transfers between devices: none -> 71.7 us  [the longest x12 51.6 us: shift(): return lax.ppermute(a, 'dp', [(i, (i + s) % nd) for i in range(nd)])]
    pallas_call x0 -> x7, Pallas kernels: none -> 60.7 us  [the longest x2 21.6 us: back(): call(functools.partial(back_body, nw, nd, top), 2 * held * size * width *...]
    all_to_all x1 -> x0, waiting for transfers between devices: 37.5 us -> none  [local(): lax.all_to_all(grads.reshape(1, local_experts, owners * capacity, hidden_...]
    dot_general x2 -> x0, matrix products: 26.2 us -> none  [the longest x1 15.2 us: local(): jnp.einsum('jsn,jsd->njd', h_recv, dy_recv, preferred_element_type=jnp.fl...]
    gather x3 -> x0, local copies, waits for them, and re-layouts: 25.6 us -> none  [the longest x1 11 us: local(): jnp.concatenate([cotangent, jnp.zeros((1, width), cotangent.dtype)], 0)]
  transfers between devices with their start and end apart: 3 -> 40, of which waited for: 2 -> 15; matrix products, arithmetic and copies ran while one was open for 7% -> 5% of each run, Pallas kernels for 0% -> 18%
where the time goes in v1:
time: 243 us; the launch traced here: 242 us
  waiting for transfers between devices  92.2 us (38%)
  starting transfers between devices  71.7 us (30%)
  Pallas kernels  60.7 us (25%)
  local copies, waits for them, and re-layouts  10.9 us (4%)
  other arithmetic  5.66 us (2%)
    ppermute x12, waiting for transfers between devices, shift(): return lax.ppermute(a, 'dp', [(i, (i + s) % nd) for i in range(nd)])  57.2 us
    ppermute x12, starting transfers between devices, shift(): return lax.ppermute(a, 'dp', [(i, (i + s) % nd) for i in range(nd)])  51.6 us
    ppermute x28, waiting for transfers between devices, swap(): return lax.ppermute(a, 'expert', [(i, i ^ mask) for i in range(ne)])  35 us
    pallas_call x2, Pallas kernels, back(): call(functools.partial(back_body, nw, nd, top), 2 * held * size * width *...  21.6 us
    ppermute x28, starting transfers between devices, swap(): return lax.ppermute(a, 'expert', [(i, i ^ mask) for i in range(ne)])  20.1 us
    pallas_call x2, Pallas kernels, local(): call(functools.partial(down_body, nb, top, plan, 512), 2 * held * part *...  16.8 us
    pallas_call x1, Pallas kernels, local(): call(functools.partial(final_body, nd, top), 0, 8 * units * routes * 4, g...  9.75 us
    pallas_call x1, Pallas kernels, local(): call(functools.partial(hidden_body, nd, top, chunks), 0, 6 * units * rout...  7.94 us
  transfers between devices with their start and end apart: 40, of which 15 were waited for; matrix products, arithmetic and copies ran while one was open for 5% of the time, Pallas kernels for 18%

profile of v1, /device:TPU:0, one launch (start us, length us, event | category | flops | bytes accessed | tf_op | source)
XLA Modules:
  0.0 242.1 jit_solution(11778470628864847589)
XLA Ops:
  0.6 1.3 convert_bitcast_fusion.idt
  1.9 7.9 %shard_map.76 = (bf16[112,1024]{1,0:T(8,128)(2,1)}, bf16[96,1024]{1,0:T(8,128)(2,1)}, bf16[112,1024]{1,0:T(8,128)(2,1)}, bf16[96,1024]{1,0:T(8,128)(2,1)}, bf16[...) custom-call(s32[1]{0:T(128)} %bitcast.pos, ...), custom_call_target="tpu_custom_call" | custom-call | bytes 18874368 | tf_op jit(solution)/shard_map/pallas_call | solution.py:247
  10.3 2.6 %collective-permute-start.7 = (bf16[112,1024]{1,0:T(8,128)(2,1)}, bf16[112,1024]{1,0:T(8,128)(2,1)S(1)}, u32[]{:S(2)}, u32[]{:S(2)}) collective-permute-start(bf16[112,1024]{1,0:T(8,128)(2,1)} %get-tuple-element.31), channel_id=1, source_target_pairs={{0,8},{8,16},{16,24},{24,0},{1,9},{9,17},{17,25},{25,1},{2,10},{10... | collective-permute-start | bytes 688136 | tf_op jit(solution)/shard_map/ppermute | solution.py:222
  12.9 1.6 collective-permute-start.30
  14.5 1.1 collective-permute-start.32
  15.5 2.9 %collective-permute-start.34 = (bf16[96,1024]{1,0:T(8,128)(2,1)}, bf16[96,1024]{1,0:T(8,128)(2,1)}, u32[]{:S(2)}, u32[]{:S(2)}) collective-permute-start(bf16[96,1024]{1,0:T(8,128)(2,1)} %get-tuple-element.52), channel_id=1, source_target_pairs={{0,24},{8,0},{16,8},{24,16},{1,25},{9,1},{17,9},{25,17},{2,26},{10... | collective-permute-start | bytes 589832 | tf_op jit(solution)/shard_map/ppermute | solution.py:222
  18.7 7.3 %collective-permute-done.30.refs_10_ = bf16[96,1024]{1,0:T(8,128)(2,1)} collective-permute-done((bf16[96,1024]{1,0:T(8,128)(2,1)}, bf16[96,1024]{1,0:T(8,128)(2,1)}, u32[]{:S(2)}, u32[]{:S(2)}) %collective-permute-start.30) | collective-permute-done | bytes 196640 | tf_op jit(solution)/shard_map/ppermute | solution.py:222
  26.0 1.5 collective-permute-start.9
  27.6 6.9 %collective-permute-done.32.refs_12_ = bf16[96,1024]{1,0:T(8,128)(2,1)} collective-permute-done((bf16[96,1024]{1,0:T(8,128)(2,1)}, bf16[96,1024]{1,0:T(8,128)(2,1)}, u32[]{:S(2)}, u32[]{:S(2)}) %collective-permute-start.32) | collective-permute-done | bytes 196640 | tf_op jit(solution)/shard_map/ppermute | solution.py:222
  35.0 12.9 %collective-permute-start.4 = (bf16[128,2048]{1,0:T(8,128)(2,1)S(1)}, bf16[128,2048]{1,0:T(8,128)(2,1)S(1)}, u32[]{:S(2)}, u32[]{:S(2)}) collective-permute-start(bf16[128,2048]{1,0:T(8,128)(2,1)S(1)} %copy-done.15), channel_id=1, source_target_pairs={{0,8},{8,16},{16,24},{24,0},{1,9},{9,17},{17,25},{25,1},{2,10},{10... | collective-permute-start | bytes 1572872 | tf_op jit(solution)/shard_map/ppermute | solution.py:222
  48.3 2.3 collective-permute-done.9.refs_12_.refs_14_.refs_22_
  50.6 13.4 %collective-permute-start.5 = (bf16[128,2048]{1,0:T(8,128)(2,1)S(1)}, bf16[128,2048]{1,0:T(8,128)(2,1)S(1)}, u32[]{:S(2)}, u32[]{:S(2)}) collective-permute-start(bf16[128,2048]{1,0:T(8,128)(2,1)S(1)} %copy-done.15), channel_id=1, source_target_pairs={{0,16},{8,24},{16,0},{24,8},{1,17},{9,25},{17,1},{25,9},{2,18},{10... | collective-permute-start | bytes 1572872 | tf_op jit(solution)/shard_map/ppermute | solution.py:222
  64.0 3.3 %collective-permute-start.6 = (bf16[128,2048]{1,0:T(8,128)(2,1)S(1)}, bf16[128,2048]{1,0:T(8,128)(2,1)}, u32[]{:S(2)}, u32[]{:S(2)}) collective-permute-start(bf16[128,2048]{1,0:T(8,128)(2,1)S(1)} %copy-done.15), channel_id=1, source_target_pairs={{0,24},{8,0},{16,8},{24,16},{1,25},{9,1},{17,9},{25,17},{2,26},{10... | collective-permute-start | bytes 1572872 | tf_op jit(solution)/shard_map/ppermute | solution.py:222
  68.1 1.6 collective-permute-done.17.refs_12_.refs_15_.refs_23_
  69.7 1.5 collective-permute-start
  71.2 1.5 collective-permute-start.1
  72.7 15.3 %collective-permute-done.5.refs_7_.refs_4_ = bf16[128,2048]{1,0:T(8,128)(2,1)S(1)} collective-permute-done((bf16[128,2048]{1,0:T(8,128)(2,1)S(1)}, bf16[128,2048]{1,0:T(8,128)(2,1)S(1)}, u32[]{:S(2)}, u32[]{:S(2)}) %collective-permute-start.5) | collective-permute-done | bytes 524320 | tf_op jit(solution)/shard_map/ppermute | solution.py:222
  88.5 0.8 copy-done.18
  92.4 8.4 %shard_map.80 = (bf16[2,2,96,1024]{3,2,1,0:T(8,128)(2,1)}, bf16[2,2,96,1024]{3,2,1,0:T(8,128)(2,1)}, bf16[2,2,96,1024]{3,2,1,0:T(8,128)(2,1)}, bf16[2,2,96,1024]{3,2,1,0:T(8,128)(2,1)}) custom-call(f32[8]{0:T(128)} %convert_element_type.64.eids, bf16[128,2048]{1,0:T(8,128)(2,1)} %refs_0_.7, bf16[128,2048]{1,0:T(8,128)(2,1)} %copy-done.18, ...), custom_call_target="tpu_custom_call" | custom-call | flops 3221225472 | bytes 8912896 | tf_op jit(solution)/shard_map/pallas_call | solution.py:305
  100.8 1.6 collective-permute-start.25
  102.4 1.6 collective-permute-start.27
  104.7 8.4 %shard_map.81 = (bf16[2,2,96,1024]{3,2,1,0:T(8,128)(2,1)}, bf16[2,2,96,1024]{3,2,1,0:T(8,128)(2,1)}, bf16[2,2,96,1024]{3,2,1,0:T(8,128)(2,1)}, bf16[2,2,96,1024]{3,2,1,0:T(8,128)(2,1)}) custom-call(f32[8]{0:T(128)} %convert_element_type.64.eids, bf16[128,2048]{1,0:T(8,128)(2,1)} %refs_0_.7, bf16[128,2048]{1,0:T(8,128)(2,1)} %copy-done.18, ...), custom_call_target="tpu_custom_call" | custom-call | flops 3221225472 | bytes 8912896 | tf_op jit(solution)/shard_map/pallas_call | solution.py:305
  113.7 1.0 slice_bitcast_fusion.6
  115.4 1.5 slice.73
  116.9 1.6 collective-permute-start.3
  118.5 1.0 slice_bitcast_fusion.4
  119.5 4.5 %collective-permute-done.25 = bf16[2,2,96,1024]{3,2,1,0:T(8,128)(2,1)S(1)} collective-permute-done((bf16[2,2,96,1024]{3,2,1,0:T(8,128)(2,1)}, bf16[2,2,96,1024]{3,2,1,0:T(8,128)(2,1)S(1)}, u32[]{:S(2)}, u32[]{:S(2)}) %collective-permute-start.25) | collective-permute-done | bytes 786464 | tf_op jit(solution)/shard_map/ppermute | solution.py:219
  124.0 1.5 collective-permute-start.38
  125.6 1.4 collective-permute-start.26
  127.2 13.7 %collective-permute-done.36 = bf16[2,2,96,1024]{3,2,1,0:T(8,128)(2,1)S(1)} collective-permute-done((bf16[2,2,96,1024]{3,2,1,0:T(8,128)(2,1)}, bf16[2,2,96,1024]{3,2,1,0:T(8,128)(2,1)S(1)}, u32[]{:S(2)}, u32[]{:S(2)}) %collective-permute-start.36) | collective-permute-done | bytes 786464 | tf_op jit(solution)/shard_map/ppermute | solution.py:219
  140.8 1.5 collective-permute-start.28
  142.5 1.6 collective-permute-start.37
  144.1 13.7 %collective-permute-done.3.refs_4_ = bf16[1,192,2048]{2,1,0:T(8,128)(2,1)} collective-permute-done((bf16[1,192,2048]{2,1,0:T(8,128)(2,1)S(1)}, bf16[1,192,2048]{2,1,0:T(8,128)(2,1)}, u32[]{:S(2)}, u32[]{:S(2)}) %collective-permute-start.3) | collective-permute-done | bytes 786464 | tf_op jit(solution)/shard_map/ppermute | solution.py:219
  157.8 10.8 %shard_map.78 = (bf16[192,1024]{1,0:T(8,128)(2,1)}, bf16[192,1024]{1,0:T(8,128)(2,1)}, bf16[192,1024]{1,0:T(8,128)(2,1)}, bf16[192,1024]{1,0:T(8,128)(2,1)}) custom-call(f32[8]{0:T(128)} %convert_element_type.64.eids, bf16[2,192,2048]{2,1,0:T(8,128)(2,1)} %refs_0_.5, bf16[2,192,2048]{2,1,0:T(8,128)(2,1)} %copy-done.7, ...), custom_call_target="tpu_custom_call" | custom-call | flops 3221225472 | bytes 9961472 | tf_op jit(solution)/shard_map/pallas_call | solution.py:272
  168.7 0.8 slice_bitcast_fusion.3.refs_1_
  170.8 0.8 slice_bitcast_fusion.2.refs_4_
  171.6 10.8 %shard_map.77 = (bf16[192,1024]{1,0:T(8,128)(2,1)}, bf16[192,1024]{1,0:T(8,128)(2,1)}, bf16[192,1024]{1,0:T(8,128)(2,1)}, bf16[192,1024]{1,0:T(8,128)(2,1)}) custom-call(f32[8]{0:T(128)} %convert_element_type.64.eids, bf16[2,192,2048]{2,1,0:T(8,128)(2,1)} %refs_0_.5, bf16[2,192,2048]{2,1,0:T(8,128)(2,1)} %copy-done.7, ...), custom_call_target="tpu_custom_call" | custom-call | flops 3221225472 | bytes 9961472 | tf_op jit(solution)/shard_map/pallas_call | solution.py:272
  182.4 1.2 add.78
  183.6 1.6 collective-permute-start.39
  185.2 1.1 add.79
  186.7 11.5 %collective-permute-start.20 = (bf16[192,1024]{1,0:T(8,128)(2,1)S(1)}, bf16[192,1024]{1,0:T(8,128)(2,1)S(1)}, u32[]{:S(2)}, u32[]{:S(2)}) collective-permute-start(bf16[192,1024]{1,0:T(8,128)(2,1)S(1)} %add.78), channel_id=1, source_target_pairs={{0,24},{8,0},{16,8},{24,16},{1,25},{9,1},{17,9},{25,17},{2,26},{10... | collective-permute-start | bytes 1179656 | tf_op jit(solution)/shard_map/ppermute | solution.py:222
  198.8 0.8 slice_bitcast_fusion.1.refs_7_
  199.6 0.8 slice_bitcast_fusion.refs_10_
  201.1 4.5 %shard_map.82 = f32[2,192,2048]{2,1,0:T(8,128)} custom-call(bf16[2,96,1024]{2,1,0:T(8,128)(2,1)} %get-tuple-element.58.refs_0_, bf16[2,96,1024]{2,1,0:T(8,128)(2,1)} %slice_bitcast_fusion.3.refs_1_, bf16[2,96,1024]{2,1,0:T(8,128)(2,1)} %copy-done.10, bf16[2,96,1024]{2,1,0:T(8,128)(2,1)} %get-tuple-element.57.refs_3_, ...), custom_call_target="tpu_custom_call" | custom-call | bytes 7864320 | tf_op jit(solution)/shard_map/pallas_call | solution.py:332
  205.6 0.9 add.77.refs_0_
  206.5 1.1 collective-permute-done.20.refs_1_
  207.7 23.8 %collective-permute-done.22.refs_2_ = bf16[192,1024]{1,0:T(8,128)(2,1)S(1)} collective-permute-done((bf16[192,1024]{1,0:T(8,128)(2,1)S(1)}, bf16[192,1024]{1,0:T(8,128)(2,1)S(1)}, u32[]{:S(2)}, u32[]{:S(2)}) %collective-permute-start.22) | collective-permute-done | bytes 393248 | tf_op jit(solution)/shard_map/ppermute | solution.py:222
  232.4 9.8 %shard_map.79 = (bf16[1024,1536]{1,0:T(8,128)(2,1)}, f32[8,128]{1,0:T(8,128)}) custom-call(s32[1]{0:T(128)} %bitcast.pos, bf16[192,1024]{1,0:T(8,128)(2,1)} %add.77.refs_0_, bf16[192,1024]{1,0:T(8,128)(2,1)} %copy-done.4, bf16[192,1024]{1,0:T(8,128)(2,1)} %copy-done.5, bf16[192,1024]{1,0:T(8,128)(2,1)} %copy-done.6, bf16[1024,1536]{1,0:T(8,128)(2,1)} %bitcast.40, ...), custom_call_target="tpu_custom_call" | custom-call | bytes 25165824 | tf_op jit(solution)/shard_map/pallas_call | solution.py:339
  (124 shorter events, 12.4 us)
Async XLA Ops:
  1.9 33.1 %copy-start.15 = (bf16[128,2048]{1,0:T(8,128)(2,1)S(1)}, bf16[128,2048]{1,0:T(8,128)(2,1)}, u32[]{:S(2)}) copy-start(bf16[128,2048]{1,0:T(8,128)(2,1)} %refs_0_.7) | copy-start | bytes 1572868
  9.9 8.5 %collective-permute-start.29 = (bf16[96,1024]{1,0:T(8,128)(2,1)}, bf16[96,1024]{1,0:T(8,128)(2,1)S(1)}, u32[]{:S(2)}, u32[]{:S(2)}) collective-permute-start(bf16[96,1024]{1,0:T(8,128)(2,1)} %get-tuple-element.49.refs_8_), channel_id=1, source_target_pairs={{0,1},{1,0},{2,3},{3,2},{4,5},{5,4},{6,7},{7,6},{8,9},{9,8},{10,11... | collective-permute-start | bytes 589832 | tf_op jit(solution)/shard_map/ppermute | solution.py:219
  10.3 24.2 %collective-permute-start.7 = (bf16[112,1024]{1,0:T(8,128)(2,1)}, bf16[112,1024]{1,0:T(8,128)(2,1)S(1)}, u32[]{:S(2)}, u32[]{:S(2)}) collective-permute-start(bf16[112,1024]{1,0:T(8,128)(2,1)} %get-tuple-element.31), channel_id=1, source_target_pairs={{0,8},{8,16},{16,24},{24,0},{1,9},{9,17},{17,25},{25,1},{2,10},{10... | collective-permute-start | bytes 688136 | tf_op jit(solution)/shard_map/ppermute | solution.py:222
  12.9 13.2 %collective-permute-start.30 = (bf16[96,1024]{1,0:T(8,128)(2,1)}, bf16[96,1024]{1,0:T(8,128)(2,1)}, u32[]{:S(2)}, u32[]{:S(2)}) collective-permute-start(bf16[96,1024]{1,0:T(8,128)(2,1)} %get-tuple-element.50), channel_id=1, source_target_pairs={{0,8},{8,16},{16,24},{24,0},{1,9},{9,17},{17,25},{25,1},{2,10},{10... | collective-permute-start | bytes 589832 | tf_op jit(solution)/shard_map/ppermute | solution.py:222
  14.5 20.0 %collective-permute-start.32 = (bf16[96,1024]{1,0:T(8,128)(2,1)}, bf16[96,1024]{1,0:T(8,128)(2,1)}, u32[]{:S(2)}, u32[]{:S(2)}) collective-permute-start(bf16[96,1024]{1,0:T(8,128)(2,1)} %get-tuple-element.51), channel_id=1, source_target_pairs={{0,16},{8,24},{16,0},{24,8},{1,17},{9,25},{17,1},{25,9},{2,18},{10... | collective-permute-start | bytes 589832 | tf_op jit(solution)/shard_map/ppermute | solution.py:222
  15.5 19.5 %collective-permute-start.34 = (bf16[96,1024]{1,0:T(8,128)(2,1)}, bf16[96,1024]{1,0:T(8,128)(2,1)}, u32[]{:S(2)}, u32[]{:S(2)}) collective-permute-start(bf16[96,1024]{1,0:T(8,128)(2,1)} %get-tuple-element.52), channel_id=1, source_target_pairs={{0,24},{8,0},{16,8},{24,16},{1,25},{9,1},{17,9},{25,17},{2,26},{10... | collective-permute-start | bytes 589832 | tf_op jit(solution)/shard_map/ppermute | solution.py:222
  18.4 82.4 %copy-start.29 = (bf16[96,1024]{1,0:T(8,128)(2,1)}, bf16[96,1024]{1,0:T(8,128)(2,1)S(1)}, u32[]{:S(2)}) copy-start(bf16[96,1024]{1,0:T(8,128)(2,1)S(1)} %collective-permute-done.29.refs_9_) | copy-start | bytes 589828
  18.4 29.9 %collective-permute-start.8 = (bf16[112,1024]{1,0:T(8,128)(2,1)}, bf16[112,1024]{1,0:T(8,128)(2,1)S(1)}, u32[]{:S(2)}, u32[]{:S(2)}) collective-permute-start(bf16[112,1024]{1,0:T(8,128)(2,1)} %get-tuple-element.32), channel_id=1, source_target_pairs={{0,16},{8,24},{16,0},{24,8},{1,17},{9,25},{17,1},{25,9},{2,18},{10... | collective-permute-start | bytes 688136 | tf_op jit(solution)/shard_map/ppermute | solution.py:222
  26.0 24.6 %collective-permute-start.9 = (bf16[112,1024]{1,0:T(8,128)(2,1)}, bf16[112,1024]{1,0:T(8,128)(2,1)S(1)}, u32[]{:S(2)}, u32[]{:S(2)}) collective-permute-start(bf16[112,1024]{1,0:T(8,128)(2,1)} %get-tuple-element.33), channel_id=1, source_target_pairs={{0,24},{8,0},{16,8},{24,16},{1,25},{9,1},{17,9},{25,17},{2,26},{10... | collective-permute-start | bytes 688136 | tf_op jit(solution)/shard_map/ppermute | solution.py:222
  34.5 29.5 %collective-permute-start.14 = (bf16[112,1024]{1,0:T(8,128)(2,1)}, bf16[112,1024]{1,0:T(8,128)(2,1)S(1)}, u32[]{:S(2)}, u32[]{:S(2)}) collective-permute-start(bf16[112,1024]{1,0:T(8,128)(2,1)} %get-tuple-element.30.refs_9_.refs_8_.refs_16_), channel_id=1, source_target_pairs={{0,1},{1,0},{2,3},{3,2},{4,5},{5,4},{6,7},{7,6},{8,9},{9,8},{10,11... | collective-permute-start | bytes 688136 | tf_op jit(solution)/shard_map/ppermute | solution.py:219
  34.5 33.3 %copy-start.23 = (bf16[112,1024]{1,0:T(8,128)(2,1)}, bf16[112,1024]{1,0:T(8,128)(2,1)S(1)}, u32[]{:S(2)}) copy-start(bf16[112,1024]{1,0:T(8,128)(2,1)S(1)} %collective-permute-done.7.refs_10_.refs_18_) | copy-start | bytes 688132
  34.5 32.8 %collective-permute-start.15 = (bf16[112,1024]{1,0:T(8,128)(2,1)S(1)}, bf16[112,1024]{1,0:T(8,128)(2,1)S(1)}, u32[]{:S(2)}, u32[]{:S(2)}) collective-permute-start(bf16[112,1024]{1,0:T(8,128)(2,1)S(1)} %collective-permute-done.7.refs_10_.refs_18_), channel_id=1, source_target_pairs={{0,1},{1,0},{2,3},{3,2},{4,5},{5,4},{6,7},{7,6},{8,9},{9,8},{10,11... | collective-permute-start | bytes 688136 | tf_op jit(solution)/shard_map/ppermute | solution.py:219
  35.0 36.1 %collective-permute-start.4 = (bf16[128,2048]{1,0:T(8,128)(2,1)S(1)}, bf16[128,2048]{1,0:T(8,128)(2,1)S(1)}, u32[]{:S(2)}, u32[]{:S(2)}) collective-permute-start(bf16[128,2048]{1,0:T(8,128)(2,1)S(1)} %copy-done.15), channel_id=1, source_target_pairs={{0,8},{8,16},{16,24},{24,0},{1,9},{9,17},{17,25},{25,1},{2,10},{10... | collective-permute-start | bytes 1572872 | tf_op jit(solution)/shard_map/ppermute | solution.py:222
  48.3 19.5 %copy-start.24 = (bf16[112,1024]{1,0:T(8,128)(2,1)}, bf16[112,1024]{1,0:T(8,128)(2,1)S(1)}, u32[]{:S(2)}) copy-start(bf16[112,1024]{1,0:T(8,128)(2,1)S(1)} %collective-permute-done.8.refs_11_.refs_12_.refs_20_) | copy-start | bytes 688132
  48.3 19.0 %collective-permute-start.16 = (bf16[112,1024]{1,0:T(8,128)(2,1)S(1)}, bf16[112,1024]{1,0:T(8,128)(2,1)S(1)}, u32[]{:S(2)}, u32[]{:S(2)}) collective-permute-start(bf16[112,1024]{1,0:T(8,128)(2,1)S(1)} %collective-permute-done.8.refs_11_.refs_12_.refs_20_), channel_id=1, source_target_pairs={{0,1},{1,0},{2,3},{3,2},{4,5},{5,4},{6,7},{7,6},{8,9},{9,8},{10,11... | collective-permute-start | bytes 688136 | tf_op jit(solution)/shard_map/ppermute | solution.py:219
  50.6 17.2 %copy-start.25 = (bf16[112,1024]{1,0:T(8,128)(2,1)}, bf16[112,1024]{1,0:T(8,128)(2,1)S(1)}, u32[]{:S(2)}) copy-start(bf16[112,1024]{1,0:T(8,128)(2,1)S(1)} %collective-permute-done.9.refs_12_.refs_14_.refs_22_) | copy-start | bytes 688132
  50.6 37.3 %collective-permute-start.5 = (bf16[128,2048]{1,0:T(8,128)(2,1)S(1)}, bf16[128,2048]{1,0:T(8,128)(2,1)S(1)}, u32[]{:S(2)}, u32[]{:S(2)}) collective-permute-start(bf16[128,2048]{1,0:T(8,128)(2,1)S(1)} %copy-done.15), channel_id=1, source_target_pairs={{0,16},{8,24},{16,0},{24,8},{1,17},{9,25},{17,1},{25,9},{2,18},{10... | collective-permute-start | bytes 1572872 | tf_op jit(solution)/shard_map/ppermute | solution.py:222
  64.0 24.0 %collective-permute-start.6 = (bf16[128,2048]{1,0:T(8,128)(2,1)S(1)}, bf16[128,2048]{1,0:T(8,128)(2,1)}, u32[]{:S(2)}, u32[]{:S(2)}) collective-permute-start(bf16[128,2048]{1,0:T(8,128)(2,1)S(1)} %copy-done.15), channel_id=1, source_target_pairs={{0,24},{8,0},{16,8},{24,16},{1,25},{9,1},{17,9},{25,17},{2,26},{10... | collective-permute-start | bytes 1572872 | tf_op jit(solution)/shard_map/ppermute | solution.py:222
  67.3 21.2 %collective-permute-start.10 = (bf16[128,2048]{1,0:T(8,128)(2,1)S(1)}, bf16[128,2048]{1,0:T(8,128)(2,1)S(1)}, u32[]{:S(2)}, u32[]{:S(2)}) collective-permute-start(bf16[128,2048]{1,0:T(8,128)(2,1)S(1)} %copy-done.15), channel_id=1, source_target_pairs={{0,1},{1,0},{2,3},{3,2},{4,5},{5,4},{6,7},{7,6},{8,9},{9,8},{10,11... | collective-permute-start | bytes 1572872 | tf_op jit(solution)/shard_map/ppermute | solution.py:219
  67.3 2.3 collective-permute-start.17
  69.7 45.0 %collective-permute-start = (bf16[2,192,2048]{2,1,0:T(8,128)(2,1)}, bf16[2,192,2048]{2,1,0:T(8,128)(2,1)S(1)}, u32[]{:S(2)}, u32[]{:S(2)}) collective-permute-start(bf16[2,192,2048]{2,1,0:T(8,128)(2,1)} %refs_0_.5), channel_id=1, source_target_pairs={{0,2},{1,3},{2,0},{3,1},{4,6},{5,7},{6,4},{7,5},{8,10},{9,11},{10,... | collective-permute-start | bytes 4718600 | tf_op jit(solution)/shard_map/ppermute | solution.py:219
  71.2 20.6 %copy-start.16 = (bf16[128,2048]{1,0:T(8,128)(2,1)}, bf16[128,2048]{1,0:T(8,128)(2,1)S(1)}, u32[]{:S(2)}) copy-start(bf16[128,2048]{1,0:T(8,128)(2,1)S(1)} %collective-permute-done.4.refs_6_.refs_2_) | copy-start | bytes 1572868
  71.2 44.3 %collective-permute-start.1 = (bf16[2,192,2048]{2,1,0:T(8,128)(2,1)}, bf16[2,192,2048]{2,1,0:T(8,128)(2,1)}, u32[]{:S(2)}, u32[]{:S(2)}) collective-permute-start(bf16[2,192,2048]{2,1,0:T(8,128)(2,1)} %refs_0_.5), channel_id=1, source_target_pairs={{0,4},{1,5},{2,6},{3,7},{4,0},{5,1},{6,2},{7,3},{8,12},{9,13},{10,... | collective-permute-start | bytes 4718600 | tf_op jit(solution)/shard_map/ppermute | solution.py:219
  88.0 2.0 collective-permute-start.11
  88.0 2.8 %collective-permute-start.12 = (bf16[128,2048]{1,0:T(8,128)(2,1)S(1)}, bf16[128,2048]{1,0:T(8,128)(2,1)}, u32[]{:S(2)}, u32[]{:S(2)}) collective-permute-start(bf16[128,2048]{1,0:T(8,128)(2,1)S(1)} %collective-permute-done.5.refs_7_.refs_4_), channel_id=1, source_target_pairs={{0,1},{1,0},{2,3},{3,2},{4,5},{5,4},{6,7},{7,6},{8,9},{9,8},{10,11... | collective-permute-start | bytes 1572872 | tf_op jit(solution)/shard_map/ppermute | solution.py:219
  89.3 2.3 collective-permute-start.13
  90.0 10.8 %collective-permute-start.31 = (bf16[96,1024]{1,0:T(8,128)(2,1)}, bf16[96,1024]{1,0:T(8,128)(2,1)S(1)}, u32[]{:S(2)}, u32[]{:S(2)}) collective-permute-start(bf16[96,1024]{1,0:T(8,128)(2,1)} %collective-permute-done.30.refs_10_), channel_id=1, source_target_pairs={{0,1},{1,0},{2,3},{3,2},{4,5},{5,4},{6,7},{7,6},{8,9},{9,8},{10,11... | collective-permute-start | bytes 589832 | tf_op jit(solution)/shard_map/ppermute | solution.py:219
  90.8 11.6 %collective-permute-start.33 = (bf16[96,1024]{1,0:T(8,128)(2,1)}, bf16[96,1024]{1,0:T(8,128)(2,1)S(1)}, u32[]{:S(2)}, u32[]{:S(2)}) collective-permute-start(bf16[96,1024]{1,0:T(8,128)(2,1)} %collective-permute-done.32.refs_12_), channel_id=1, source_target_pairs={{0,1},{1,0},{2,3},{3,2},{4,5},{5,4},{6,7},{7,6},{8,9},{9,8},{10,11... | collective-permute-start | bytes 589832 | tf_op jit(solution)/shard_map/ppermute | solution.py:219
  91.6 12.4 %collective-permute-start.35 = (bf16[96,1024]{1,0:T(8,128)(2,1)}, bf16[96,1024]{1,0:T(8,128)(2,1)S(1)}, u32[]{:S(2)}, u32[]{:S(2)}) collective-permute-start(bf16[96,1024]{1,0:T(8,128)(2,1)} %collective-permute-done.34.refs_14_), channel_id=1, source_target_pairs={{0,1},{1,0},{2,3},{3,2},{4,5},{5,4},{6,7},{7,6},{8,9},{9,8},{10,11... | collective-permute-start | bytes 589832 | tf_op jit(solution)/shard_map/ppermute | solution.py:219
  100.8 23.1 %collective-permute-start.25 = (bf16[2,2,96,1024]{3,2,1,0:T(8,128)(2,1)}, bf16[2,2,96,1024]{3,2,1,0:T(8,128)(2,1)S(1)}, u32[]{:S(2)}, u32[]{:S(2)}) collective-permute-start(bf16[2,2,96,1024]{3,2,1,0:T(8,128)(2,1)} %get-tuple-element.46), channel_id=1, source_target_pairs={{0,2},{1,3},{2,0},{3,1},{4,6},{5,7},{6,4},{7,5},{8,10},{9,11},{10,... | collective-permute-start | bytes 2359304 | tf_op jit(solution)/shard_map/ppermute | solution.py:219
  102.4 23.2 %collective-permute-start.27 = (bf16[2,2,96,1024]{3,2,1,0:T(8,128)(2,1)}, bf16[2,2,96,1024]{3,2,1,0:T(8,128)(2,1)S(1)}, u32[]{:S(2)}, u32[]{:S(2)}) collective-permute-start(bf16[2,2,96,1024]{3,2,1,0:T(8,128)(2,1)} %get-tuple-element.48), channel_id=1, source_target_pairs={{0,4},{1,5},{2,6},{3,7},{4,0},{5,1},{6,2},{7,3},{8,12},{9,13},{10,... | collective-permute-start | bytes 2359304 | tf_op jit(solution)/shard_map/ppermute | solution.py:219
  113.1 27.7 %collective-permute-start.36 = (bf16[2,2,96,1024]{3,2,1,0:T(8,128)(2,1)}, bf16[2,2,96,1024]{3,2,1,0:T(8,128)(2,1)S(1)}, u32[]{:S(2)}, u32[]{:S(2)}) collective-permute-start(bf16[2,2,96,1024]{3,2,1,0:T(8,128)(2,1)} %get-tuple-element.54), channel_id=1, source_target_pairs={{0,2},{1,3},{2,0},{3,1},{4,6},{5,7},{6,4},{7,5},{8,10},{9,11},{10,... | collective-permute-start | bytes 2359304 | tf_op jit(solution)/shard_map/ppermute | solution.py:219
  114.8 27.7 %collective-permute-start.2 = (bf16[1,192,2048]{2,1,0:T(8,128)(2,1)S(1)}, bf16[1,192,2048]{2,1,0:T(8,128)(2,1)S(1)}, u32[]{:S(2)}, u32[]{:S(2)}) collective-permute-start(bf16[1,192,2048]{2,1,0:T(8,128)(2,1)S(1)} %slice.72), channel_id=1, source_target_pairs={{0,4},{1,5},{2,6},{3,7},{4,0},{5,1},{6,2},{7,3},{8,12},{9,13},{10,... | collective-permute-start | bytes 2359304 | tf_op jit(solution)/shard_map/ppermute | solution.py:219
  116.9 40.8 %collective-permute-start.3 = (bf16[1,192,2048]{2,1,0:T(8,128)(2,1)S(1)}, bf16[1,192,2048]{2,1,0:T(8,128)(2,1)}, u32[]{:S(2)}, u32[]{:S(2)}) collective-permute-start(bf16[1,192,2048]{2,1,0:T(8,128)(2,1)S(1)} %slice.73), channel_id=1, source_target_pairs={{0,2},{1,3},{2,0},{3,1},{4,6},{5,7},{6,4},{7,5},{8,10},{9,11},{10,... | collective-permute-start | bytes 2359304 | tf_op jit(solution)/shard_map/ppermute | solution.py:219
  124.0 45.6 %collective-permute-start.38 = (bf16[2,2,96,1024]{3,2,1,0:T(8,128)(2,1)}, bf16[2,2,96,1024]{3,2,1,0:T(8,128)(2,1)S(1)}, u32[]{:S(2)}, u32[]{:S(2)}) collective-permute-start(bf16[2,2,96,1024]{3,2,1,0:T(8,128)(2,1)} %get-tuple-element.56), channel_id=1, source_target_pairs={{0,4},{1,5},{2,6},{3,7},{4,0},{5,1},{6,2},{7,3},{8,12},{9,13},{10,... | collective-permute-start | bytes 2359304 | tf_op jit(solution)/shard_map/ppermute | solution.py:219
  125.6 61.0 %collective-permute-start.26 = (bf16[2,96,1024]{2,1,0:T(8,128)(2,1)S(1)}, bf16[2,96,1024]{2,1,0:T(8,128)(2,1)S(1)}, u32[]{:S(2)}, u32[]{:S(2)}) collective-permute-start(bf16[2,96,1024]{2,1,0:T(8,128)(2,1)S(1)} %fusion), channel_id=1, source_target_pairs={{0,4},{1,5},{2,6},{3,7},{4,0},{5,1},{6,2},{7,3},{8,12},{9,13},{10,... | collective-permute-start | bytes 1179656 | tf_op jit(solution)/shard_map/ppermute | solution.py:219
  140.8 57.3 %collective-permute-start.28 = (bf16[2,96,1024]{2,1,0:T(8,128)(2,1)S(1)}, bf16[2,96,1024]{2,1,0:T(8,128)(2,1)S(1)}, u32[]{:S(2)}, u32[]{:S(2)}) collective-permute-start(bf16[2,96,1024]{2,1,0:T(8,128)(2,1)S(1)} %fusion.1), channel_id=1, source_target_pairs={{0,2},{1,3},{2,0},{3,1},{4,6},{5,7},{6,4},{7,5},{8,10},{9,11},{10,... | collective-permute-start | bytes 1179656 | tf_op jit(solution)/shard_map/ppermute | solution.py:219
  142.5 15.3 %copy-start.14 = (bf16[1,192,2048]{2,1,0:T(8,128)(2,1)}, bf16[1,192,2048]{2,1,0:T(8,128)(2,1)S(1)}, u32[]{:S(2)}) copy-start(bf16[1,192,2048]{2,1,0:T(8,128)(2,1)S(1)} %collective-permute-done.2.refs_3_) | copy-start | bytes 2359300
  142.5 55.7 %collective-permute-start.37 = (bf16[2,96,1024]{2,1,0:T(8,128)(2,1)S(1)}, bf16[2,96,1024]{2,1,0:T(8,128)(2,1)S(1)}, u32[]{:S(2)}, u32[]{:S(2)}) collective-permute-start(bf16[2,96,1024]{2,1,0:T(8,128)(2,1)S(1)} %fusion.2), channel_id=1, source_target_pairs={{0,4},{1,5},{2,6},{3,7},{4,0},{5,1},{6,2},{7,3},{8,12},{9,13},{10,... | collective-permute-start | bytes 1179656 | tf_op jit(solution)/shard_map/ppermute | solution.py:219
  168.6 2.0 collective-permute-start.19
  169.7 13.9 %collective-permute-start.21 = (bf16[192,1024]{1,0:T(8,128)(2,1)S(1)}, bf16[192,1024]{1,0:T(8,128)(2,1)S(1)}, u32[]{:S(2)}, u32[]{:S(2)}) collective-permute-start(bf16[192,1024]{1,0:T(8,128)(2,1)S(1)} %copy-done.22), channel_id=1, source_target_pairs={{0,1},{1,0},{2,3},{3,2},{4,5},{5,4},{6,7},{7,6},{8,9},{9,8},{10,11... | collective-permute-start | bytes 1179656 | tf_op jit(solution)/shard_map/ppermute | solution.py:219
  170.6 15.7 %collective-permute-start.23 = (bf16[192,1024]{1,0:T(8,128)(2,1)S(1)}, bf16[192,1024]{1,0:T(8,128)(2,1)S(1)}, u32[]{:S(2)}, u32[]{:S(2)}) collective-permute-start(bf16[192,1024]{1,0:T(8,128)(2,1)S(1)} %copy-done.21), channel_id=1, source_target_pairs={{0,1},{1,0},{2,3},{3,2},{4,5},{5,4},{6,7},{7,6},{8,9},{9,8},{10,11... | collective-permute-start | bytes 1179656 | tf_op jit(solution)/shard_map/ppermute | solution.py:219
  183.6 16.7 %collective-permute-start.39 = (bf16[2,96,1024]{2,1,0:T(8,128)(2,1)S(1)}, bf16[2,96,1024]{2,1,0:T(8,128)(2,1)S(1)}, u32[]{:S(2)}, u32[]{:S(2)}) collective-permute-start(bf16[2,96,1024]{2,1,0:T(8,128)(2,1)S(1)} %fusion.3), channel_id=1, source_target_pairs={{0,2},{1,3},{2,0},{3,1},{4,6},{5,7},{6,4},{7,5},{8,10},{9,11},{10,... | collective-permute-start | bytes 1179656 | tf_op jit(solution)/shard_map/ppermute | solution.py:219
  186.4 19.3 %collective-permute-start.18 = (bf16[192,1024]{1,0:T(8,128)(2,1)S(1)}, bf16[192,1024]{1,0:T(8,128)(2,1)S(1)}, u32[]{:S(2)}, u32[]{:S(2)}) collective-permute-start(bf16[192,1024]{1,0:T(8,128)(2,1)S(1)} %copy-done.20), channel_id=1, source_target_pairs={{0,1},{1,0},{2,3},{3,2},{4,5},{5,4},{6,7},{7,6},{8,9},{9,8},{10,11... | collective-permute-start | bytes 1179656 | tf_op jit(solution)/shard_map/ppermute | solution.py:219
  186.7 21.0 %collective-permute-start.20 = (bf16[192,1024]{1,0:T(8,128)(2,1)S(1)}, bf16[192,1024]{1,0:T(8,128)(2,1)S(1)}, u32[]{:S(2)}, u32[]{:S(2)}) collective-permute-start(bf16[192,1024]{1,0:T(8,128)(2,1)S(1)} %add.78), channel_id=1, source_target_pairs={{0,24},{8,0},{16,8},{24,16},{1,25},{9,1},{17,9},{25,17},{2,26},{10... | collective-permute-start | bytes 1179656 | tf_op jit(solution)/shard_map/ppermute | solution.py:222
  198.1 33.4 %collective-permute-start.22 = (bf16[192,1024]{1,0:T(8,128)(2,1)S(1)}, bf16[192,1024]{1,0:T(8,128)(2,1)S(1)}, u32[]{:S(2)}, u32[]{:S(2)}) collective-permute-start(bf16[192,1024]{1,0:T(8,128)(2,1)S(1)} %add.79), channel_id=1, source_target_pairs={{0,16},{8,24},{16,0},{24,8},{1,17},{9,25},{17,1},{25,9},{2,18},{10... | collective-permute-start | bytes 1179656 | tf_op jit(solution)/shard_map/ppermute | solution.py:222
  198.2 33.3 %collective-permute-start.24 = (bf16[192,1024]{1,0:T(8,128)(2,1)S(1)}, bf16[192,1024]{1,0:T(8,128)(2,1)S(1)}, u32[]{:S(2)}, u32[]{:S(2)}) collective-permute-start(bf16[192,1024]{1,0:T(8,128)(2,1)S(1)} %add.80), channel_id=1, source_target_pairs={{0,8},{8,16},{16,24},{24,0},{1,9},{9,17},{17,25},{25,1},{2,10},{10... | collective-permute-start | bytes 1179656 | tf_op jit(solution)/shard_map/ppermute | solution.py:222
  207.7 23.8 %copy-start.4 = (bf16[192,1024]{1,0:T(8,128)(2,1)}, bf16[192,1024]{1,0:T(8,128)(2,1)S(1)}, u32[]{:S(2)}) copy-start(bf16[192,1024]{1,0:T(8,128)(2,1)S(1)} %collective-permute-done.20.refs_1_) | copy-start | bytes 1179652
  (25 other events, 84.8 us)

commit v2 on v1

v2 whole, which is shorter than its diff:
```python
import functools

import jax
import jax.numpy as jnp
from jax import lax
from jax.experimental import pallas as pl
from jax.experimental.pallas import tpu as pltpu
from jax.sharding import PartitionSpec as P

BF16 = jnp.bfloat16
F32 = jnp.float32
ANY = pl.BlockSpec(memory_space=pl.ANY)
VMEM = pl.BlockSpec(memory_space=pltpu.VMEM)
SMEM = pl.BlockSpec(memory_space=pltpu.SMEM)
LIMIT = 56 * 1024 * 1024
ROWS = 16


def call(kernel, flops, moved, **kw):
    return pl.pallas_call(
        kernel,
        compiler_params=pltpu.CompilerParams(vmem_limit_bytes=LIMIT),
        cost_estimate=pl.CostEstimate(flops=int(flops), bytes_accessed=int(moved), transcendentals=0),
        **kw,
    )


def hidden_body(nd, top, chunks, pos, gu, wt, *rest):
    outs, keep, rows, packed = rest[: nd * chunks], rest[nd * chunks], rest[-2], rest[-1]
    step = pl.program_id(0)
    block, units = gu.shape[0], gu.shape[1] // 2
    g = gu[:, :units].astype(F32)
    u = gu[:, units:].astype(F32)
    h = g * jax.nn.sigmoid(g) * u
    for c in range(units // 128):
        rows[c, pl.ds(pl.multiple_of(step * block, block), block), :] = h[:, c * 128 : (c + 1) * 128]

    @pl.when(step == pl.num_programs(0) - 1)
    def _():
        tokens = wt.shape[1]
        slice_units = packed.shape[1]
        for k in range(top):
            for c in range(units // 128):
                part = rows[c, pl.ds(k, tokens, stride=top), :]
                part = part.T.astype(BF16)
                keep[c * 128 : (c + 1) * 128, k * tokens : (k + 1) * tokens] = part
        for z in range(nd):
            for k in range(top):
                w = wt[k : k + 1, :]
                part = keep[z * slice_units : (z + 1) * slice_units, k * tokens : (k + 1) * tokens]
                packed[z, :, k * tokens : (k + 1) * tokens] = (part.astype(F32) * w).astype(BF16)
        size = slice_units // chunks
        for s in range(nd):
            z = lax.rem(pos[0] + s, nd)
            for c in range(chunks):
                outs[s * chunks + c][0, :size, :] = packed[z, c * size : (c + 1) * size, :]


def spread(names, idv, top):
    for b in range(idv.shape[0]):
        rows = names[b].astype(F32)
        for k in range(top):
            idv[b, k] = jnp.broadcast_to(rows[k : k + 1, :], idv.shape[2:]).astype(BF16)


def tagged(eids, tokens):
    return [jnp.full((ROWS, tokens), eids[e], F32).astype(BF16) for e in range(eids.shape[0])]


def back_body(nw, groups, top, eids, *refs):
    ws, cots, outs = refs[:nw], refs[nw : nw + groups], refs[nw + groups : nw + 2 * groups]
    wv, cv, nv, idv, grads, sem = refs[nw + 2 * groups :]
    units, width = wv.shape[1:]
    blocks, tokens = idv.shape[0], idv.shape[3]
    per = blocks // groups
    copies = []
    for g in range(groups):
        copies.append(
            pltpu.make_async_copy(
                cots[g].at[:, pl.ds(0, width)], cv.at[pl.ds(g * per * tokens, per * tokens), :], sem.at[g]
            )
        )
        for b in range(per):
            src = cots[g].at[pl.ds(b * tokens, ROWS), pl.ds(width, tokens)]
            copies.append(pltpu.make_async_copy(src, nv.at[g * per + b], sem.at[groups + g * per + b]))
    at, places = 0, []
    for i, w in enumerate(ws):
        places.append((at, w.shape[0]))
        copies.append(pltpu.make_async_copy(w, wv.at[pl.ds(at, w.shape[0])], sem.at[groups + blocks + i]))
        at += w.shape[0]
    for c in copies:
        c.start()
    for c in copies[: groups + blocks]:
        c.wait()
    spread(nv, idv, top)
    tags = tagged(eids, tokens)
    for i, (start, count) in enumerate(places):
        copies[groups + blocks + i].wait()
        w = wv[start : start + count].reshape(count * units, width)
        got = lax.dot_general(w, cv[...], (((1,), (1,)), ((), ())), preferred_element_type=F32)
        grads[start : start + count] = got.astype(BF16).reshape(count, units, cv.shape[0])
    for s in range(blocks):
        cols = slice(s * tokens, (s + 1) * tokens)

        def body(j, _, s=s, cols=cols):
            f = pl.multiple_of(j * ROWS, ROWS)
            held = [grads[e, pl.ds(f, ROWS), cols] for e in range(at)]
            for k in range(top):
                row = idv[s, k]
                acc = jnp.zeros((ROWS, tokens), BF16)
                for e in range(at):
                    acc = jnp.where(row == tags[e], held[e], acc)
                outs[s // per][s % per, pl.ds(f, ROWS), k * tokens : (k + 1) * tokens] = acc
            return 0

        lax.fori_loop(0, units // ROWS, body, 0)


def down_body(top, plan, columns, eids, *refs):
    cots, hs, outs = refs[:2], refs[2:4], refs[4 : 4 + len(plan)]
    cv, hv, nv, idv, dense, result, sem = refs[4 + len(plan) :]
    experts, units = dense.shape[:2]
    nb, tokens = idv.shape[0], idv.shape[3]
    half = nb // 2
    width = cv.shape[1]
    early, late = [], []
    for i in range(2):
        early.append(pltpu.make_async_copy(hs[i], hv.at[pl.ds(i * half, half)], sem.at[i]))
        for b in range(half):
            src = cots[i].at[pl.ds(b * tokens, ROWS), pl.ds(width, tokens)]
            early.append(pltpu.make_async_copy(src, nv.at[i * half + b], sem.at[4 + i * half + b]))
        src = cots[i].at[:, pl.ds(0, width)]
        late.append(pltpu.make_async_copy(src, cv.at[pl.ds(i * half * tokens, half * tokens), :], sem.at[2 + i]))
    for c in early:
        c.start()
    for c in early:
        c.wait()
    for c in late:
        c.start()
    spread(nv, idv, top)
    tags = tagged(eids, tokens)
    for b in range(nb):
        cols = slice(b * tokens, (b + 1) * tokens)

        def body(j, _, b=b, cols=cols):
            f = pl.multiple_of(j * ROWS, ROWS)
            held = [hv[b, pl.ds(f, ROWS), k * tokens : (k + 1) * tokens] for k in range(top)]
            rows = [idv[b, k] for k in range(top)]
            for e in range(experts):
                acc = jnp.zeros((ROWS, tokens), BF16)
                for k in range(top):
                    acc = jnp.where(rows[k] == tags[e], held[k], acc)
                dense[e, pl.ds(f, ROWS), cols] = acc
            return 0

        lax.fori_loop(0, units // ROWS, body, 0)
    for c in late:
        c.wait()
    lhs = dense[...].reshape(experts * units, nb * tokens)
    copies = []
    for t, start in enumerate(range(0, width, columns)):
        got = jnp.dot(lhs, cv[:, start : start + columns], preferred_element_type=F32)
        result[t] = got.astype(BF16).reshape(experts, units, columns)
        for out, (groups, low, high) in zip(outs, plan):
            if low <= start < high:
                per = out.shape[1]
                for i, r in enumerate(groups):
                    dst = out.at[i, :, :, pl.ds(start - low, columns)]
                    src = result.at[t, pl.ds(r * per, per)]
                    copies.append(pltpu.make_async_copy(src, dst, sem.at[4 + nb + len(copies)]))
                    copies[-1].start()
    for c in copies:
        c.wait()


def final_body(nd, top, pos, *refs):
    backs, (g_ref, u_ref, wt, keep, out, route, turned, rows, held, sem) = refs[:nd], refs[nd:]
    step = pl.program_id(0)
    last = pl.num_programs(0) - 1
    tokens = wt.shape[1]
    units = turned.shape[0]

    @pl.when(step == 0)
    def _():
        size = backs[0].shape[0]
        for s in range(nd):
            at = pl.multiple_of(lax.rem(pos[0] + s, nd) * size, ROWS)
            turned[pl.ds(at, size), :] = backs[s][...]
        route[...] = jnp.zeros_like(route)

    f = pl.multiple_of(step * 128, 128)

    def copies(n):
        slot = lax.rem(n, 2)
        for i in range(2):
            col = pl.multiple_of(i * units + n * 128, 128)
            yield pltpu.make_async_copy(held.at[slot, i], out.at[:, pl.ds(col, 128)], sem.at[slot, i])

    for k in range(top):
        span = slice(k * tokens, (k + 1) * tokens)
        q = turned[pl.ds(f, 128), span].astype(F32)
        route[k : k + 1, :] += jnp.sum(q * keep[:, span].astype(F32), axis=0, keepdims=True)
        rows[pl.ds(k, tokens, stride=top), :] = (q * wt[k : k + 1, :]).T

    @pl.when(step >= 2)
    def _():
        for c in copies(step - 2):
            c.wait()

    slot = lax.rem(step, 2)
    g = g_ref[...].astype(F32)
    u = u_ref[...].astype(F32)
    d = rows[...]
    sig = jax.nn.sigmoid(g)
    held[slot, 0] = (d * u * sig * (1.0 + g * (1.0 - sig))).astype(BF16)
    held[slot, 1] = (d * (g * sig)).astype(BF16)
    for c in copies(step):
        c.start()

    @pl.when(step == last)
    def _():
        for n in (last - 1, last):
            for c in copies(n):
                c.wait()


def total_body(chunks, halves, parts, *refs):
    ins, out = refs[:-1], refs[-1]
    width = out.shape[3] // halves
    at = 0
    for c in range(chunks):
        for h in range(halves):
            acc = ins[at][0].astype(F32)
            for i in range(1, parts):
                acc = acc + ins[at + i][0].astype(F32)
            at += parts
            out[:, c, :, h * width : (h + 1) * width] = acc


def local(cotangent, saved_gate_up, route_ids, route_weights, w_down):
    tokens, top = route_ids.shape
    width = cotangent.shape[1]
    units = saved_gate_up.shape[2] // 2
    nd, ne = lax.axis_size("dp"), lax.axis_size("expert")
    per, size = w_down.shape[0], w_down.shape[1]
    routes = tokens * top
    chunks = 2 if (size // 2) % ROWS == 0 else 1
    part = size // chunks
    bits = ne.bit_length() - 1
    groups = ne // 2
    held = groups * per
    p = lax.axis_index("dp").astype(jnp.int32)
    q = lax.axis_index("expert").astype(jnp.int32)
    pos = p.reshape(1)

    def owner_of(r):
        return ((q // 2) ^ r) * 2 + q % 2

    def swap(a, mask):
        return lax.ppermute(a, "expert", [(i, i ^ mask) for i in range(ne)])

    def shift(a, s):
        return lax.ppermute(a, "dp", [(i, (i + s) % nd) for i in range(nd)])

    eids = jnp.stack([owner_of(r) * per + e for r in range(groups) for e in range(per)]).astype(F32)

    gu = saved_gate_up.reshape(routes, 2 * units)
    wt = route_weights.T

    names = jnp.zeros((tokens, 128 * -(-tokens // 128)), BF16).at[:top, :tokens].set(route_ids.T.astype(BF16))
    sent = jnp.concatenate([cotangent, names], 1)

    def after(a, *done):
        return lax.optimization_barrier((a,) + done)[0]

    block = routes // 8
    shapes = []
    for s in range(nd):
        for c in range(chunks):
            shapes.append(jax.ShapeDtypeStruct((1, part, routes), BF16))
    whole = lambda shape: pl.BlockSpec(shape, lambda i: (0,) * len(shape))
    made = call(
        functools.partial(hidden_body, nd, top, chunks),
        0,
        6 * units * routes * 4,
        grid=(8,),
        in_specs=[SMEM, pl.BlockSpec((block, 2 * units), lambda i: (i, 0)), whole((top, tokens))],
        out_specs=[whole(o.shape) for o in shapes] + [whole((units, routes))],
        out_shape=shapes + [jax.ShapeDtypeStruct((units, routes), BF16)],
        scratch_shapes=[pltpu.VMEM((units // 128, routes, 128), F32), pltpu.VMEM((nd, size, routes), BF16)],
    )(pos, gu, wt)
    keep = made[-1]
    hs = [[made[s * chunks + c] for s in range(nd)] for c in range(chunks)]

    near = [swap(w_down, 2), swap(w_down, 4)] if bits == 3 else []
    far = [shift(sent, s) for s in range(1, nd)]
    near, far, hs, keep, sent = lax.optimization_barrier((near, far, hs, keep, sent))

    if bits == 3:
        corner = [swap(near[0][: per // 2], 4), swap(near[1][per // 2 :], 2)]
        weights = [w_down] + near + corner
    else:
        weights = w_down
        for b in range(1, bits):
            weights = jnp.concatenate([weights, swap(weights, 1 << b)], 0)
        weights = [weights]
    cots = jnp.concatenate([sent] + far, 0)

    def send(c):
        return [hs[c][0]] + [shift(hs[c][s], s) for s in range(1, nd)]

    mine = [send(0)]
    weights, cots, mine, hs = lax.optimization_barrier((weights, cots, mine, hs))

    cots_theirs = swap(cots, 1)
    mine[0] = jnp.concatenate(mine[0], 0)
    theirs = [swap(mine[0], 1)]
    for c in range(1, chunks):
        mine.append(send(c))

    def back(eids, *cots):
        nw, ng = len(weights), len(cots)
        n = ng * nd * tokens
        return call(
            functools.partial(back_body, nw, ng, top),
            2 * held * size * width * n,
            2 * (held * size * width + n * width + n * top * size),
            in_specs=[SMEM] + [ANY] * (nw + ng),
            out_specs=[VMEM] * ng,
            out_shape=[jax.ShapeDtypeStruct((nd, size, routes), BF16)] * ng,
            scratch_shapes=[
                pltpu.VMEM((held, size, width), BF16),
                pltpu.VMEM((n, width), BF16),
                pltpu.VMEM((ng * nd, ROWS, tokens), BF16),
                pltpu.VMEM((ng * nd, top, ROWS, tokens), BF16),
                pltpu.VMEM((held, size, n), BF16),
                pltpu.SemaphoreType.DMA((nw + ng + ng * nd,)),
            ],
        )(eids, *weights, *cots)

    half = width // 2
    if bits == 3:
        plan = [((1, 3), 0, half), ((0, 2), 0, half), ((2, 3), half, width), ((0, 1), half, width)]
    else:
        plan = [(tuple(range(groups)), 0, width)]
    nb = 2 * nd
    columns = 512

    def down(eids, c):
        return call(
            functools.partial(down_body, top, plan, columns),
            2 * held * part * width * nb * tokens,
            2 * (held * part * width + nb * tokens * width + nb * routes * part),
            in_specs=[SMEM] + [ANY] * 4,
            out_specs=[ANY] * len(plan),
            out_shape=[jax.ShapeDtypeStruct((len(g), per, part, b - a), BF16) for g, a, b in plan],
            scratch_shapes=[
                pltpu.VMEM((nb * tokens, width), BF16),
                pltpu.VMEM((nb, part, routes), BF16),
                pltpu.VMEM((nb, ROWS, tokens), BF16),
                pltpu.VMEM((nb, top, ROWS, tokens), BF16),
                pltpu.VMEM((held, part, nb * tokens), BF16),
                pltpu.VMEM((width // columns, held, part, columns), BF16),
                pltpu.SemaphoreType.DMA((4 + nb + width // columns * groups,)),
            ],
        )(eids, cots, cots_theirs, mine[c], theirs[c])

    sums = [down(eids, 0)]
    weights, cots, cots_theirs, mine, theirs, sums = lax.optimization_barrier(
        (weights, cots, cots_theirs, mine, theirs, sums)
    )

    def first_step(parts):
        return [swap(parts[0], 2), swap(parts[2], 4)] if bits == 3 else []

    got = [first_step(sums[0])]
    for c in range(1, chunks):
        mine[c] = jnp.concatenate(mine[c], 0)
        theirs.append(swap(mine[c], 1))
    own, other = back(eids, cots, cots_theirs)
    cots, cots_theirs, mine, theirs, sums, got, own, other = lax.optimization_barrier(
        (cots, cots_theirs, mine, theirs, sums, got, own, other)
    )

    def second_step(parts, got):
        mids = [(parts[i][1:].astype(F32) + a[1:].astype(F32)).astype(BF16) for i, a in zip((1, 3), got)]
        return [swap(mids[0], 4), swap(mids[1], 2)]

    ends = [second_step(sums[0], got[0])] if bits == 3 else []
    other = swap(other, 1)
    for c in range(1, chunks):
        sums.append(down(eids, c))
    sums, got, ends, own, other = lax.optimization_barrier((sums, got, ends, own, other))

    for c in range(1, chunks):
        got.append(first_step(sums[c]))
    backs = [own[s] + other[s] for s in range(nd)]
    backs = [backs[0]] + [shift(backs[s], nd - s) for s in range(1, nd)]
    sums, got, backs = lax.optimization_barrier((sums, got, backs))

    terms = []
    if bits == 3:
        for c in range(chunks):
            if c:
                ends.append(second_step(sums[c], got[c]))
            for i in range(2):
                terms += [sums[c][2 * i + 1], got[c][i], ends[c][i]]
    else:
        for parts in sums:
            acc = parts[0]
            for b in reversed(range(1, bits)):
                n = acc.shape[0] // 2
                acc = (acc[:n].astype(F32) + swap(acc[n:], 1 << b).astype(F32)).astype(BF16)
            terms.append(acc)
    halves, parts = (2, 3) if bits == 3 else (1, 1)
    rows = part // 2 if part % (2 * ROWS) == 0 else part
    first = pl.BlockSpec((1, per, rows, width // halves), lambda j: (0, 0, j, 0))
    grad_down = call(
        functools.partial(total_body, chunks, halves, parts),
        0,
        2 * 5 * per * size * width,
        grid=(part // rows,),
        in_specs=[first] * len(terms),
        out_specs=pl.BlockSpec((per, chunks, rows, width), lambda j: (0, 0, j, 0)),
        out_shape=jax.ShapeDtypeStruct((per, chunks, part, width), F32),
    )(*terms).reshape(per, size, width)

    cols = units // 128
    out, route = call(
        functools.partial(final_body, nd, top),
        0,
        8 * units * routes * 4,
        grid=(cols,),
        in_specs=[SMEM]
        + [whole((size, routes))] * nd
        + [
            pl.BlockSpec((routes, 128), lambda i: (0, i)),
            pl.BlockSpec((routes, 128), lambda i: (0, cols + i)),
            whole((top, tokens)),
            pl.BlockSpec((128, routes), lambda i: (i, 0)),
        ],
        out_specs=[ANY, whole((top, tokens))],
        out_shape=[
            jax.ShapeDtypeStruct((routes, 2 * units), BF16),
            jax.ShapeDtypeStruct((top, tokens), F32),
        ],
        scratch_shapes=[
            pltpu.VMEM((units, routes), BF16),
            pltpu.VMEM((routes, 128), F32),
            pltpu.VMEM((2, 2, routes, 128), BF16),
            pltpu.SemaphoreType.DMA((2, 2)),
        ],
    )(pos, *backs, gu, gu, wt, keep)
    return out.reshape(tokens, top, 2 * units), route.T, grad_down


def solution(mesh):
    return jax.shard_map(
        local,
        mesh=mesh,
        in_specs=(
            P(("dp", "expert"), None),
            P(("dp", "expert"), None, None),
            P(("dp", "expert"), None),
            P(("dp", "expert"), None),
            P("expert", "dp", None),
        ),
        out_specs=(
            P(("dp", "expert"), None, None),
            P(("dp", "expert"), None),
            P("expert", "dp", None),
        ),
        check_vma=False,
    )
```

time: 243 us -> 191 us (0.79)
  starting transfers between devices: 71.7 us -> 49.5 us
  waiting for transfers between devices: 92.2 us -> 73.8 us
  local copies, waits for them, and re-layouts: 10.9 us -> 5.37 us
  Pallas kernels: 60.7 us -> 55.4 us
    ppermute x28 -> x16, waiting for transfers between devices: 35 us -> 1.19 us  [swap(): return lax.ppermute(a, 'expert', [(i, i ^ mask) for i in range(ne)])]
    ppermute x12, starting transfers between devices: 51.6 us -> 34.1 us  [shift(): return lax.ppermute(a, 'dp', [(i, (i + s) % nd) for i in range(nd)])]
    ppermute x12, waiting for transfers between devices: 57.2 us -> 72.7 us  [shift(): return lax.ppermute(a, 'dp', [(i, (i + s) % nd) for i in range(nd)])]
    squeeze x6 -> x0, local copies, waits for them, and re-layouts: 5.12 us -> none  [local(): terms += [kept[0], got[0], swap(mid, two)]]
    ppermute x28 -> x16, starting transfers between devices: 20.1 us -> 15.4 us  [swap(): return lax.ppermute(a, 'expert', [(i, i ^ mask) for i in range(ne)])]
    pallas_call x4 -> x3, Pallas kernels: 38.4 us -> 35.8 us  [the longest x2 18.1 us: down(): call(functools.partial(down_body, top, plan, columns), 2 * held * part *...]
    concatenate x0 -> x2, other arithmetic: none -> 2.46 us  [the longest x1 1.38 us: local(): cots = jnp.concatenate([sent] + far, 0)]
    add x4 -> x1, other arithmetic: 3.34 us -> 0.9 us  [local(): backs = [own[s] + other[s] for s in range(nd)]]
  transfers between devices with their start and end apart: 40 -> 28, of which waited for: 15 -> 11; matrix products, arithmetic and copies ran while one was open for 5% -> 3% of each run, Pallas kernels for 18% -> 27%
where the time goes in v2:
time: 191 us; the launch traced here: 190 us
  waiting for transfers between devices  73.8 us (39%)
  Pallas kernels  55.4 us (29%)
  starting transfers between devices  49.5 us (26%)
  local copies, waits for them, and re-layouts  5.37 us (3%)
  other arithmetic  5.2 us (3%)
    ppermute x12, waiting for transfers between devices, shift(): return lax.ppermute(a, 'dp', [(i, (i + s) % nd) for i in range(nd)])  72.7 us
    ppermute x12, starting transfers between devices, shift(): return lax.ppermute(a, 'dp', [(i, (i + s) % nd) for i in range(nd)])  34.1 us
    pallas_call x2, Pallas kernels, down(): call(functools.partial(down_body, top, plan, columns), 2 * held * part *...  18.1 us
    pallas_call x1, Pallas kernels, back(): call(functools.partial(back_body, nw, ng, top), 2 * held * size * width *...  17.8 us
    ppermute x16, starting transfers between devices, swap(): return lax.ppermute(a, 'expert', [(i, i ^ mask) for i in range(ne)])  15.4 us
    pallas_call x1, Pallas kernels, local(): call(functools.partial(final_body, nd, top), 0, 8 * units * routes * 4, g...  7.91 us
    pallas_call x1, Pallas kernels, local(): call(functools.partial(hidden_body, nd, top, chunks), 0, 6 * units * rout...  7.81 us
    pallas_call x1, Pallas kernels, local(): call(functools.partial(total_body, chunks, halves, parts), 0, 2 * 5 * per...  3.87 us
  transfers between devices with their start and end apart: 28, of which 11 were waited for; matrix products, arithmetic and copies ran while one was open for 3% of the time, Pallas kernels for 27%

profile of v2, /device:TPU:0, one launch (start us, length us, event | category | flops | bytes accessed | tf_op | source)
XLA Modules:
  0.0 190.4 jit_solution(8469358046649642497)
XLA Ops:
  0.6 3.0 %collective-permute-start = (bf16[2,192,2048]{2,1,0:T(8,128)(2,1)}, bf16[2,192,2048]{2,1,0:T(8,128)(2,1)}, u32[]{:S(2)}, u32[]{:S(2)}) collective-permute-start(bf16[2,192,2048]{2,1,0:T(8,128)(2,1)} %refs_0_), channel_id=1, source_target_pairs={{0,2},{1,3},{2,0},{3,1},{4,6},{5,7},{6,4},{7,5},{8,10},{9,11},{10,... | collective-permute-start | bytes 4718600 | tf_op jit(solution)/shard_map/ppermute | solution.py:260
  3.6 1.5 collective-permute-start.1
  5.2 0.7 convert_bitcast_fusion
  5.8 1.1 fusion.1
  6.9 1.6 collective-permute-start.2
  8.6 2.6 %collective-permute-start.3 = (bf16[128,2176]{1,0:T(8,128)(2,1)S(1)}, bf16[128,2176]{1,0:T(8,128)(2,1)S(1)}, u32[]{:S(2)}, u32[]{:S(2)}) collective-permute-start(bf16[128,2176]{1,0:T(8,128)(2,1)S(1)} %fusion.1), channel_id=1, source_target_pairs={{0,16},{8,24},{16,0},{24,8},{1,17},{9,25},{17,1},{25,9},{2,18},{10... | collective-permute-start | bytes 1671176 | tf_op jit(solution)/shard_map/ppermute | solution.py:263
  11.1 1.3 collective-permute-start.4
  12.5 7.8 %shard_map.76 = (bf16[1,96,1024]{2,1,0:T(8,128)(2,1)}, bf16[1,96,1024]{2,1,0:T(8,128)(2,1)}, bf16[1,96,1024]{2,1,0:T(8,128)(2,1)}, bf16[1,96,1024]{2,1,0:T(8,128...) custom-call(s32[1]{0:T(128)} %bitcast.pos, ...), custom_call_target="tpu_custom_call" | custom-call | bytes 18874368 | tf_op jit(solution)/shard_map/pallas_call | solution.py:282
  20.3 4.2 %collective-permute-done.2 = bf16[128,2176]{1,0:T(8,128)(2,1)S(1)} collective-permute-done((bf16[128,2176]{1,0:T(8,128)(2,1)S(1)}, bf16[128,2176]{1,0:T(8,128)(2,1)S(1)}, u32[]{:S(2)}, u32[]{:S(2)}) %collective-permute-start.2) | collective-permute-done | bytes 557088 | tf_op jit(solution)/shard_map/ppermute | solution.py:263
  24.5 22.2 %collective-permute-done.3 = bf16[128,2176]{1,0:T(8,128)(2,1)S(1)} collective-permute-done((bf16[128,2176]{1,0:T(8,128)(2,1)S(1)}, bf16[128,2176]{1,0:T(8,128)(2,1)S(1)}, u32[]{:S(2)}, u32[]{:S(2)}) %collective-permute-start.3) | collective-permute-done | bytes 557088 | tf_op jit(solution)/shard_map/ppermute | solution.py:263
  46.7 1.6 slice.70
  48.3 0.6 collective-permute-start.5
  48.8 1.2 slice.71
  50.1 0.6 collective-permute-start.6
  50.7 12.2 %collective-permute-start.7 = (bf16[1,96,1024]{2,1,0:T(8,128)(2,1)S(1)}, bf16[1,96,1024]{2,1,0:T(8,128)(2,1)S(1)}, u32[]{:S(2)}, u32[]{:S(2)}) collective-permute-start(bf16[1,96,1024]{2,1,0:T(8,128)(2,1)S(1)} %copy-done.29), channel_id=1, source_target_pairs={{0,8},{8,16},{16,24},{24,0},{1,9},{9,17},{17,25},{25,1},{2,10},{10... | collective-permute-start | bytes 589832 | tf_op jit(solution)/shard_map/ppermute | solution.py:263
  62.9 1.8 collective-permute-start.8
  64.7 0.7 collective-permute-start.9
  65.3 1.4 pad_maximum_fusion.refs_0_.refs_5_
  66.7 3.2 %collective-permute-done.7 = bf16[1,96,1024]{2,1,0:T(8,128)(2,1)S(1)} collective-permute-done((bf16[1,96,1024]{2,1,0:T(8,128)(2,1)S(1)}, bf16[1,96,1024]{2,1,0:T(8,128)(2,1)S(1)}, u32[]{:S(2)}, u32[]{:S(2)}) %collective-permute-start.7) | collective-permute-done | bytes 196640 | tf_op jit(solution)/shard_map/ppermute | solution.py:263
  69.9 6.0 %collective-permute-done.8 = bf16[1,96,1024]{2,1,0:T(8,128)(2,1)S(1)} collective-permute-done((bf16[1,96,1024]{2,1,0:T(8,128)(2,1)S(1)}, bf16[1,96,1024]{2,1,0:T(8,128)(2,1)S(1)}, u32[]{:S(2)}, u32[]{:S(2)}) %collective-permute-start.8) | collective-permute-done | bytes 196640 | tf_op jit(solution)/shard_map/ppermute | solution.py:263
  76.2 0.7 copy-done.23
  77.2 0.6 convert_element_type.47.eids
  77.8 5.3 %collective-permute-start.11 = (bf16[1,96,1024]{2,1,0:T(8,128)(2,1)}, bf16[1,96,1024]{2,1,0:T(8,128)(2,1)S(1)}, u32[]{:S(2)}, u32[]{:S(2)}) collective-permute-start(bf16[1,96,1024]{2,1,0:T(8,128)(2,1)} %get-tuple-element.148), channel_id=1, source_target_pairs={{0,8},{8,16},{16,24},{24,0},{1,9},{9,17},{17,25},{25,1},{2,10},{10... | collective-permute-start | bytes 589832 | tf_op jit(solution)/shard_map/ppermute | solution.py:263
  83.2 1.7 collective-permute-start.12
  84.9 0.7 collective-permute-start.13
  85.6 8.9 %shard_map.77 = (bf16[2,2,96,1024]{3,2,1,0:T(8,128)(2,1)}, bf16[2,2,96,1024]{3,2,1,0:T(8,128)(2,1)}, bf16[2,2,96,1024]{3,2,1,0:T(8,128)(2,1)}, bf16[2,2,96,1024]{3,2,1,0:T(8,128)(2,1)}) custom-call(f32[8]{0:T(128)} %convert_element_type.47.eids, bf16[512,2176]{1,0:T(8,128)(2,1)} %copy-done, bf16[512,2176]{1,0:T(8,128)(2,1)} %collective-permute-done.10.refs_1_.refs_6_, ...), custom_call_target="tpu_custom_call" | custom-call | flops 3221225472 | bytes 8912896 | tf_op jit(solution)/shard_map/pallas_call | solution.py:350
  94.5 4.0 %collective-permute-done.12 = bf16[1,96,1024]{2,1,0:T(8,128)(2,1)S(1)} collective-permute-done((bf16[1,96,1024]{2,1,0:T(8,128)(2,1)}, bf16[1,96,1024]{2,1,0:T(8,128)(2,1)S(1)}, u32[]{:S(2)}, u32[]{:S(2)}) %collective-permute-start.12) | collective-permute-done | bytes 196640 | tf_op jit(solution)/shard_map/ppermute | solution.py:263
  98.7 1.6 collective-permute-start.16
  100.3 1.5 collective-permute-start.17
  101.8 17.8 %shard_map.78 = (bf16[4,192,1024]{2,1,0:T(8,128)(2,1)}, bf16[4,192,1024]{2,1,0:T(8,128)(2,1)}) custom-call(f32[8]{0:T(128)} %convert_element_type.47.eids, bf16[2,192,2048]{2,1,0:T(8,128)(2,1)} %refs_0_, bf16[2,192,2048]{2,1,0:T(8,128)(2,1)} %collective-permute-done.refs_1_, bf16[2,192,2048]{2,1,0:T(8,128)(2,1)} %collective-permute-done.1.refs_2_, ...), custom_call_target="tpu_custom_call" | custom-call | flops 6442450944 | bytes 13631488 | tf_op jit(solution)/shard_map/pallas_call | solution.py:324
  119.6 0.5 collective-permute-done.17.refs_4_
  120.2 0.6 collective-permute-start.19
  121.0 1.6 collective-permute-start.18
  122.6 9.2 %shard_map.79 = (bf16[2,2,96,1024]{3,2,1,0:T(8,128)(2,1)}, bf16[2,2,96,1024]{3,2,1,0:T(8,128)(2,1)}, bf16[2,2,96,1024]{3,2,1,0:T(8,128)(2,1)}, bf16[2,2,96,1024]{3,2,1,0:T(8,128)(2,1)}) custom-call(f32[8]{0:T(128)} %convert_element_type.47.eids, bf16[512,2176]{1,0:T(8,128)(2,1)} %copy-done, bf16[512,2176]{1,0:T(8,128)(2,1)} %collective-permute-done.10.refs_1_.refs_6_, ...), custom_call_target="tpu_custom_call" | custom-call | flops 3221225472 | bytes 8912896 | tf_op jit(solution)/shard_map/pallas_call | solution.py:350
  131.8 0.5 collective-permute-done.18.refs_2_
  132.3 1.6 collective-permute-start.21
  133.9 1.5 collective-permute-start.22
  135.4 0.9 add_bitcast_fusion
  136.3 4.7 %collective-permute-start.23 = (bf16[192,1024]{1,0:T(8,128)(2,1)S(1)}, bf16[192,1024]{1,0:T(8,128)(2,1)S(1)}, u32[]{:S(2)}, u32[]{:S(2)}) collective-permute-start(bf16[192,1024]{1,0:T(8,128)(2,1)S(1)} %get-tuple-element.215), channel_id=1, source_target_pairs={{0,24},{8,0},{16,8},{24,16},{1,25},{9,1},{17,9},{25,17},{2,26},{10... | collective-permute-start | bytes 1179656 | tf_op jit(solution)/shard_map/ppermute | solution.py:263
  141.0 1.5 collective-permute-start.24
  142.4 8.2 %collective-permute-done.23.refs_1_ = bf16[192,1024]{1,0:T(8,128)(2,1)S(1)} collective-permute-done((bf16[192,1024]{1,0:T(8,128)(2,1)S(1)}, bf16[192,1024]{1,0:T(8,128)(2,1)S(1)}, u32[]{:S(2)}, u32[]{:S(2)}) %collective-permute-start.23) | collective-permute-done | bytes 393248 | tf_op jit(solution)/shard_map/ppermute | solution.py:263
  150.6 25.0 %collective-permute-done.24.refs_2_ = bf16[192,1024]{1,0:T(8,128)(2,1)S(1)} collective-permute-done((bf16[192,1024]{1,0:T(8,128)(2,1)S(1)}, bf16[192,1024]{1,0:T(8,128)(2,1)S(1)}, u32[]{:S(2)}, u32[]{:S(2)}) %collective-permute-start.24) | collective-permute-done | bytes 393248 | tf_op jit(solution)/shard_map/ppermute | solution.py:263
  175.7 0.6 collective-permute-start.27
  176.5 0.6 collective-permute-start.26
  177.1 7.9 %shard_map.80 = (bf16[1024,1536]{1,0:T(8,128)(2,1)}, f32[8,128]{1,0:T(8,128)}) custom-call(s32[1]{0:T(128)} %bitcast.pos, bf16[192,1024]{1,0:T(8,128)(2,1)} %get-tuple-element.196.refs_0_, bf16[192,1024]{1,0:T(8,128)(2,1)} %copy-done.14, bf16[192,1024]{1,0:T(8,128)(2,1)} %copy-done.15, bf16[192,1024]{1,0:T(8,128)(2,1)} %copy-done.16, ...), custom_call_target="tpu_custom_call" | custom-call | bytes 25165824 | tf_op jit(solution)/shard_map/pallas_call | solution.py:429
  185.2 0.6 copy-done.17
  185.8 0.7 copy-done.18
  186.6 3.9 %shard_map.81 = f32[2,2,96,2048]{3,2,1,0:T(8,128)} custom-call(bf16[2,2,96,1024]{3,2,1,0:T(8,128)(2,1)} %get-tuple-element.203.refs_0_, bf16[2,2,96,1024]{3,2,1,0:T(8,128)(2,1)} %copy-done.3, bf16[1,2,96,1024]{3,2,1,0:T(8,128)(2,1)} %copy-done.13, bf16[2,2,96,1024]{3,2,1,0:T(8,128)(2,1)} %get-tuple-element.206.refs_3_, bf16[2,2,96,1024]{3,2,1,0:T(8,128)(2,1)} %copy-done.4, ...), custom_call_target="tpu_custom_call" | custom-call | bytes 7864320 | tf_op jit(solution)/shard_map/pallas_call | solution.py:418
  (94 shorter events, 1.5 us)
Async XLA Ops:
  0.6 46.0 %collective-permute-start = (bf16[2,192,2048]{2,1,0:T(8,128)(2,1)}, bf16[2,192,2048]{2,1,0:T(8,128)(2,1)}, u32[]{:S(2)}, u32[]{:S(2)}) collective-permute-start(bf16[2,192,2048]{2,1,0:T(8,128)(2,1)} %refs_0_), channel_id=1, source_target_pairs={{0,2},{1,3},{2,0},{3,1},{4,6},{5,7},{6,4},{7,5},{8,10},{9,11},{10,... | collective-permute-start | bytes 4718600 | tf_op jit(solution)/shard_map/ppermute | solution.py:260
  3.6 43.0 %collective-permute-start.1 = (bf16[2,192,2048]{2,1,0:T(8,128)(2,1)}, bf16[2,192,2048]{2,1,0:T(8,128)(2,1)}, u32[]{:S(2)}, u32[]{:S(2)}) collective-permute-start(bf16[2,192,2048]{2,1,0:T(8,128)(2,1)} %refs_0_), channel_id=1, source_target_pairs={{0,4},{1,5},{2,6},{3,7},{4,0},{5,1},{6,2},{7,3},{8,12},{9,13},{10,... | collective-permute-start | bytes 4718600 | tf_op jit(solution)/shard_map/ppermute | solution.py:260
  6.9 17.6 %collective-permute-start.2 = (bf16[128,2176]{1,0:T(8,128)(2,1)S(1)}, bf16[128,2176]{1,0:T(8,128)(2,1)S(1)}, u32[]{:S(2)}, u32[]{:S(2)}) collective-permute-start(bf16[128,2176]{1,0:T(8,128)(2,1)S(1)} %fusion.1), channel_id=1, source_target_pairs={{0,8},{8,16},{16,24},{24,0},{1,9},{9,17},{17,25},{25,1},{2,10},{10... | collective-permute-start | bytes 1671176 | tf_op jit(solution)/shard_map/ppermute | solution.py:263
  8.6 38.1 %collective-permute-start.3 = (bf16[128,2176]{1,0:T(8,128)(2,1)S(1)}, bf16[128,2176]{1,0:T(8,128)(2,1)S(1)}, u32[]{:S(2)}, u32[]{:S(2)}) collective-permute-start(bf16[128,2176]{1,0:T(8,128)(2,1)S(1)} %fusion.1), channel_id=1, source_target_pairs={{0,16},{8,24},{16,0},{24,8},{1,17},{9,25},{17,1},{25,9},{2,18},{10... | collective-permute-start | bytes 1671176 | tf_op jit(solution)/shard_map/ppermute | solution.py:263
  11.1 35.5 %collective-permute-start.4 = (bf16[128,2176]{1,0:T(8,128)(2,1)S(1)}, bf16[128,2176]{1,0:T(8,128)(2,1)S(1)}, u32[]{:S(2)}, u32[]{:S(2)}) collective-permute-start(bf16[128,2176]{1,0:T(8,128)(2,1)S(1)} %fusion.1), channel_id=1, source_target_pairs={{0,24},{8,0},{16,8},{24,16},{1,25},{9,1},{17,9},{25,17},{2,26},{10... | collective-permute-start | bytes 1671176 | tf_op jit(solution)/shard_map/ppermute | solution.py:263
  20.3 30.4 %copy-start.29 = (bf16[1,96,1024]{2,1,0:T(8,128)(2,1)S(1)}, bf16[1,96,1024]{2,1,0:T(8,128)(2,1)}, u32[]{:S(2)}) copy-start(bf16[1,96,1024]{2,1,0:T(8,128)(2,1)} %get-tuple-element.130) | copy-start | bytes 589828
  20.3 42.6 %copy-start.28 = (bf16[1,96,1024]{2,1,0:T(8,128)(2,1)S(1)}, bf16[1,96,1024]{2,1,0:T(8,128)(2,1)}, u32[]{:S(2)}) copy-start(bf16[1,96,1024]{2,1,0:T(8,128)(2,1)} %get-tuple-element.131) | copy-start | bytes 589828
  20.3 44.3 %copy-start.27 = (bf16[1,96,1024]{2,1,0:T(8,128)(2,1)S(1)}, bf16[1,96,1024]{2,1,0:T(8,128)(2,1)}, u32[]{:S(2)}) copy-start(bf16[1,96,1024]{2,1,0:T(8,128)(2,1)} %get-tuple-element.132) | copy-start | bytes 589828
  46.7 18.0 %copy-start.10 = (bf16[128,2176]{1,0:T(8,128)(2,1)}, bf16[128,2176]{1,0:T(8,128)(2,1)S(1)}, u32[]{:S(2)}) copy-start(bf16[128,2176]{1,0:T(8,128)(2,1)S(1)} %collective-permute-done.3) | copy-start | bytes 1671172
  46.7 18.0 %copy-start.11 = (bf16[128,2176]{1,0:T(8,128)(2,1)}, bf16[128,2176]{1,0:T(8,128)(2,1)S(1)}, u32[]{:S(2)}) copy-start(bf16[128,2176]{1,0:T(8,128)(2,1)S(1)} %collective-permute-done.4) | copy-start | bytes 1671172
  48.3 27.7 %collective-permute-start.5 = (bf16[1,192,2048]{2,1,0:T(8,128)(2,1)S(1)}, bf16[1,192,2048]{2,1,0:T(8,128)(2,1)S(1)}, u32[]{:S(2)}, u32[]{:S(2)}) collective-permute-start(bf16[1,192,2048]{2,1,0:T(8,128)(2,1)S(1)} %slice.70), channel_id=1, source_target_pairs={{0,4},{1,5},{2,6},{3,7},{4,0},{5,1},{6,2},{7,3},{8,12},{9,13},{10,... | collective-permute-start | bytes 2359304 | tf_op jit(solution)/shard_map/ppermute | solution.py:260
  50.0 26.0 %copy-start.20 = (bf16[1,96,1024]{2,1,0:T(8,128)(2,1)S(1)}, bf16[1,96,1024]{2,1,0:T(8,128)(2,1)}, u32[]{:S(2)}) copy-start(bf16[1,96,1024]{2,1,0:T(8,128)(2,1)} %get-tuple-element.143) | copy-start | bytes 589828
  50.0 34.8 %copy-start.26 = (bf16[1,96,1024]{2,1,0:T(8,128)(2,1)S(1)}, bf16[1,96,1024]{2,1,0:T(8,128)(2,1)}, u32[]{:S(2)}) copy-start(bf16[1,96,1024]{2,1,0:T(8,128)(2,1)} %get-tuple-element.150) | copy-start | bytes 589828
  50.1 25.9 %collective-permute-start.6 = (bf16[1,192,2048]{2,1,0:T(8,128)(2,1)S(1)}, bf16[1,192,2048]{2,1,0:T(8,128)(2,1)S(1)}, u32[]{:S(2)}, u32[]{:S(2)}) collective-permute-start(bf16[1,192,2048]{2,1,0:T(8,128)(2,1)S(1)} %slice.71), channel_id=1, source_target_pairs={{0,2},{1,3},{2,0},{3,1},{4,6},{5,7},{6,4},{7,5},{8,10},{9,11},{10,... | collective-permute-start | bytes 2359304 | tf_op jit(solution)/shard_map/ppermute | solution.py:260
  50.7 19.3 %collective-permute-start.7 = (bf16[1,96,1024]{2,1,0:T(8,128)(2,1)S(1)}, bf16[1,96,1024]{2,1,0:T(8,128)(2,1)S(1)}, u32[]{:S(2)}, u32[]{:S(2)}) collective-permute-start(bf16[1,96,1024]{2,1,0:T(8,128)(2,1)S(1)} %copy-done.29), channel_id=1, source_target_pairs={{0,8},{8,16},{16,24},{24,0},{1,9},{9,17},{17,25},{25,1},{2,10},{10... | collective-permute-start | bytes 589832 | tf_op jit(solution)/shard_map/ppermute | solution.py:263
  62.9 13.1 %collective-permute-start.8 = (bf16[1,96,1024]{2,1,0:T(8,128)(2,1)S(1)}, bf16[1,96,1024]{2,1,0:T(8,128)(2,1)S(1)}, u32[]{:S(2)}, u32[]{:S(2)}) collective-permute-start(bf16[1,96,1024]{2,1,0:T(8,128)(2,1)S(1)} %copy-done.28), channel_id=1, source_target_pairs={{0,16},{8,24},{16,0},{24,8},{1,17},{9,25},{17,1},{25,9},{2,18},{10... | collective-permute-start | bytes 589832 | tf_op jit(solution)/shard_map/ppermute | solution.py:263
  64.7 11.3 %collective-permute-start.9 = (bf16[1,96,1024]{2,1,0:T(8,128)(2,1)S(1)}, bf16[1,96,1024]{2,1,0:T(8,128)(2,1)S(1)}, u32[]{:S(2)}, u32[]{:S(2)}) collective-permute-start(bf16[1,96,1024]{2,1,0:T(8,128)(2,1)S(1)} %copy-done.27), channel_id=1, source_target_pairs={{0,24},{8,0},{16,8},{24,16},{1,25},{9,1},{17,9},{25,17},{2,26},{10... | collective-permute-start | bytes 589832 | tf_op jit(solution)/shard_map/ppermute | solution.py:263
  66.7 18.8 %copy-start = (bf16[512,2176]{1,0:T(8,128)(2,1)}, bf16[512,2176]{1,0:T(8,128)(2,1)S(1)}, u32[]{:S(2)}) copy-start(bf16[512,2176]{1,0:T(8,128)(2,1)S(1)} %pad_maximum_fusion.refs_0_.refs_5_) | copy-start | bytes 6684676
  76.0 9.6 %collective-permute-start.10 = (bf16[512,2176]{1,0:T(8,128)(2,1)S(1)}, bf16[512,2176]{1,0:T(8,128)(2,1)}, u32[]{:S(2)}, u32[]{:S(2)}) collective-permute-start(bf16[512,2176]{1,0:T(8,128)(2,1)S(1)} %pad_maximum_fusion.refs_0_.refs_5_), channel_id=1, source_target_pairs={{0,1},{1,0},{2,3},{3,2},{4,5},{5,4},{6,7},{7,6},{8,9},{9,8},{10,11... | collective-permute-start | bytes 6684680 | tf_op jit(solution)/shard_map/ppermute | solution.py:260
  77.1 8.4 %collective-permute-start.14 = (bf16[4,96,1024]{2,1,0:T(8,128)(2,1)S(1)}, bf16[4,96,1024]{2,1,0:T(8,128)(2,1)}, u32[]{:S(2)}, u32[]{:S(2)}) collective-permute-start(bf16[4,96,1024]{2,1,0:T(8,128)(2,1)S(1)} %constant_dynamic-update-slice_fusion.refs_2_), channel_id=1, source_target_pairs={{0,1},{1,0},{2,3},{3,2},{4,5},{5,4},{6,7},{7,6},{8,9},{9,8},{10,11... | collective-permute-start | bytes 2359304 | tf_op jit(solution)/shard_map/ppermute | solution.py:260
  77.8 20.7 %copy-start.19 = (bf16[1,96,1024]{2,1,0:T(8,128)(2,1)S(1)}, bf16[1,96,1024]{2,1,0:T(8,128)(2,1)}, u32[]{:S(2)}) copy-start(bf16[1,96,1024]{2,1,0:T(8,128)(2,1)} %get-tuple-element.157) | copy-start | bytes 589828
  77.8 16.7 %collective-permute-start.11 = (bf16[1,96,1024]{2,1,0:T(8,128)(2,1)}, bf16[1,96,1024]{2,1,0:T(8,128)(2,1)S(1)}, u32[]{:S(2)}, u32[]{:S(2)}) collective-permute-start(bf16[1,96,1024]{2,1,0:T(8,128)(2,1)} %get-tuple-element.148), channel_id=1, source_target_pairs={{0,8},{8,16},{16,24},{24,0},{1,9},{9,17},{17,25},{25,1},{2,10},{10... | collective-permute-start | bytes 589832 | tf_op jit(solution)/shard_map/ppermute | solution.py:263
  83.2 15.3 %collective-permute-start.12 = (bf16[1,96,1024]{2,1,0:T(8,128)(2,1)}, bf16[1,96,1024]{2,1,0:T(8,128)(2,1)S(1)}, u32[]{:S(2)}, u32[]{:S(2)}) collective-permute-start(bf16[1,96,1024]{2,1,0:T(8,128)(2,1)} %get-tuple-element.149), channel_id=1, source_target_pairs={{0,16},{8,24},{16,0},{24,8},{1,17},{9,25},{17,1},{25,9},{2,18},{10... | collective-permute-start | bytes 589832 | tf_op jit(solution)/shard_map/ppermute | solution.py:263
  84.9 13.6 %collective-permute-start.13 = (bf16[1,96,1024]{2,1,0:T(8,128)(2,1)S(1)}, bf16[1,96,1024]{2,1,0:T(8,128)(2,1)S(1)}, u32[]{:S(2)}, u32[]{:S(2)}) collective-permute-start(bf16[1,96,1024]{2,1,0:T(8,128)(2,1)S(1)} %copy-done.26), channel_id=1, source_target_pairs={{0,24},{8,0},{16,8},{24,16},{1,25},{9,1},{17,9},{25,17},{2,26},{10... | collective-permute-start | bytes 589832 | tf_op jit(solution)/shard_map/ppermute | solution.py:263
  98.6 21.0 %copy-start.22 = (bf16[4,96,1024]{2,1,0:T(8,128)(2,1)}, bf16[4,96,1024]{2,1,0:T(8,128)(2,1)S(1)}, u32[]{:S(2)}) copy-start(bf16[4,96,1024]{2,1,0:T(8,128)(2,1)S(1)} %constant_dynamic-update-slice_fusion.4.refs_2_) | copy-start | bytes 2359300
  98.6 21.5 %copy-start.2 = (bf16[2,2,96,1024]{3,2,1,0:T(8,128)(2,1)S(1)}, bf16[2,2,96,1024]{3,2,1,0:T(8,128)(2,1)}, u32[]{:S(2)}) copy-start(bf16[2,2,96,1024]{3,2,1,0:T(8,128)(2,1)} %get-tuple-element.206.refs_3_) | copy-start | bytes 2359300
  98.6 22.2 %copy-start.1 = (bf16[2,2,96,1024]{3,2,1,0:T(8,128)(2,1)S(1)}, bf16[2,2,96,1024]{3,2,1,0:T(8,128)(2,1)}, u32[]{:S(2)}) copy-start(bf16[2,2,96,1024]{3,2,1,0:T(8,128)(2,1)} %get-tuple-element.203.refs_0_) | copy-start | bytes 2359300
  98.6 20.9 %collective-permute-start.15 = (bf16[4,96,1024]{2,1,0:T(8,128)(2,1)S(1)}, bf16[4,96,1024]{2,1,0:T(8,128)(2,1)S(1)}, u32[]{:S(2)}, u32[]{:S(2)}) collective-permute-start(bf16[4,96,1024]{2,1,0:T(8,128)(2,1)S(1)} %constant_dynamic-update-slice_fusion.4.refs_2_), channel_id=1, source_target_pairs={{0,1},{1,0},{2,3},{3,2},{4,5},{5,4},{6,7},{7,6},{8,9},{9,8},{10,11... | collective-permute-start | bytes 2359304 | tf_op jit(solution)/shard_map/ppermute | solution.py:260
  98.7 20.9 %collective-permute-start.16 = (bf16[2,2,96,1024]{3,2,1,0:T(8,128)(2,1)}, bf16[2,2,96,1024]{3,2,1,0:T(8,128)(2,1)S(1)}, u32[]{:S(2)}, u32[]{:S(2)}) collective-permute-start(bf16[2,2,96,1024]{3,2,1,0:T(8,128)(2,1)} %get-tuple-element.161), channel_id=1, source_target_pairs={{0,2},{1,3},{2,0},{3,1},{4,6},{5,7},{6,4},{7,5},{8,10},{9,11},{10,... | collective-permute-start | bytes 2359304 | tf_op jit(solution)/shard_map/ppermute | solution.py:260
  100.3 19.8 %collective-permute-start.17 = (bf16[2,2,96,1024]{3,2,1,0:T(8,128)(2,1)}, bf16[2,2,96,1024]{3,2,1,0:T(8,128)(2,1)S(1)}, u32[]{:S(2)}, u32[]{:S(2)}) collective-permute-start(bf16[2,2,96,1024]{3,2,1,0:T(8,128)(2,1)} %get-tuple-element.163), channel_id=1, source_target_pairs={{0,4},{1,5},{2,6},{3,7},{4,0},{5,1},{6,2},{7,3},{8,12},{9,13},{10,... | collective-permute-start | bytes 2359304 | tf_op jit(solution)/shard_map/ppermute | solution.py:260
  119.6 12.1 %copy-start.3 = (bf16[2,2,96,1024]{3,2,1,0:T(8,128)(2,1)}, bf16[2,2,96,1024]{3,2,1,0:T(8,128)(2,1)S(1)}, u32[]{:S(2)}) copy-start(bf16[2,2,96,1024]{3,2,1,0:T(8,128)(2,1)S(1)} %collective-permute-done.16.refs_1_) | copy-start | bytes 2359300
  120.1 11.7 %copy-start.4 = (bf16[2,2,96,1024]{3,2,1,0:T(8,128)(2,1)}, bf16[2,2,96,1024]{3,2,1,0:T(8,128)(2,1)S(1)}, u32[]{:S(2)}) copy-start(bf16[2,2,96,1024]{3,2,1,0:T(8,128)(2,1)S(1)} %collective-permute-done.17.refs_4_) | copy-start | bytes 2359300
  120.1 12.2 %collective-permute-start.20 = (bf16[4,192,1024]{2,1,0:T(8,128)(2,1)}, bf16[4,192,1024]{2,1,0:T(8,128)(2,1)S(1)}, u32[]{:S(2)}, u32[]{:S(2)}) collective-permute-start(bf16[4,192,1024]{2,1,0:T(8,128)(2,1)} %get-tuple-element.185), channel_id=1, source_target_pairs={{0,1},{1,0},{2,3},{3,2},{4,5},{5,4},{6,7},{7,6},{8,9},{9,8},{10,11... | collective-permute-start | bytes 4718600 | tf_op jit(solution)/shard_map/ppermute | solution.py:260
  120.2 11.6 %collective-permute-start.19 = (bf16[1,2,96,1024]{3,2,1,0:T(8,128)(2,1)S(1)}, bf16[1,2,96,1024]{3,2,1,0:T(8,128)(2,1)S(1)}, u32[]{:S(2)}, u32[]{:S(2)}) collective-permute-start(bf16[1,2,96,1024]{3,2,1,0:T(8,128)(2,1)S(1)} %add_convert_fusion.2), channel_id=1, source_target_pairs={{0,2},{1,3},{2,0},{3,1},{4,6},{5,7},{6,4},{7,5},{8,10},{9,11},{10,... | collective-permute-start | bytes 1179656 | tf_op jit(solution)/shard_map/ppermute | solution.py:260
  121.0 14.4 %copy-start.9 = (bf16[4,192,1024]{2,1,0:T(8,128)(2,1)S(1)}, bf16[4,192,1024]{2,1,0:T(8,128)(2,1)}, u32[]{:S(2)}) copy-start(bf16[4,192,1024]{2,1,0:T(8,128)(2,1)} %get-tuple-element.194) | copy-start | bytes 4718596
  121.0 11.3 %collective-permute-start.18 = (bf16[1,2,96,1024]{3,2,1,0:T(8,128)(2,1)S(1)}, bf16[1,2,96,1024]{3,2,1,0:T(8,128)(2,1)S(1)}, u32[]{:S(2)}, u32[]{:S(2)}) collective-permute-start(bf16[1,2,96,1024]{3,2,1,0:T(8,128)(2,1)S(1)} %add_convert_fusion.3), channel_id=1, source_target_pairs={{0,4},{1,5},{2,6},{3,7},{4,0},{5,1},{6,2},{7,3},{8,12},{9,13},{10,... | collective-permute-start | bytes 1179656 | tf_op jit(solution)/shard_map/ppermute | solution.py:260
  132.3 43.3 %copy-start.6 = (bf16[2,2,96,1024]{3,2,1,0:T(8,128)(2,1)S(1)}, bf16[2,2,96,1024]{3,2,1,0:T(8,128)(2,1)}, u32[]{:S(2)}) copy-start(bf16[2,2,96,1024]{3,2,1,0:T(8,128)(2,1)} %get-tuple-element.211.refs_9_) | copy-start | bytes 2359300
  132.3 44.1 %copy-start.5 = (bf16[2,2,96,1024]{3,2,1,0:T(8,128)(2,1)S(1)}, bf16[2,2,96,1024]{3,2,1,0:T(8,128)(2,1)}, u32[]{:S(2)}) copy-start(bf16[2,2,96,1024]{3,2,1,0:T(8,128)(2,1)} %get-tuple-element.209.refs_6_) | copy-start | bytes 2359300
  132.3 43.3 %collective-permute-start.21 = (bf16[2,2,96,1024]{3,2,1,0:T(8,128)(2,1)}, bf16[2,2,96,1024]{3,2,1,0:T(8,128)(2,1)S(1)}, u32[]{:S(2)}, u32[]{:S(2)}) collective-permute-start(bf16[2,2,96,1024]{3,2,1,0:T(8,128)(2,1)} %get-tuple-element.188), channel_id=1, source_target_pairs={{0,2},{1,3},{2,0},{3,1},{4,6},{5,7},{6,4},{7,5},{8,10},{9,11},{10,... | collective-permute-start | bytes 2359304 | tf_op jit(solution)/shard_map/ppermute | solution.py:260
  133.9 41.7 %collective-permute-start.22 = (bf16[2,2,96,1024]{3,2,1,0:T(8,128)(2,1)}, bf16[2,2,96,1024]{3,2,1,0:T(8,128)(2,1)S(1)}, u32[]{:S(2)}, u32[]{:S(2)}) collective-permute-start(bf16[2,2,96,1024]{3,2,1,0:T(8,128)(2,1)} %get-tuple-element.190), channel_id=1, source_target_pairs={{0,4},{1,5},{2,6},{3,7},{4,0},{5,1},{6,2},{7,3},{8,12},{9,13},{10,... | collective-permute-start | bytes 2359304 | tf_op jit(solution)/shard_map/ppermute | solution.py:260
  136.3 14.3 %collective-permute-start.23 = (bf16[192,1024]{1,0:T(8,128)(2,1)S(1)}, bf16[192,1024]{1,0:T(8,128)(2,1)S(1)}, u32[]{:S(2)}, u32[]{:S(2)}) collective-permute-start(bf16[192,1024]{1,0:T(8,128)(2,1)S(1)} %get-tuple-element.215), channel_id=1, source_target_pairs={{0,24},{8,0},{16,8},{24,16},{1,25},{9,1},{17,9},{25,17},{2,26},{10... | collective-permute-start | bytes 1179656 | tf_op jit(solution)/shard_map/ppermute | solution.py:263
  141.0 34.6 %collective-permute-start.24 = (bf16[192,1024]{1,0:T(8,128)(2,1)S(1)}, bf16[192,1024]{1,0:T(8,128)(2,1)S(1)}, u32[]{:S(2)}, u32[]{:S(2)}) collective-permute-start(bf16[192,1024]{1,0:T(8,128)(2,1)S(1)} %get-tuple-element.214), channel_id=1, source_target_pairs={{0,16},{8,24},{16,0},{24,8},{1,17},{9,25},{17,1},{25,9},{2,18},{10... | collective-permute-start | bytes 1179656 | tf_op jit(solution)/shard_map/ppermute | solution.py:263
  142.4 33.1 %collective-permute-start.25 = (bf16[192,1024]{1,0:T(8,128)(2,1)S(1)}, bf16[192,1024]{1,0:T(8,128)(2,1)S(1)}, u32[]{:S(2)}, u32[]{:S(2)}) collective-permute-start(bf16[192,1024]{1,0:T(8,128)(2,1)S(1)} %get-tuple-element.213), channel_id=1, source_target_pairs={{0,8},{8,16},{16,24},{24,0},{1,9},{9,17},{17,25},{25,1},{2,10},{10... | collective-permute-start | bytes 1179656 | tf_op jit(solution)/shard_map/ppermute | solution.py:263
  150.6 26.5 %copy-start.14 = (bf16[192,1024]{1,0:T(8,128)(2,1)}, bf16[192,1024]{1,0:T(8,128)(2,1)S(1)}, u32[]{:S(2)}) copy-start(bf16[192,1024]{1,0:T(8,128)(2,1)S(1)} %collective-permute-done.23.refs_1_) | copy-start | bytes 1179652
  175.6 9.5 %copy-start.7 = (bf16[2,2,96,1024]{3,2,1,0:T(8,128)(2,1)}, bf16[2,2,96,1024]{3,2,1,0:T(8,128)(2,1)S(1)}, u32[]{:S(2)}) copy-start(bf16[2,2,96,1024]{3,2,1,0:T(8,128)(2,1)S(1)} %collective-permute-done.21.refs_7_) | copy-start | bytes 2359300
  175.6 9.5 %copy-start.8 = (bf16[2,2,96,1024]{3,2,1,0:T(8,128)(2,1)}, bf16[2,2,96,1024]{3,2,1,0:T(8,128)(2,1)S(1)}, u32[]{:S(2)}) copy-start(bf16[2,2,96,1024]{3,2,1,0:T(8,128)(2,1)S(1)} %collective-permute-done.22.refs_10_) | copy-start | bytes 2359300
  175.7 9.3 %collective-permute-start.27 = (bf16[1,2,96,1024]{3,2,1,0:T(8,128)(2,1)S(1)}, bf16[1,2,96,1024]{3,2,1,0:T(8,128)(2,1)S(1)}, u32[]{:S(2)}, u32[]{:S(2)}) collective-permute-start(bf16[1,2,96,1024]{3,2,1,0:T(8,128)(2,1)S(1)} %add_convert_fusion), channel_id=1, source_target_pairs={{0,2},{1,3},{2,0},{3,1},{4,6},{5,7},{6,4},{7,5},{8,10},{9,11},{10,... | collective-permute-start | bytes 1179656 | tf_op jit(solution)/shard_map/ppermute | solution.py:260
  176.5 8.7 %collective-permute-start.26 = (bf16[1,2,96,1024]{3,2,1,0:T(8,128)(2,1)S(1)}, bf16[1,2,96,1024]{3,2,1,0:T(8,128)(2,1)S(1)}, u32[]{:S(2)}, u32[]{:S(2)}) collective-permute-start(bf16[1,2,96,1024]{3,2,1,0:T(8,128)(2,1)S(1)} %add_convert_fusion.1), channel_id=1, source_target_pairs={{0,4},{1,5},{2,6},{3,7},{4,0},{5,1},{6,2},{7,3},{8,12},{9,13},{10,... | collective-permute-start | bytes 1179656 | tf_op jit(solution)/shard_map/ppermute | solution.py:260
  (10 other events, 26.6 us)

commit v3 on v2

--- a/solution.py
+++ b/solution.py
@@ -68,52 +68,63 @@
 
 
 def back_body(nw, groups, top, eids, *refs):
-    ws, cots, outs = refs[:nw], refs[nw : nw + groups], refs[nw + groups : nw + 2 * groups]
-    wv, cv, nv, idv, grads, sem = refs[nw + 2 * groups :]
+    ng = len(groups)
+    ws, cots, refs = refs[:nw], refs[nw : nw + ng], refs[nw + ng :]
+    earlier = sum(begun for _, begun in groups)
+    befores, outs = refs[:earlier], refs[earlier : earlier + ng]
+    wv, cv, nv, idv, grads, pv, sem = refs[earlier + ng :]
     units, width = wv.shape[1:]
     blocks, tokens = idv.shape[0], idv.shape[3]
-    per = blocks // groups
-    copies = []
-    for g in range(groups):
-        copies.append(
-            pltpu.make_async_copy(
-                cots[g].at[:, pl.ds(0, width)], cv.at[pl.ds(g * per * tokens, per * tokens), :], sem.at[g]
-            )
-        )
+    per = blocks // ng
+    ready, copies = [], []
+    for g in range(ng):
+        rows = pl.ds(g * per * tokens, per * tokens)
+        ready.append(pltpu.make_async_copy(cots[g].at[:, pl.ds(0, width)], cv.at[rows, :], sem.at[g]))
         for b in range(per):
             src = cots[g].at[pl.ds(b * tokens, ROWS), pl.ds(width, tokens)]
-            copies.append(pltpu.make_async_copy(src, nv.at[g * per + b], sem.at[groups + g * per + b]))
+            ready.append(pltpu.make_async_copy(src, nv.at[g * per + b], sem.at[ng + g * per + b]))
     at, places = 0, []
     for i, w in enumerate(ws):
         places.append((at, w.shape[0]))
-        copies.append(pltpu.make_async_copy(w, wv.at[pl.ds(at, w.shape[0])], sem.at[groups + blocks + i]))
+        copies.append(pltpu.make_async_copy(w, wv.at[pl.ds(at, w.shape[0])], sem.at[ng + blocks + i]))
         at += w.shape[0]
-    for c in copies:
+    for i in range(earlier):
+        copies.append(pltpu.make_async_copy(befores[i], pv.at[i], sem.at[ng + blocks + nw + i]))
+    for c in ready + copies:
         c.start()
-    for c in copies[: groups + blocks]:
+    for c in ready:
         c.wait()
     spread(nv, idv, top)
     tags = tagged(eids, tokens)
     for i, (start, count) in enumerate(places):
-        copies[groups + blocks + i].wait()
+        copies[i].wait()
+        meets = [g for g in range(ng) if groups[g][0] <= i]
+        low, high = meets[0] * per * tokens, (meets[-1] + 1) * per * tokens
         w = wv[start : start + count].reshape(count * units, width)
-        got = lax.dot_general(w, cv[...], (((1,), (1,)), ((), ())), preferred_element_type=F32)
-        grads[start : start + count] = got.astype(BF16).reshape(count, units, cv.shape[0])
-    for s in range(blocks):
-        cols = slice(s * tokens, (s + 1) * tokens)
-
-        def body(j, _, s=s, cols=cols):
-            f = pl.multiple_of(j * ROWS, ROWS)
-            held = [grads[e, pl.ds(f, ROWS), cols] for e in range(at)]
-            for k in range(top):
-                row = idv[s, k]
-                acc = jnp.zeros((ROWS, tokens), BF16)
-                for e in range(at):
-                    acc = jnp.where(row == tags[e], held[e], acc)
-                outs[s // per][s % per, pl.ds(f, ROWS), k * tokens : (k + 1) * tokens] = acc
-            return 0
-
-        lax.fori_loop(0, units // ROWS, body, 0)
+        got = lax.dot_general(w, cv[low:high, :], (((1,), (1,)), ((), ())), preferred_element_type=F32)
+        grads[start : start + count, :, low:high] = got.astype(BF16).reshape(count, units, high - low)
+    for c in copies[nw:]:
+        c.wait()
+    source = 0
+    for g, (first, begun) in enumerate(groups):
+        for s in range(per):
+            block = g * per + s
+            cols = slice(block * tokens, (block + 1) * tokens)
+
+            def body(j, _, g=g, s=s, block=block, cols=cols, begin=places[first][0], begun=begun, source=source):
+                f = pl.multiple_of(j * ROWS, ROWS)
+                held = {e: grads[e, pl.ds(f, ROWS), cols] for e in range(begin, at)}
+                for k in range(top):
+                    span = slice(k * tokens, (k + 1) * tokens)
+                    row = idv[block, k]
+                    acc = pv[source, s, pl.ds(f, ROWS), span] if begun else jnp.zeros((ROWS, tokens), BF16)
+                    for e in held:
+                        acc = jnp.where(row == tags[e], held[e], acc)
+                    outs[g][s, pl.ds(f, ROWS), span] = acc
+                return 0
+
+            lax.fori_loop(0, units // ROWS, body, 0)
+        source += begun
 
 
 def down_body(top, plan, columns, eids, *refs):
@@ -292,7 +303,29 @@
     keep = made[-1]
     hs = [[made[s * chunks + c] for s in range(nd)] for c in range(chunks)]
 
-    near = [swap(w_down, 2), swap(w_down, 4)] if bits == 3 else []
+    def back(weights, groups, cots, befores):
+        nw, ng, count = len(weights), len(cots), sum(w.shape[0] for w in weights)
+        n = ng * nd * tokens
+        return call(
+            functools.partial(back_body, nw, groups, top),
+            2 * count * size * width * n,
+            2 * (count * size * width + n * width + n * top * size),
+            in_specs=[SMEM] + [ANY] * (nw + ng + len(befores)),
+            out_specs=[VMEM] * ng,
+            out_shape=[jax.ShapeDtypeStruct((nd, size, routes), BF16)] * ng,
+            scratch_shapes=[
+                pltpu.VMEM((count, size, width), BF16),
+                pltpu.VMEM((n, width), BF16),
+                pltpu.VMEM((ng * nd, ROWS, tokens), BF16),
+                pltpu.VMEM((ng * nd, top, ROWS, tokens), BF16),
+                pltpu.VMEM((count, size, n), BF16),
+                pltpu.VMEM((max(1, len(befores)), nd, size, routes), BF16),
+                pltpu.SemaphoreType.DMA((nw + ng + ng * nd + len(befores),)),
+            ],
+        )(eids[:count], *weights, *cots, *befores)
+
+    first = after(w_down, sent)
+    near = [swap(first, 2), swap(first, 4)] if bits == 3 else []
     far = [shift(sent, s) for s in range(1, nd)]
     near, far, hs, keep, sent = lax.optimization_barrier((near, far, hs, keep, sent))
 
@@ -310,33 +343,8 @@
         return [hs[c][0]] + [shift(hs[c][s], s) for s in range(1, nd)]
 
     mine = [send(0)]
-    weights, cots, mine, hs = lax.optimization_barrier((weights, cots, mine, hs))
-
-    cots_theirs = swap(cots, 1)
-    mine[0] = jnp.concatenate(mine[0], 0)
-    theirs = [swap(mine[0], 1)]
-    for c in range(1, chunks):
-        mine.append(send(c))
-
-    def back(eids, *cots):
-        nw, ng = len(weights), len(cots)
-        n = ng * nd * tokens
-        return call(
-            functools.partial(back_body, nw, ng, top),
-            2 * held * size * width * n,
-            2 * (held * size * width + n * width + n * top * size),
-            in_specs=[SMEM] + [ANY] * (nw + ng),
-            out_specs=[VMEM] * ng,
-            out_shape=[jax.ShapeDtypeStruct((nd, size, routes), BF16)] * ng,
-            scratch_shapes=[
-                pltpu.VMEM((held, size, width), BF16),
-                pltpu.VMEM((n, width), BF16),
-                pltpu.VMEM((ng * nd, ROWS, tokens), BF16),
-                pltpu.VMEM((ng * nd, top, ROWS, tokens), BF16),
-                pltpu.VMEM((held, size, n), BF16),
-                pltpu.SemaphoreType.DMA((nw + ng + ng * nd,)),
-            ],
-        )(eids, *weights, *cots)
+    begun = back(weights[:3], ((0, False),), [cots], []) if bits == 3 else []
+    weights, cots, mine, hs, begun = lax.optimization_barrier((weights, cots, mine, hs, begun))
 
     half = width // 2
     if bits == 3:
@@ -365,38 +373,45 @@
             ],
         )(eids, cots, cots_theirs, mine[c], theirs[c])
 
-    sums = [down(eids, 0)]
-    weights, cots, cots_theirs, mine, theirs, sums = lax.optimization_barrier(
-        (weights, cots, cots_theirs, mine, theirs, sums)
+    cots_theirs = swap(cots, 1)
+    mine[0] = jnp.concatenate(mine[0], 0)
+    theirs = [swap(mine[0], 1)]
+    for c in range(1, chunks):
+        mine.append(send(c))
+    groups_met = ((3 if bits == 3 else 0, bits == 3), (0, False))
+    own, other = back(weights, groups_met, [cots, cots_theirs], begun)
+    cots, cots_theirs, mine, theirs, own, other = lax.optimization_barrier(
+        (cots, cots_theirs, mine, theirs, own, other)
     )
 
-    def first_step(parts):
-        return [swap(parts[0], 2), swap(parts[2], 4)] if bits == 3 else []
-
-    got = [first_step(sums[0])]
+    other = swap(other, 1)
     for c in range(1, chunks):
         mine[c] = jnp.concatenate(mine[c], 0)
         theirs.append(swap(mine[c], 1))
-    own, other = back(eids, cots, cots_theirs)
-    cots, cots_theirs, mine, theirs, sums, got, own, other = lax.optimization_barrier(
-        (cots, cots_theirs, mine, theirs, sums, got, own, other)
+    sums = [down(eids, 0)]
+    cots, cots_theirs, mine, theirs, own, other, sums = lax.optimization_barrier(
+        (cots, cots_theirs, mine, theirs, own, other, sums)
     )
+
+    def first_step(parts):
+        return [swap(parts[0], 2), swap(parts[2], 4)] if bits == 3 else []
 
     def second_step(parts, got):
         mids = [(parts[i][1:].astype(F32) + a[1:].astype(F32)).astype(BF16) for i, a in zip((1, 3), got)]
         return [swap(mids[0], 4), swap(mids[1], 2)]
 
-    ends = [second_step(sums[0], got[0])] if bits == 3 else []
-    other = swap(other, 1)
+    got = [first_step(sums[0])]
+    backs = [own[s] + other[s] for s in range(nd)]
+    backs = [a if s in (0, nd // 2) else shift(a, nd - s) for s, a in enumerate(backs)]
     for c in range(1, chunks):
         sums.append(down(eids, c))
-    sums, got, ends, own, other = lax.optimization_barrier((sums, got, ends, own, other))
-
+    sums, got, backs = lax.optimization_barrier((sums, got, backs))
+
+    backs[nd // 2] = shift(backs[nd // 2], nd - nd // 2)
     for c in range(1, chunks):
         got.append(first_step(sums[c]))
-    backs = [own[s] + other[s] for s in range(nd)]
-    backs = [backs[0]] + [shift(backs[s], nd - s) for s in range(1, nd)]
-    sums, got, backs = lax.optimization_barrier((sums, got, backs))
+    ends = [second_step(sums[0], got[0])] if bits == 3 else []
+    sums, got, backs, ends = lax.optimization_barrier((sums, got, backs, ends))
 
     terms = []
     if bits == 3:

time: 191 us -> 179 us (0.937)
  waiting for transfers between devices: 73.8 us -> 56.4 us
  Pallas kernels: 55.4 us -> 60.5 us
    ppermute x12, waiting for transfers between devices: 72.7 us -> 34.2 us  [shift(): return lax.ppermute(a, 'dp', [(i, (i + s) % nd) for i in range(nd)])]
    ppermute x16, waiting for transfers between devices: 1.19 us -> 22.3 us  [swap(): return lax.ppermute(a, 'expert', [(i, i ^ mask) for i in range(ne)])]
    pallas_call x1 -> x2, Pallas kernels: 17.8 us -> 22.8 us  [back(): call(functools.partial(back_body, nw, groups, top), 2 * count * size * wi...]
    unnamed x66 -> x69, local copies, waits for them, and re-layouts: 2.49 us -> 4.62 us
  transfers between devices with their start and end apart: 28 -> 28, of which waited for: 11 -> 8; matrix products, arithmetic and copies ran while one was open for 3% -> 2% of each run, Pallas kernels for 27% -> 32%
where the time goes in v3:
time: 179 us; the launch traced here: 178 us
  Pallas kernels  60.5 us (34%)
  waiting for transfers between devices  56.4 us (32%)
  starting transfers between devices  49.1 us (27%)
  local copies, waits for them, and re-layouts  7.19 us (4%)
  other arithmetic  3.71 us (2%)
    ppermute x12, waiting for transfers between devices, shift(): return lax.ppermute(a, 'dp', [(i, (i + s) % nd) for i in range(nd)])  34.2 us
    ppermute x12, starting transfers between devices, shift(): return lax.ppermute(a, 'dp', [(i, (i + s) % nd) for i in range(nd)])  33.5 us
    pallas_call x2, Pallas kernels, back(): call(functools.partial(back_body, nw, groups, top), 2 * count * size * wi...  22.8 us
    ppermute x16, waiting for transfers between devices, swap(): return lax.ppermute(a, 'expert', [(i, i ^ mask) for i in range(ne)])  22.3 us
    pallas_call x2, Pallas kernels, down(): call(functools.partial(down_body, top, plan, columns), 2 * held * part *...  18.1 us
    ppermute x16, starting transfers between devices, swap(): return lax.ppermute(a, 'expert', [(i, i ^ mask) for i in range(ne)])  15.6 us
    pallas_call x1, Pallas kernels, local(): call(functools.partial(final_body, nd, top), 0, 8 * units * routes * 4, g...  7.88 us
    pallas_call x1, Pallas kernels, local(): call(functools.partial(hidden_body, nd, top, chunks), 0, 6 * units * rout...  7.83 us
  transfers between devices with their start and end apart: 28, of which 8 were waited for; matrix products, arithmetic and copies ran while one was open for 2% of the time, Pallas kernels for 32%

profile of v3, /device:TPU:0, one launch (start us, length us, event | category | flops | bytes accessed | tf_op | source)
XLA Modules:
  0.0 178.1 jit_solution(12336217932804152246)
XLA Ops:
  0.6 0.7 convert_bitcast_fusion
  1.3 1.1 fusion.1
  2.4 3.0 %collective-permute-start = (bf16[2,192,2048]{2,1,0:T(8,128)(2,1)}, bf16[2,192,2048]{2,1,0:T(8,128)(2,1)}, u32[]{:S(2)}, u32[]{:S(2)}) collective-permute-start(bf16[2,192,2048]{2,1,0:T(8,128)(2,1)} %refs_0_.2), channel_id=1, source_target_pairs={{0,2},{1,3},{2,0},{3,1},{4,6},{5,7},{6,4},{7,5},{8,10},{9,11},{10,... | collective-permute-start | bytes 4718600 | tf_op jit(solution)/shard_map/ppermute | solution.py:271
  5.4 1.5 collective-permute-start.1
  6.9 1.6 collective-permute-start.2
  8.5 2.6 %collective-permute-start.3 = (bf16[128,2176]{1,0:T(8,128)(2,1)S(1)}, bf16[128,2176]{1,0:T(8,128)(2,1)S(1)}, u32[]{:S(2)}, u32[]{:S(2)}) collective-permute-start(bf16[128,2176]{1,0:T(8,128)(2,1)S(1)} %fusion.1), channel_id=1, source_target_pairs={{0,16},{8,24},{16,0},{24,8},{1,17},{9,25},{17,1},{25,9},{2,18},{10... | collective-permute-start | bytes 1671176 | tf_op jit(solution)/shard_map/ppermute | solution.py:274
  11.1 1.3 collective-permute-start.4
  12.5 0.5 convert_element_type.47.eids
  13.0 7.8 %shard_map.76 = (bf16[1,96,1024]{2,1,0:T(8,128)(2,1)}, bf16[1,96,1024]{2,1,0:T(8,128)(2,1)}, bf16[1,96,1024]{2,1,0:T(8,128)(2,1)}, bf16[1,96,1024]{2,1,0:T(8,128...) custom-call(s32[1]{0:T(128)} %bitcast.pos, ...), custom_call_target="tpu_custom_call" | custom-call | bytes 18874368 | tf_op jit(solution)/shard_map/pallas_call | solution.py:293
  20.9 3.6 %collective-permute-done.2 = bf16[128,2176]{1,0:T(8,128)(2,1)S(1)} collective-permute-done((bf16[128,2176]{1,0:T(8,128)(2,1)S(1)}, bf16[128,2176]{1,0:T(8,128)(2,1)S(1)}, u32[]{:S(2)}, u32[]{:S(2)}) %collective-permute-start.2) | collective-permute-done | bytes 557088 | tf_op jit(solution)/shard_map/ppermute | solution.py:274
  24.4 22.2 %collective-permute-done.3 = bf16[128,2176]{1,0:T(8,128)(2,1)S(1)} collective-permute-done((bf16[128,2176]{1,0:T(8,128)(2,1)S(1)}, bf16[128,2176]{1,0:T(8,128)(2,1)S(1)}, u32[]{:S(2)}, u32[]{:S(2)}) %collective-permute-start.3) | collective-permute-done | bytes 557088 | tf_op jit(solution)/shard_map/ppermute | solution.py:274
  46.7 1.2 slice.73
  47.9 0.6 collective-permute-start.5
  48.4 1.2 slice.74
  49.7 0.6 collective-permute-start.6
  50.3 12.4 %collective-permute-start.7 = (bf16[1,96,1024]{2,1,0:T(8,128)(2,1)}, bf16[1,96,1024]{2,1,0:T(8,128)(2,1)S(1)}, u32[]{:S(2)}, u32[]{:S(2)}) collective-permute-start(bf16[1,96,1024]{2,1,0:T(8,128)(2,1)} %get-tuple-element.130), channel_id=1, source_target_pairs={{0,8},{8,16},{16,24},{24,0},{1,9},{9,17},{17,25},{25,1},{2,10},{10... | collective-permute-start | bytes 589832 | tf_op jit(solution)/shard_map/ppermute | solution.py:274
  62.7 1.6 collective-permute-start.8
  64.3 0.8 collective-permute-start.9
  65.2 1.4 copy-done.18
  66.6 8.8 %shard_map.77.refs_7_ = bf16[4,192,1024]{2,1,0:T(8,128)(2,1)} custom-call(f32[6]{0:T(128)} %bitcast.33, bf16[2,192,2048]{2,1,0:T(8,128)(2,1)} %refs_0_.2, bf16[2,192,2048]{2,1,0:T(8,128)(2,1)} %collective-permute-done.refs_1_, bf16[2,192,2048]{2,1,0:T(8,128)(2,1)} %collective-permute-done.1.refs_2_, bf16[512,2176]{1,0:T(8,128)(2,1)} %copy-done.18), custom_call_target="tpu_custom_call" | custom-call | flops 2415919104 | bytes 8388608 | tf_op jit(solution)/shard_map/pallas_call | solution.py:309
  75.9 0.6 collective-permute-start.14
  76.4 5.6 %collective-permute-start.11 = (bf16[1,96,1024]{2,1,0:T(8,128)(2,1)S(1)}, bf16[1,96,1024]{2,1,0:T(8,128)(2,1)S(1)}, u32[]{:S(2)}, u32[]{:S(2)}) collective-permute-start(bf16[1,96,1024]{2,1,0:T(8,128)(2,1)S(1)} %copy-done.27), channel_id=1, source_target_pairs={{0,8},{8,16},{16,24},{24,0},{1,9},{9,17},{17,25},{25,1},{2,10},{10... | collective-permute-start | bytes 589832 | tf_op jit(solution)/shard_map/ppermute | solution.py:274
  82.1 1.6 collective-permute-start.12
  83.7 0.8 collective-permute-start.13
  84.5 1.4 copy-done.21
  85.9 14.1 %shard_map.78 = (bf16[4,192,1024]{2,1,0:T(8,128)(2,1)}, bf16[4,192,1024]{2,1,0:T(8,128)(2,1)}) custom-call(f32[8]{0:T(128)} %convert_element_type.47.eids, bf16[2,192,2048]{2,1,0:T(8,128)(2,1)} %refs_0_.2, bf16[2,192,2048]{2,1,0:T(8,128)(2,1)} %collective-permute-done.refs_1_, bf16[2,192,2048]{2,1,0:T(8,128)(2,1)} %collective-permute-done.1.refs_2_, ...), custom_call_target="tpu_custom_call" | custom-call | flops 6442450944 | bytes 13631488 | tf_op jit(solution)/shard_map/pallas_call | solution.py:309
  100.2 0.6 collective-permute-start.15
  100.9 9.1 %shard_map.79 = (bf16[2,2,96,1024]{3,2,1,0:T(8,128)(2,1)}, bf16[2,2,96,1024]{3,2,1,0:T(8,128)(2,1)}, bf16[2,2,96,1024]{3,2,1,0:T(8,128)(2,1)}, bf16[2,2,96,1024]{3,2,1,0:T(8,128)(2,1)}) custom-call(f32[8]{0:T(128)} %convert_element_type.47.eids, bf16[512,2176]{1,0:T(8,128)(2,1)} %copy-done.18, bf16[512,2176]{1,0:T(8,128)(2,1)} %copy-done.21, ...), custom_call_target="tpu_custom_call" | custom-call | flops 3221225472 | bytes 8912896 | tf_op jit(solution)/shard_map/pallas_call | solution.py:358
  110.0 0.8 collective-permute-start.17
  110.8 1.5 collective-permute-start.18
  112.3 0.9 add_bitcast_fusion
  113.2 4.4 %collective-permute-start.19 = (bf16[192,1024]{1,0:T(8,128)(2,1)S(1)}, bf16[192,1024]{1,0:T(8,128)(2,1)S(1)}, u32[]{:S(2)}, u32[]{:S(2)}) collective-permute-start(bf16[192,1024]{1,0:T(8,128)(2,1)S(1)} %get-tuple-element.213), channel_id=1, source_target_pairs={{0,24},{8,0},{16,8},{24,16},{1,25},{9,1},{17,9},{25,17},{2,26},{10... | collective-permute-start | bytes 1179656 | tf_op jit(solution)/shard_map/ppermute | solution.py:274
  117.6 9.1 %shard_map.80 = (bf16[2,2,96,1024]{3,2,1,0:T(8,128)(2,1)}, bf16[2,2,96,1024]{3,2,1,0:T(8,128)(2,1)}, bf16[2,2,96,1024]{3,2,1,0:T(8,128)(2,1)}, bf16[2,2,96,1024]{3,2,1,0:T(8,128)(2,1)}) custom-call(f32[8]{0:T(128)} %convert_element_type.47.eids, bf16[512,2176]{1,0:T(8,128)(2,1)} %copy-done.18, bf16[512,2176]{1,0:T(8,128)(2,1)} %copy-done.21, ...), custom_call_target="tpu_custom_call" | custom-call | flops 3221225472 | bytes 8912896 | tf_op jit(solution)/shard_map/pallas_call | solution.py:358
  126.7 0.5 collective-permute-done.19.refs_1_
  127.2 7.7 %collective-permute-done.20.refs_3_ = bf16[192,1024]{1,0:T(8,128)(2,1)S(1)} collective-permute-done((bf16[192,1024]{1,0:T(8,128)(2,1)S(1)}, bf16[192,1024]{1,0:T(8,128)(2,1)S(1)}, u32[]{:S(2)}, u32[]{:S(2)}) %collective-permute-start.20) | collective-permute-done | bytes 393248 | tf_op jit(solution)/shard_map/ppermute | solution.py:274
  134.9 0.7 collective-permute-start.21
  135.6 0.5 collective-permute-start.22
  136.3 1.4 collective-permute-start.25
  137.9 1.6 collective-permute-start.24
  139.4 0.7 collective-permute-start.23
  140.2 21.9 %collective-permute-done.25.refs_5_ = bf16[1,2,96,1024]{3,2,1,0:T(8,128)(2,1)S(1)} collective-permute-done((bf16[1,2,96,1024]{3,2,1,0:T(8,128)(2,1)S(1)}, bf16[1,2,96,1024]{3,2,1,0:T(8,128)(2,1)S(1)}, u32[]{:S(2)}, u32[]{:S(2)}) %collective-permute-start.25) | collective-permute-done | bytes 393248 | tf_op jit(solution)/shard_map/ppermute | solution.py:271
  162.0 0.3 collective-permute-done.24.refs_2_
  162.5 1.5 collective-permute-start.27
  164.2 0.6 collective-permute-start.26
  164.8 7.9 %shard_map.81 = (bf16[1024,1536]{1,0:T(8,128)(2,1)}, f32[8,128]{1,0:T(8,128)}) custom-call(s32[1]{0:T(128)} %bitcast.pos, bf16[192,1024]{1,0:T(8,128)(2,1)} %get-tuple-element.194.refs_0_, bf16[192,1024]{1,0:T(8,128)(2,1)} %copy-done.9, bf16[192,1024]{1,0:T(8,128)(2,1)} %copy-done.13, bf16[192,1024]{1,0:T(8,128)(2,1)} %copy-done.10, ...), custom_call_target="tpu_custom_call" | custom-call | bytes 25165824 | tf_op jit(solution)/shard_map/pallas_call | solution.py:444
  172.8 0.7 copy-done.14
  173.5 0.7 copy-done.15
  174.2 3.9 %shard_map.82 = f32[2,2,96,2048]{3,2,1,0:T(8,128)} custom-call(bf16[2,2,96,1024]{3,2,1,0:T(8,128)(2,1)} %get-tuple-element.201.refs_0_, bf16[2,2,96,1024]{3,2,1,0:T(8,128)(2,1)} %copy-done.2, bf16[1,2,96,1024]{3,2,1,0:T(8,128)(2,1)} %copy-done.12, bf16[2,2,96,1024]{3,2,1,0:T(8,128)(2,1)} %get-tuple-element.204.refs_3_, bf16[2,2,96,1024]{3,2,1,0:T(8,128)(2,1)} %copy-done.3, ...), custom_call_target="tpu_custom_call" | custom-call | bytes 7864320 | tf_op jit(solution)/shard_map/pallas_call | solution.py:433
  (98 shorter events, 1.7 us)
Async XLA Ops:
  2.4 44.2 %collective-permute-start = (bf16[2,192,2048]{2,1,0:T(8,128)(2,1)}, bf16[2,192,2048]{2,1,0:T(8,128)(2,1)}, u32[]{:S(2)}, u32[]{:S(2)}) collective-permute-start(bf16[2,192,2048]{2,1,0:T(8,128)(2,1)} %refs_0_.2), channel_id=1, source_target_pairs={{0,2},{1,3},{2,0},{3,1},{4,6},{5,7},{6,4},{7,5},{8,10},{9,11},{10,... | collective-permute-start | bytes 4718600 | tf_op jit(solution)/shard_map/ppermute | solution.py:271
  5.4 41.2 %collective-permute-start.1 = (bf16[2,192,2048]{2,1,0:T(8,128)(2,1)}, bf16[2,192,2048]{2,1,0:T(8,128)(2,1)}, u32[]{:S(2)}, u32[]{:S(2)}) collective-permute-start(bf16[2,192,2048]{2,1,0:T(8,128)(2,1)} %refs_0_.2), channel_id=1, source_target_pairs={{0,4},{1,5},{2,6},{3,7},{4,0},{5,1},{6,2},{7,3},{8,12},{9,13},{10,... | collective-permute-start | bytes 4718600 | tf_op jit(solution)/shard_map/ppermute | solution.py:271
  6.9 17.5 %collective-permute-start.2 = (bf16[128,2176]{1,0:T(8,128)(2,1)S(1)}, bf16[128,2176]{1,0:T(8,128)(2,1)S(1)}, u32[]{:S(2)}, u32[]{:S(2)}) collective-permute-start(bf16[128,2176]{1,0:T(8,128)(2,1)S(1)} %fusion.1), channel_id=1, source_target_pairs={{0,8},{8,16},{16,24},{24,0},{1,9},{9,17},{17,25},{25,1},{2,10},{10... | collective-permute-start | bytes 1671176 | tf_op jit(solution)/shard_map/ppermute | solution.py:274
  8.5 38.1 %collective-permute-start.3 = (bf16[128,2176]{1,0:T(8,128)(2,1)S(1)}, bf16[128,2176]{1,0:T(8,128)(2,1)S(1)}, u32[]{:S(2)}, u32[]{:S(2)}) collective-permute-start(bf16[128,2176]{1,0:T(8,128)(2,1)S(1)} %fusion.1), channel_id=1, source_target_pairs={{0,16},{8,24},{16,0},{24,8},{1,17},{9,25},{17,1},{25,9},{2,18},{10... | collective-permute-start | bytes 1671176 | tf_op jit(solution)/shard_map/ppermute | solution.py:274
  11.1 35.5 %collective-permute-start.4 = (bf16[128,2176]{1,0:T(8,128)(2,1)S(1)}, bf16[128,2176]{1,0:T(8,128)(2,1)S(1)}, u32[]{:S(2)}, u32[]{:S(2)}) collective-permute-start(bf16[128,2176]{1,0:T(8,128)(2,1)S(1)} %fusion.1), channel_id=1, source_target_pairs={{0,24},{8,0},{16,8},{24,16},{1,25},{9,1},{17,9},{25,17},{2,26},{10... | collective-permute-start | bytes 1671176 | tf_op jit(solution)/shard_map/ppermute | solution.py:274
  20.9 41.8 %copy-start.29 = (bf16[1,96,1024]{2,1,0:T(8,128)(2,1)S(1)}, bf16[1,96,1024]{2,1,0:T(8,128)(2,1)}, u32[]{:S(2)}) copy-start(bf16[1,96,1024]{2,1,0:T(8,128)(2,1)} %get-tuple-element.131) | copy-start | bytes 589828
  20.9 43.4 %copy-start.28 = (bf16[1,96,1024]{2,1,0:T(8,128)(2,1)S(1)}, bf16[1,96,1024]{2,1,0:T(8,128)(2,1)}, u32[]{:S(2)}) copy-start(bf16[1,96,1024]{2,1,0:T(8,128)(2,1)} %get-tuple-element.132) | copy-start | bytes 589828
  47.9 27.8 %collective-permute-start.5 = (bf16[1,192,2048]{2,1,0:T(8,128)(2,1)S(1)}, bf16[1,192,2048]{2,1,0:T(8,128)(2,1)S(1)}, u32[]{:S(2)}, u32[]{:S(2)}) collective-permute-start(bf16[1,192,2048]{2,1,0:T(8,128)(2,1)S(1)} %slice.73), channel_id=1, source_target_pairs={{0,4},{1,5},{2,6},{3,7},{4,0},{5,1},{6,2},{7,3},{8,12},{9,13},{10,... | collective-permute-start | bytes 2359304 | tf_op jit(solution)/shard_map/ppermute | solution.py:271
  49.7 26.0 %collective-permute-start.6 = (bf16[1,192,2048]{2,1,0:T(8,128)(2,1)S(1)}, bf16[1,192,2048]{2,1,0:T(8,128)(2,1)}, u32[]{:S(2)}, u32[]{:S(2)}) collective-permute-start(bf16[1,192,2048]{2,1,0:T(8,128)(2,1)S(1)} %slice.74), channel_id=1, source_target_pairs={{0,2},{1,3},{2,0},{3,1},{4,6},{5,7},{6,4},{7,5},{8,10},{9,11},{10,... | collective-permute-start | bytes 2359304 | tf_op jit(solution)/shard_map/ppermute | solution.py:271
  50.3 25.1 %collective-permute-start.7 = (bf16[1,96,1024]{2,1,0:T(8,128)(2,1)}, bf16[1,96,1024]{2,1,0:T(8,128)(2,1)S(1)}, u32[]{:S(2)}, u32[]{:S(2)}) collective-permute-start(bf16[1,96,1024]{2,1,0:T(8,128)(2,1)} %get-tuple-element.130), channel_id=1, source_target_pairs={{0,8},{8,16},{16,24},{24,0},{1,9},{9,17},{17,25},{25,1},{2,10},{10... | collective-permute-start | bytes 589832 | tf_op jit(solution)/shard_map/ppermute | solution.py:274
  62.7 13.0 %collective-permute-start.8 = (bf16[1,96,1024]{2,1,0:T(8,128)(2,1)S(1)}, bf16[1,96,1024]{2,1,0:T(8,128)(2,1)S(1)}, u32[]{:S(2)}, u32[]{:S(2)}) collective-permute-start(bf16[1,96,1024]{2,1,0:T(8,128)(2,1)S(1)} %copy-done.29), channel_id=1, source_target_pairs={{0,16},{8,24},{16,0},{24,8},{1,17},{9,25},{17,1},{25,9},{2,18},{10... | collective-permute-start | bytes 589832 | tf_op jit(solution)/shard_map/ppermute | solution.py:274
  64.3 11.4 %collective-permute-start.9 = (bf16[1,96,1024]{2,1,0:T(8,128)(2,1)S(1)}, bf16[1,96,1024]{2,1,0:T(8,128)(2,1)S(1)}, u32[]{:S(2)}, u32[]{:S(2)}) collective-permute-start(bf16[1,96,1024]{2,1,0:T(8,128)(2,1)S(1)} %copy-done.28), channel_id=1, source_target_pairs={{0,24},{8,0},{16,8},{24,16},{1,25},{9,1},{17,9},{25,17},{2,26},{10... | collective-permute-start | bytes 589832 | tf_op jit(solution)/shard_map/ppermute | solution.py:274
  66.6 9.9 %copy-start.27 = (bf16[1,96,1024]{2,1,0:T(8,128)(2,1)S(1)}, bf16[1,96,1024]{2,1,0:T(8,128)(2,1)}, u32[]{:S(2)}) copy-start(bf16[1,96,1024]{2,1,0:T(8,128)(2,1)} %get-tuple-element.143) | copy-start | bytes 589828
  66.6 15.5 %copy-start.26 = (bf16[1,96,1024]{2,1,0:T(8,128)(2,1)S(1)}, bf16[1,96,1024]{2,1,0:T(8,128)(2,1)}, u32[]{:S(2)}) copy-start(bf16[1,96,1024]{2,1,0:T(8,128)(2,1)} %get-tuple-element.144) | copy-start | bytes 589828
  66.6 17.1 %copy-start.25 = (bf16[1,96,1024]{2,1,0:T(8,128)(2,1)S(1)}, bf16[1,96,1024]{2,1,0:T(8,128)(2,1)}, u32[]{:S(2)}) copy-start(bf16[1,96,1024]{2,1,0:T(8,128)(2,1)} %get-tuple-element.145) | copy-start | bytes 589828
  75.7 8.8 %collective-permute-start.10 = (bf16[512,2176]{1,0:T(8,128)(2,1)}, bf16[512,2176]{1,0:T(8,128)(2,1)S(1)}, u32[]{:S(2)}, u32[]{:S(2)}) collective-permute-start(bf16[512,2176]{1,0:T(8,128)(2,1)} %copy-done.18), channel_id=1, source_target_pairs={{0,1},{1,0},{2,3},{3,2},{4,5},{5,4},{6,7},{7,6},{8,9},{9,8},{10,11... | collective-permute-start | bytes 6684680 | tf_op jit(solution)/shard_map/ppermute | solution.py:271
  75.9 24.1 %copy-start.19 = (bf16[4,96,1024]{2,1,0:T(8,128)(2,1)}, bf16[4,96,1024]{2,1,0:T(8,128)(2,1)S(1)}, u32[]{:S(2)}) copy-start(bf16[4,96,1024]{2,1,0:T(8,128)(2,1)S(1)} %constant_dynamic-update-slice_fusion.4.refs_2_) | copy-start | bytes 2359300
  75.9 24.2 %copy-start.16 = (bf16[1,96,1024]{2,1,0:T(8,128)(2,1)S(1)}, bf16[1,96,1024]{2,1,0:T(8,128)(2,1)}, u32[]{:S(2)}) copy-start(bf16[1,96,1024]{2,1,0:T(8,128)(2,1)} %get-tuple-element.157) | copy-start | bytes 589828
  75.9 24.1 %collective-permute-start.14 = (bf16[4,96,1024]{2,1,0:T(8,128)(2,1)S(1)}, bf16[4,96,1024]{2,1,0:T(8,128)(2,1)S(1)}, u32[]{:S(2)}, u32[]{:S(2)}) collective-permute-start(bf16[4,96,1024]{2,1,0:T(8,128)(2,1)S(1)} %constant_dynamic-update-slice_fusion.4.refs_2_), channel_id=1, source_target_pairs={{0,1},{1,0},{2,3},{3,2},{4,5},{5,4},{6,7},{7,6},{8,9},{9,8},{10,11... | collective-permute-start | bytes 2359304 | tf_op jit(solution)/shard_map/ppermute | solution.py:271
  76.4 23.5 %collective-permute-start.11 = (bf16[1,96,1024]{2,1,0:T(8,128)(2,1)S(1)}, bf16[1,96,1024]{2,1,0:T(8,128)(2,1)S(1)}, u32[]{:S(2)}, u32[]{:S(2)}) collective-permute-start(bf16[1,96,1024]{2,1,0:T(8,128)(2,1)S(1)} %copy-done.27), channel_id=1, source_target_pairs={{0,8},{8,16},{16,24},{24,0},{1,9},{9,17},{17,25},{25,1},{2,10},{10... | collective-permute-start | bytes 589832 | tf_op jit(solution)/shard_map/ppermute | solution.py:274
  82.1 17.9 %collective-permute-start.12 = (bf16[1,96,1024]{2,1,0:T(8,128)(2,1)S(1)}, bf16[1,96,1024]{2,1,0:T(8,128)(2,1)S(1)}, u32[]{:S(2)}, u32[]{:S(2)}) collective-permute-start(bf16[1,96,1024]{2,1,0:T(8,128)(2,1)S(1)} %copy-done.26), channel_id=1, source_target_pairs={{0,16},{8,24},{16,0},{24,8},{1,17},{9,25},{17,1},{25,9},{2,18},{10... | collective-permute-start | bytes 589832 | tf_op jit(solution)/shard_map/ppermute | solution.py:274
  83.7 16.3 %collective-permute-start.13 = (bf16[1,96,1024]{2,1,0:T(8,128)(2,1)S(1)}, bf16[1,96,1024]{2,1,0:T(8,128)(2,1)S(1)}, u32[]{:S(2)}, u32[]{:S(2)}) collective-permute-start(bf16[1,96,1024]{2,1,0:T(8,128)(2,1)S(1)} %copy-done.25), channel_id=1, source_target_pairs={{0,24},{8,0},{16,8},{24,16},{1,25},{9,1},{17,9},{25,17},{2,26},{10... | collective-permute-start | bytes 589832 | tf_op jit(solution)/shard_map/ppermute | solution.py:274
  100.0 10.0 %collective-permute-start.16 = (bf16[4,192,1024]{2,1,0:T(8,128)(2,1)}, bf16[4,192,1024]{2,1,0:T(8,128)(2,1)S(1)}, u32[]{:S(2)}, u32[]{:S(2)}) collective-permute-start(bf16[4,192,1024]{2,1,0:T(8,128)(2,1)} %get-tuple-element.163), channel_id=1, source_target_pairs={{0,1},{1,0},{2,3},{3,2},{4,5},{5,4},{6,7},{7,6},{8,9},{9,8},{10,11... | collective-permute-start | bytes 4718600 | tf_op jit(solution)/shard_map/ppermute | solution.py:271
  100.2 12.1 %copy-start.8 = (bf16[4,192,1024]{2,1,0:T(8,128)(2,1)S(1)}, bf16[4,192,1024]{2,1,0:T(8,128)(2,1)}, u32[]{:S(2)}) copy-start(bf16[4,192,1024]{2,1,0:T(8,128)(2,1)} %get-tuple-element.180) | copy-start | bytes 4718596
  100.2 9.8 %collective-permute-start.15 = (bf16[4,96,1024]{2,1,0:T(8,128)(2,1)S(1)}, bf16[4,96,1024]{2,1,0:T(8,128)(2,1)S(1)}, u32[]{:S(2)}, u32[]{:S(2)}) collective-permute-start(bf16[4,96,1024]{2,1,0:T(8,128)(2,1)S(1)} %constant_dynamic-update-slice_fusion.8.refs_2_), channel_id=1, source_target_pairs={{0,1},{1,0},{2,3},{3,2},{4,5},{5,4},{6,7},{7,6},{8,9},{9,8},{10,11... | collective-permute-start | bytes 2359304 | tf_op jit(solution)/shard_map/ppermute | solution.py:271
  110.0 24.9 %collective-permute-start.17 = (bf16[2,2,96,1024]{3,2,1,0:T(8,128)(2,1)}, bf16[2,2,96,1024]{3,2,1,0:T(8,128)(2,1)S(1)}, u32[]{:S(2)}, u32[]{:S(2)}) collective-permute-start(bf16[2,2,96,1024]{3,2,1,0:T(8,128)(2,1)} %get-tuple-element.168), channel_id=1, source_target_pairs={{0,2},{1,3},{2,0},{3,1},{4,6},{5,7},{6,4},{7,5},{8,10},{9,11},{10,... | collective-permute-start | bytes 2359304 | tf_op jit(solution)/shard_map/ppermute | solution.py:271
  110.8 24.1 %collective-permute-start.18 = (bf16[2,2,96,1024]{3,2,1,0:T(8,128)(2,1)}, bf16[2,2,96,1024]{3,2,1,0:T(8,128)(2,1)S(1)}, u32[]{:S(2)}, u32[]{:S(2)}) collective-permute-start(bf16[2,2,96,1024]{3,2,1,0:T(8,128)(2,1)} %get-tuple-element.170), channel_id=1, source_target_pairs={{0,4},{1,5},{2,6},{3,7},{4,0},{5,1},{6,2},{7,3},{8,12},{9,13},{10,... | collective-permute-start | bytes 2359304 | tf_op jit(solution)/shard_map/ppermute | solution.py:271
  113.2 14.0 %collective-permute-start.19 = (bf16[192,1024]{1,0:T(8,128)(2,1)S(1)}, bf16[192,1024]{1,0:T(8,128)(2,1)S(1)}, u32[]{:S(2)}, u32[]{:S(2)}) collective-permute-start(bf16[192,1024]{1,0:T(8,128)(2,1)S(1)} %get-tuple-element.213), channel_id=1, source_target_pairs={{0,24},{8,0},{16,8},{24,16},{1,25},{9,1},{17,9},{25,17},{2,26},{10... | collective-permute-start | bytes 1179656 | tf_op jit(solution)/shard_map/ppermute | solution.py:274
  117.6 18.5 %copy-start.1 = (bf16[2,2,96,1024]{3,2,1,0:T(8,128)(2,1)S(1)}, bf16[2,2,96,1024]{3,2,1,0:T(8,128)(2,1)}, u32[]{:S(2)}) copy-start(bf16[2,2,96,1024]{3,2,1,0:T(8,128)(2,1)} %get-tuple-element.204.refs_3_) | copy-start | bytes 2359300
  117.6 20.1 %copy-start = (bf16[2,2,96,1024]{3,2,1,0:T(8,128)(2,1)S(1)}, bf16[2,2,96,1024]{3,2,1,0:T(8,128)(2,1)}, u32[]{:S(2)}) copy-start(bf16[2,2,96,1024]{3,2,1,0:T(8,128)(2,1)} %get-tuple-element.201.refs_0_) | copy-start | bytes 2359300
  117.6 17.3 %collective-permute-start.20 = (bf16[192,1024]{1,0:T(8,128)(2,1)S(1)}, bf16[192,1024]{1,0:T(8,128)(2,1)S(1)}, u32[]{:S(2)}, u32[]{:S(2)}) collective-permute-start(bf16[192,1024]{1,0:T(8,128)(2,1)S(1)} %get-tuple-element.211), channel_id=1, source_target_pairs={{0,8},{8,16},{16,24},{24,0},{1,9},{9,17},{17,25},{25,1},{2,10},{10... | collective-permute-start | bytes 1179656 | tf_op jit(solution)/shard_map/ppermute | solution.py:274
  126.7 35.7 %copy-start.5 = (bf16[2,2,96,1024]{3,2,1,0:T(8,128)(2,1)S(1)}, bf16[2,2,96,1024]{3,2,1,0:T(8,128)(2,1)}, u32[]{:S(2)}) copy-start(bf16[2,2,96,1024]{3,2,1,0:T(8,128)(2,1)} %get-tuple-element.209.refs_9_) | copy-start | bytes 2359300
  126.7 37.3 %copy-start.4 = (bf16[2,2,96,1024]{3,2,1,0:T(8,128)(2,1)S(1)}, bf16[2,2,96,1024]{3,2,1,0:T(8,128)(2,1)}, u32[]{:S(2)}) copy-start(bf16[2,2,96,1024]{3,2,1,0:T(8,128)(2,1)} %get-tuple-element.207.refs_6_) | copy-start | bytes 2359300
  127.2 37.0 %copy-start.9 = (bf16[192,1024]{1,0:T(8,128)(2,1)}, bf16[192,1024]{1,0:T(8,128)(2,1)S(1)}, u32[]{:S(2)}) copy-start(bf16[192,1024]{1,0:T(8,128)(2,1)S(1)} %collective-permute-done.19.refs_1_) | copy-start | bytes 1179652
  134.9 29.3 %copy-start.10 = (bf16[192,1024]{1,0:T(8,128)(2,1)}, bf16[192,1024]{1,0:T(8,128)(2,1)S(1)}, u32[]{:S(2)}) copy-start(bf16[192,1024]{1,0:T(8,128)(2,1)S(1)} %collective-permute-done.20.refs_3_) | copy-start | bytes 1179652
  134.9 29.3 %copy-start.2 = (bf16[2,2,96,1024]{3,2,1,0:T(8,128)(2,1)}, bf16[2,2,96,1024]{3,2,1,0:T(8,128)(2,1)S(1)}, u32[]{:S(2)}) copy-start(bf16[2,2,96,1024]{3,2,1,0:T(8,128)(2,1)S(1)} %collective-permute-done.17.refs_1_) | copy-start | bytes 2359300
  134.9 29.3 %copy-start.3 = (bf16[2,2,96,1024]{3,2,1,0:T(8,128)(2,1)}, bf16[2,2,96,1024]{3,2,1,0:T(8,128)(2,1)S(1)}, u32[]{:S(2)}) copy-start(bf16[2,2,96,1024]{3,2,1,0:T(8,128)(2,1)S(1)} %collective-permute-done.18.refs_4_) | copy-start | bytes 2359300
  134.9 27.4 %collective-permute-start.21 = (bf16[2,2,96,1024]{3,2,1,0:T(8,128)(2,1)}, bf16[2,2,96,1024]{3,2,1,0:T(8,128)(2,1)S(1)}, u32[]{:S(2)}, u32[]{:S(2)}) collective-permute-start(bf16[2,2,96,1024]{3,2,1,0:T(8,128)(2,1)} %get-tuple-element.184), channel_id=1, source_target_pairs={{0,2},{1,3},{2,0},{3,1},{4,6},{5,7},{6,4},{7,5},{8,10},{9,11},{10,... | collective-permute-start | bytes 2359304 | tf_op jit(solution)/shard_map/ppermute | solution.py:271
  135.6 26.7 %collective-permute-start.22 = (bf16[2,2,96,1024]{3,2,1,0:T(8,128)(2,1)}, bf16[2,2,96,1024]{3,2,1,0:T(8,128)(2,1)S(1)}, u32[]{:S(2)}, u32[]{:S(2)}) collective-permute-start(bf16[2,2,96,1024]{3,2,1,0:T(8,128)(2,1)} %get-tuple-element.186), channel_id=1, source_target_pairs={{0,4},{1,5},{2,6},{3,7},{4,0},{5,1},{6,2},{7,3},{8,12},{9,13},{10,... | collective-permute-start | bytes 2359304 | tf_op jit(solution)/shard_map/ppermute | solution.py:271
  136.3 25.8 %collective-permute-start.25 = (bf16[1,2,96,1024]{3,2,1,0:T(8,128)(2,1)S(1)}, bf16[1,2,96,1024]{3,2,1,0:T(8,128)(2,1)S(1)}, u32[]{:S(2)}, u32[]{:S(2)}) collective-permute-start(bf16[1,2,96,1024]{3,2,1,0:T(8,128)(2,1)S(1)} %add_convert_fusion.2), channel_id=1, source_target_pairs={{0,2},{1,3},{2,0},{3,1},{4,6},{5,7},{6,4},{7,5},{8,10},{9,11},{10,... | collective-permute-start | bytes 1179656 | tf_op jit(solution)/shard_map/ppermute | solution.py:271
  137.9 24.5 %collective-permute-start.24 = (bf16[1,2,96,1024]{3,2,1,0:T(8,128)(2,1)S(1)}, bf16[1,2,96,1024]{3,2,1,0:T(8,128)(2,1)S(1)}, u32[]{:S(2)}, u32[]{:S(2)}) collective-permute-start(bf16[1,2,96,1024]{3,2,1,0:T(8,128)(2,1)S(1)} %add_convert_fusion.3), channel_id=1, source_target_pairs={{0,4},{1,5},{2,6},{3,7},{4,0},{5,1},{6,2},{7,3},{8,12},{9,13},{10,... | collective-permute-start | bytes 1179656 | tf_op jit(solution)/shard_map/ppermute | solution.py:271
  139.4 22.9 %collective-permute-start.23 = (bf16[192,1024]{1,0:T(8,128)(2,1)S(1)}, bf16[192,1024]{1,0:T(8,128)(2,1)S(1)}, u32[]{:S(2)}, u32[]{:S(2)}) collective-permute-start(bf16[192,1024]{1,0:T(8,128)(2,1)S(1)} %get-tuple-element.192), channel_id=1, source_target_pairs={{0,16},{8,24},{16,0},{24,8},{1,17},{9,25},{17,1},{25,9},{2,18},{10... | collective-permute-start | bytes 1179656 | tf_op jit(solution)/shard_map/ppermute | solution.py:274
  162.0 10.6 %copy-start.11 = (bf16[1,2,96,1024]{3,2,1,0:T(8,128)(2,1)}, bf16[1,2,96,1024]{3,2,1,0:T(8,128)(2,1)S(1)}, u32[]{:S(2)}) copy-start(bf16[1,2,96,1024]{3,2,1,0:T(8,128)(2,1)S(1)} %collective-permute-done.25.refs_5_) | copy-start | bytes 1179652
  162.3 10.4 %copy-start.12 = (bf16[1,2,96,1024]{3,2,1,0:T(8,128)(2,1)}, bf16[1,2,96,1024]{3,2,1,0:T(8,128)(2,1)S(1)}, u32[]{:S(2)}) copy-start(bf16[1,2,96,1024]{3,2,1,0:T(8,128)(2,1)S(1)} %collective-permute-done.24.refs_2_) | copy-start | bytes 1179652
  162.3 10.4 %copy-start.6 = (bf16[2,2,96,1024]{3,2,1,0:T(8,128)(2,1)}, bf16[2,2,96,1024]{3,2,1,0:T(8,128)(2,1)S(1)}, u32[]{:S(2)}) copy-start(bf16[2,2,96,1024]{3,2,1,0:T(8,128)(2,1)S(1)} %collective-permute-done.21.refs_7_) | copy-start | bytes 2359300
  162.4 10.3 %copy-start.7 = (bf16[2,2,96,1024]{3,2,1,0:T(8,128)(2,1)}, bf16[2,2,96,1024]{3,2,1,0:T(8,128)(2,1)S(1)}, u32[]{:S(2)}) copy-start(bf16[2,2,96,1024]{3,2,1,0:T(8,128)(2,1)S(1)} %collective-permute-done.22.refs_10_) | copy-start | bytes 2359300
  162.5 10.2 %collective-permute-start.27 = (bf16[1,2,96,1024]{3,2,1,0:T(8,128)(2,1)S(1)}, bf16[1,2,96,1024]{3,2,1,0:T(8,128)(2,1)S(1)}, u32[]{:S(2)}, u32[]{:S(2)}) collective-permute-start(bf16[1,2,96,1024]{3,2,1,0:T(8,128)(2,1)S(1)} %add_convert_fusion), channel_id=1, source_target_pairs={{0,2},{1,3},{2,0},{3,1},{4,6},{5,7},{6,4},{7,5},{8,10},{9,11},{10,... | collective-permute-start | bytes 1179656 | tf_op jit(solution)/shard_map/ppermute | solution.py:271
  164.2 8.6 %collective-permute-start.26 = (bf16[1,2,96,1024]{3,2,1,0:T(8,128)(2,1)S(1)}, bf16[1,2,96,1024]{3,2,1,0:T(8,128)(2,1)S(1)}, u32[]{:S(2)}, u32[]{:S(2)}) collective-permute-start(bf16[1,2,96,1024]{3,2,1,0:T(8,128)(2,1)S(1)} %add_convert_fusion.1), channel_id=1, source_target_pairs={{0,4},{1,5},{2,6},{3,7},{4,0},{5,1},{6,2},{7,3},{8,12},{9,13},{10,... | collective-permute-start | bytes 1179656 | tf_op jit(solution)/shard_map/ppermute | solution.py:271
  (10 other events, 38.6 us)

commit v4 on v3

--- a/solution.py
+++ b/solution.py
@@ -1,4 +1,5 @@
 import functools
+import math
 
 import jax
 import jax.numpy as jnp
@@ -12,14 +13,18 @@
 ANY = pl.BlockSpec(memory_space=pl.ANY)
 VMEM = pl.BlockSpec(memory_space=pltpu.VMEM)
 SMEM = pl.BlockSpec(memory_space=pltpu.SMEM)
-LIMIT = 56 * 1024 * 1024
+MIB = 1024 * 1024
 ROWS = 16
 
 
-def call(kernel, flops, moved, **kw):
+def call(kernel, flops, moved, windows, **kw):
+    need = windows
+    for buffer in kw.get("scratch_shapes", ()):
+        if jnp.issubdtype(buffer.dtype, jnp.floating):
+            need += math.prod(buffer.shape) * jnp.dtype(buffer.dtype).itemsize
     return pl.pallas_call(
         kernel,
-        compiler_params=pltpu.CompilerParams(vmem_limit_bytes=LIMIT),
+        compiler_params=pltpu.CompilerParams(vmem_limit_bytes=(26 if need < 22 * MIB else 56) * MIB),
         cost_estimate=pl.CostEstimate(flops=int(flops), bytes_accessed=int(moved), transcendentals=0),
         **kw,
     )
@@ -294,6 +299,7 @@
         functools.partial(hidden_body, nd, top, chunks),
         0,
         6 * units * routes * 4,
+        2 * (4 * block * units + 4 * units * routes),
         grid=(8,),
         in_specs=[SMEM, pl.BlockSpec((block, 2 * units), lambda i: (i, 0)), whole((top, tokens))],
         out_specs=[whole(o.shape) for o in shapes] + [whole((units, routes))],
@@ -310,6 +316,7 @@
             functools.partial(back_body, nw, groups, top),
             2 * count * size * width * n,
             2 * (count * size * width + n * width + n * top * size),
+            2 * 2 * ng * nd * size * routes,
             in_specs=[SMEM] + [ANY] * (nw + ng + len(befores)),
             out_specs=[VMEM] * ng,
             out_shape=[jax.ShapeDtypeStruct((nd, size, routes), BF16)] * ng,
@@ -359,6 +366,7 @@
             functools.partial(down_body, top, plan, columns),
             2 * held * part * width * nb * tokens,
             2 * (held * part * width + nb * tokens * width + nb * routes * part),
+            0,
             in_specs=[SMEM] + [ANY] * 4,
             out_specs=[ANY] * len(plan),
             out_shape=[jax.ShapeDtypeStruct((len(g), per, part, b - a), BF16) for g, a, b in plan],
@@ -393,58 +401,65 @@
         (cots, cots_theirs, mine, theirs, own, other, sums)
     )
 
-    def first_step(parts):
-        return [swap(parts[0], 2), swap(parts[2], 4)] if bits == 3 else []
-
-    def second_step(parts, got):
-        mids = [(parts[i][1:].astype(F32) + a[1:].astype(F32)).astype(BF16) for i, a in zip((1, 3), got)]
-        return [swap(mids[0], 4), swap(mids[1], 2)]
-
-    got = [first_step(sums[0])]
+    def middle(parts, got):
+        return [(parts[i][1:].astype(F32) + a[1:2].astype(F32)).astype(BF16) for i, a in zip((1, 3), got)]
+
+    plane = bits == 3
+    got = [[swap(sums[0][0], 2), swap(sums[0][2], 4)]] if plane else []
     backs = [own[s] + other[s] for s in range(nd)]
-    backs = [a if s in (0, nd // 2) else shift(a, nd - s) for s, a in enumerate(backs)]
+    backs[1] = shift(backs[1], nd - 1)
     for c in range(1, chunks):
         sums.append(down(eids, c))
     sums, got, backs = lax.optimization_barrier((sums, got, backs))
 
-    backs[nd // 2] = shift(backs[nd // 2], nd - nd // 2)
-    for c in range(1, chunks):
-        got.append(first_step(sums[c]))
-    ends = [second_step(sums[0], got[0])] if bits == 3 else []
-    sums, got, backs, ends = lax.optimization_barrier((sums, got, backs, ends))
+    backs = [a if s < 2 else shift(a, nd - s) for s, a in enumerate(backs)]
+    mids = []
+    for c in range(1, chunks if plane else 1):
+        mids = middle(sums[c - 1], got[c - 1])
+        got.append(
+            [
+                swap(jnp.concatenate([sums[c][0], mids[1]], 0), 2),
+                swap(jnp.concatenate([sums[c][2], mids[0]], 0), 4),
+            ]
+        )
+        sums, got, backs = lax.optimization_barrier((sums, got, backs))
 
     terms = []
-    if bits == 3:
+    if plane:
+        mids = middle(sums[-1], got[-1])
+        ends = [swap(mids[0], 4), swap(mids[1], 2)]
         for c in range(chunks):
-            if c:
-                ends.append(second_step(sums[c], got[c]))
             for i in range(2):
-                terms += [sums[c][2 * i + 1], got[c][i], ends[c][i]]
+                end = (ends[i], 0) if c == chunks - 1 else (got[c + 1][1 - i], 2)
+                terms += [(sums[c][2 * i + 1], 0), (got[c][i], 0), end]
     else:
         for parts in sums:
             acc = parts[0]
             for b in reversed(range(1, bits)):
                 n = acc.shape[0] // 2
                 acc = (acc[:n].astype(F32) + swap(acc[n:], 1 << b).astype(F32)).astype(BF16)
-            terms.append(acc)
+            terms.append((acc, 0))
     halves, parts = (2, 3) if bits == 3 else (1, 1)
     rows = part // 2 if part % (2 * ROWS) == 0 else part
-    first = pl.BlockSpec((1, per, rows, width // halves), lambda j: (0, 0, j, 0))
     grad_down = call(
         functools.partial(total_body, chunks, halves, parts),
         0,
         2 * 5 * per * size * width,
+        2 * per * rows * width * (2 * parts + 4) * chunks,
         grid=(part // rows,),
-        in_specs=[first] * len(terms),
+        in_specs=[
+            pl.BlockSpec((1, per, rows, width // halves), lambda j, at=at: (at, 0, j, 0)) for _, at in terms
+        ],
         out_specs=pl.BlockSpec((per, chunks, rows, width), lambda j: (0, 0, j, 0)),
         out_shape=jax.ShapeDtypeStruct((per, chunks, part, width), F32),
-    )(*terms).reshape(per, size, width)
+    )(*[a for a, _ in terms]).reshape(per, size, width)
 
     cols = units // 128
     out, route = call(
         functools.partial(final_body, nd, top),
         0,
         8 * units * routes * 4,
+        2 * (2 * units * routes + 3 * 2 * 128 * routes),
         grid=(cols,),
         in_specs=[SMEM]
         + [whole((size, routes))] * nd

time: 179 us -> 171 us (0.955)
  Pallas kernels: 60.5 us -> 42.1 us
  waiting for transfers between devices: 56.4 us -> 62.4 us
  starting transfers between devices: 49.1 us -> 53 us
    ppermute x12, waiting for transfers between devices: 34.2 us -> 55.5 us  [shift(): return lax.ppermute(a, 'dp', [(i, (i + s) % nd) for i in range(nd)])]
    ppermute x16 -> x14, waiting for transfers between devices: 22.3 us -> 6.84 us  [swap(): return lax.ppermute(a, 'expert', [(i, i ^ mask) for i in range(ne)])]
    pallas_call x2, Pallas kernels: 22.8 us -> 16.5 us  [back(): call(functools.partial(back_body, nw, groups, top), 2 * count * size * wi...]
    pallas_call x1, Pallas kernels: 7.83 us -> 2.24 us  [local(): call(functools.partial(hidden_body, nd, top, chunks), 0, 6 * units * rout...]
    ppermute x12, starting transfers between devices: 33.5 us -> 38.9 us  [shift(): return lax.ppermute(a, 'dp', [(i, (i + s) % nd) for i in range(nd)])]
    pallas_call x1, Pallas kernels: 7.88 us -> 4.99 us  [local(): call(functools.partial(final_body, nd, top), 0, 8 * units * routes * 4, 2...]
    slice x2, local copies, waits for them, and re-layouts: 2.4 us -> 0.1 us  [local(): corner = [swap(near[0][:per // 2], 4), swap(near[1][per // 2:], 2)]]
    pallas_call x2, Pallas kernels: 18.1 us -> 16.1 us  [down(): call(functools.partial(down_body, top, plan, columns), 2 * held * part *...]
  transfers between devices with their start and end apart: 28 -> 26, of which waited for: 8 -> 10; matrix products, arithmetic and copies ran while one was open for 2% -> 2% of each run, Pallas kernels for 32% -> 24%
where the time goes in v4:
time: 171 us; the launch traced here: 169 us
  waiting for transfers between devices  62.4 us (36%)
  starting transfers between devices  53 us (31%)
  Pallas kernels  42.1 us (25%)
  local copies, waits for them, and re-layouts  7.33 us (4%)
  other arithmetic  3.55 us (2%)
    ppermute x12, waiting for transfers between devices, shift(): return lax.ppermute(a, 'dp', [(i, (i + s) % nd) for i in range(nd)])  55.5 us
    ppermute x12, starting transfers between devices, shift(): return lax.ppermute(a, 'dp', [(i, (i + s) % nd) for i in range(nd)])  38.9 us
    pallas_call x2, Pallas kernels, back(): call(functools.partial(back_body, nw, groups, top), 2 * count * size * wi...  16.5 us
    pallas_call x2, Pallas kernels, down(): call(functools.partial(down_body, top, plan, columns), 2 * held * part *...  16.1 us
    ppermute x14, starting transfers between devices, swap(): return lax.ppermute(a, 'expert', [(i, i ^ mask) for i in range(ne)])  14.1 us
    ppermute x14, waiting for transfers between devices, swap(): return lax.ppermute(a, 'expert', [(i, i ^ mask) for i in range(ne)])  6.84 us
    unnamed x19, local copies, waits for them, and re-layouts  6 us
    pallas_call x1, Pallas kernels, local(): call(functools.partial(final_body, nd, top), 0, 8 * units * routes * 4, 2...  4.99 us
  transfers between devices with their start and end apart: 26, of which 10 were waited for; matrix products, arithmetic and copies ran while one was open for 2% of the time, Pallas kernels for 24%

profile of v4, /device:TPU:0, one launch (start us, length us, event | category | flops | bytes accessed | tf_op | source)
XLA Modules:
  0.0 169.3 jit_solution(2969433169226805305)
XLA Ops:
  0.6 0.7 convert_bitcast_fusion
  1.3 1.9 %fusion.1 = bf16[128,2176]{1,0:T(8,128)(2,1)} fusion(bf16[8,128]{1,0:T(8,128)(2,1)S(1)} %convert_bitcast_fusion, bf16[128,2048]{1,0:T(8,128)(2,1)} %param.7), kind=kLoop, calls=%fused_computation.8 | loop fusion | flops 1671168 | bytes 1083392 | tf_op jit(solution)/shard_map/concatenate | solution.py:287
  3.2 2.9 %collective-permute-start = (bf16[2,192,2048]{2,1,0:T(8,128)(2,1)}, bf16[2,192,2048]{2,1,0:T(8,128)(2,1)S(1)}, u32[]{:S(2)}, u32[]{:S(2)}) collective-permute-start(bf16[2,192,2048]{2,1,0:T(8,128)(2,1)} %refs_0_.2), channel_id=1, source_target_pairs={{0,2},{1,3},{2,0},{3,1},{4,6},{5,7},{6,4},{7,5},{8,10},{9,11},{10,... | collective-permute-start | bytes 4718600 | tf_op jit(solution)/shard_map/ppermute | solution.py:276
  6.1 1.5 collective-permute-start.1
  7.7 1.6 collective-permute-start.2
  9.2 2.6 %collective-permute-start.3 = (bf16[128,2176]{1,0:T(8,128)(2,1)}, bf16[128,2176]{1,0:T(8,128)(2,1)}, u32[]{:S(2)}, u32[]{:S(2)}) collective-permute-start(bf16[128,2176]{1,0:T(8,128)(2,1)} %fusion.1), channel_id=1, source_target_pairs={{0,16},{8,24},{16,0},{24,8},{1,17},{9,25},{17,1},{25,9},{2,18},{10... | collective-permute-start | bytes 1671176 | tf_op jit(solution)/shard_map/ppermute | solution.py:279
  11.8 1.3 collective-permute-start.4
  13.3 1.9 %copy-done = bf16[128,8,1536]{2,1,0:T(8,128)(2,1)S(1)} copy-done((bf16[128,8,1536]{2,1,0:T(8,128)(2,1)S(1)}, bf16[128,8,1536]{2,1,0:T(8,128)(2,1)}, u32[]{:S(2)}) %copy-start) | copy-done | bytes 3145752
  15.2 0.7 copy-done.2
  15.9 2.2 %shard_map.76 = (bf16[1,96,1024]{2,1,0:T(8,128)(2,1)S(1)}, bf16[1,96,1024]{2,1,0:T(8,128)(2,1)S(1)}, bf16[1,96,1024]{2,1,0:T(8,128)(2,1)S(1)}, bf16[1,96,1024]{2...) custom-call(s32[1]{0:T(128)} %bitcast.pos, ...), custom_call_target="tpu_custom_call" | custom-call | bytes 18874368 | tf_op jit(solution)/shard_map/pallas_call | solution.py:298
  18.1 7.4 %collective-permute-done.2 = bf16[128,2176]{1,0:T(8,128)(2,1)} collective-permute-done((bf16[128,2176]{1,0:T(8,128)(2,1)}, bf16[128,2176]{1,0:T(8,128)(2,1)}, u32[]{:S(2)}, u32[]{:S(2)}) %collective-permute-start.2) | collective-permute-done | bytes 557088 | tf_op jit(solution)/shard_map/ppermute | solution.py:279
  25.5 22.2 %collective-permute-done.3 = bf16[128,2176]{1,0:T(8,128)(2,1)} collective-permute-done((bf16[128,2176]{1,0:T(8,128)(2,1)}, bf16[128,2176]{1,0:T(8,128)(2,1)}, u32[]{:S(2)}, u32[]{:S(2)}) %collective-permute-start.3) | collective-permute-done | bytes 557088 | tf_op jit(solution)/shard_map/ppermute | solution.py:279
  47.7 1.1 constant_dynamic-update-slice_fusion.3
  48.8 0.6 collective-permute-start.5
  49.5 0.6 collective-permute-start.6
  50.1 12.4 %collective-permute-start.7 = (bf16[1,96,1024]{2,1,0:T(8,128)(2,1)S(1)}, bf16[1,96,1024]{2,1,0:T(8,128)(2,1)S(1)}, u32[]{:S(2)}, u32[]{:S(2)}) collective-permute-start(bf16[1,96,1024]{2,1,0:T(8,128)(2,1)S(1)} %get-tuple-element.128), channel_id=1, source_target_pairs={{0,8},{8,16},{16,24},{24,0},{1,9},{9,17},{17,25},{25,1},{2,10},{10... | collective-permute-start | bytes 589832 | tf_op jit(solution)/shard_map/ppermute | solution.py:279
  62.5 1.6 collective-permute-start.8
  64.1 0.8 collective-permute-start.9
  64.8 1.1 constant_dynamic-update-slice_fusion.2
  65.9 1.1 constant_dynamic-update-slice_fusion.1
  67.1 1.1 constant_dynamic-update-slice_fusion.refs_3_.refs_5_.refs_0_
  68.2 5.9 %shard_map.77.refs_7_ = bf16[4,192,1024]{2,1,0:T(8,128)(2,1)S(1)} custom-call(f32[6]{0:T(128)S(1)} %bitcast.30, bf16[2,192,2048]{2,1,0:T(8,128)(2,1)S(1)} %copy-done.4, bf16[2,192,2048]{2,1,0:T(8,128)(2,1)S(1)} %collective-permute-done.refs_1_, bf16[2,192,2048]{2,1,0:T(8,128)(2,1)S(1)} %collective-permute-done.1.refs_2_, ...), custom_call_target="tpu_custom_call" | custom-call | flops 2415919104 | bytes 8388608 | tf_op jit(solution)/shard_map/pallas_call | solution.py:315
  74.1 1.4 collective-permute-done.8
  76.2 5.6 %collective-permute-start.11 = (bf16[1,96,1024]{2,1,0:T(8,128)(2,1)S(1)}, bf16[1,96,1024]{2,1,0:T(8,128)(2,1)S(1)}, u32[]{:S(2)}, u32[]{:S(2)}) collective-permute-start(bf16[1,96,1024]{2,1,0:T(8,128)(2,1)S(1)} %get-tuple-element.141), channel_id=1, source_target_pairs={{0,8},{8,16},{16,24},{24,0},{1,9},{9,17},{17,25},{25,1},{2,10},{10... | collective-permute-start | bytes 589832 | tf_op jit(solution)/shard_map/ppermute | solution.py:279
  81.8 1.5 collective-permute-start.12
  83.3 0.8 collective-permute-start.13
  84.2 10.6 %shard_map.78 = (bf16[4,192,1024]{2,1,0:T(8,128)(2,1)S(1)}, bf16[4,192,1024]{2,1,0:T(8,128)(2,1)S(1)}) custom-call(f32[8]{0:T(128)S(1)} %convert_element_type.47.eids, bf16[2,192,2048]{2,1,0:T(8,128)(2,1)S(1)} %copy-done.4, bf16[2,192,2048]{2,1,0:T(8,128)(2,1)S(1)} %collective-permute-done.refs_1_, bf16[2,192,2048]{2,1,0:T(8,128)(2,1)S(1)} %collective-permute-done.1.refs_2_, ...), custom_call_target="tpu_custom_call" | custom-call | flops 6442450944 | bytes 13631488 | tf_op jit(solution)/shard_map/pallas_call | solution.py:315
  94.8 1.6 collective-permute-done.12
  96.5 0.6 collective-permute-start.15
  97.1 8.0 %shard_map.79 = (bf16[2,2,96,1024]{3,2,1,0:T(8,128)(2,1)S(1)}, bf16[2,2,96,1024]{3,2,1,0:T(8,128)(2,1)S(1)}, bf16[2,2,96,1024]{3,2,1,0:T(8,128)(2,1)S(1)}, bf16[2,2,96,1024]{3,2,1,0:T(8,128)(2,1)S(1)}) custom-call(f32[8]{0:T(128)S(1)} %convert_element_type.47.eids, bf16[512,2176]{1,0:T(8,128)(2,1)S(1)} %constant_dynamic-update-slice_fusion.refs_3_.refs_5_.refs_0_, ...), custom_call_target="tpu_custom_call" | custom-call | flops 3221225472 | bytes 8912896 | tf_op jit(solution)/shard_map/pallas_call | solution.py:365
  105.2 1.6 collective-permute-start.17
  106.7 1.5 collective-permute-start.18
  108.5 4.6 %collective-permute-start.19 = (bf16[192,1024]{1,0:T(8,128)(2,1)S(1)}, bf16[192,1024]{1,0:T(8,128)(2,1)S(1)}, u32[]{:S(2)}, u32[]{:S(2)}) collective-permute-start(bf16[192,1024]{1,0:T(8,128)(2,1)S(1)} %get-tuple-element.209), channel_id=1, source_target_pairs={{0,24},{8,0},{16,8},{24,16},{1,25},{9,1},{17,9},{25,17},{2,26},{10... | collective-permute-start | bytes 1179656 | tf_op jit(solution)/shard_map/ppermute | solution.py:279
  113.1 8.0 %shard_map.80 = (bf16[2,2,96,1024]{3,2,1,0:T(8,128)(2,1)S(1)}, bf16[2,2,96,1024]{3,2,1,0:T(8,128)(2,1)S(1)}, bf16[2,2,96,1024]{3,2,1,0:T(8,128)(2,1)S(1)}, bf16[2,2,96,1024]{3,2,1,0:T(8,128)(2,1)S(1)}) custom-call(f32[8]{0:T(128)S(1)} %convert_element_type.47.eids, bf16[512,2176]{1,0:T(8,128)(2,1)S(1)} %constant_dynamic-update-slice_fusion.refs_3_.refs_5_.refs_0_, ...), custom_call_target="tpu_custom_call" | custom-call | flops 3221225472 | bytes 8912896 | tf_op jit(solution)/shard_map/pallas_call | solution.py:365
  121.1 0.8 collective-permute-done.19.refs_1_
  122.0 2.7 %collective-permute-done.17.refs_1_ = bf16[2,2,96,1024]{3,2,1,0:T(8,128)(2,1)S(1)} collective-permute-done((bf16[2,2,96,1024]{3,2,1,0:T(8,128)(2,1)S(1)}, bf16[2,2,96,1024]{3,2,1,0:T(8,128)(2,1)S(1)}, u32[]{:S(2)}, u32[]{:S(2)}) %collective-permute-start.17) | collective-permute-done | bytes 786464 | tf_op jit(solution)/shard_map/ppermute | solution.py:276
  124.7 1.2 collective-permute-done.18.refs_4_
  126.2 1.6 collective-permute-start.21
  128.0 0.6 collective-permute-start.20
  128.6 3.7 %collective-permute-start.22 = (bf16[192,1024]{1,0:T(8,128)(2,1)S(1)}, bf16[192,1024]{1,0:T(8,128)(2,1)S(1)}, u32[]{:S(2)}, u32[]{:S(2)}) collective-permute-start(bf16[192,1024]{1,0:T(8,128)(2,1)S(1)} %get-tuple-element.190), channel_id=1, source_target_pairs={{0,16},{8,24},{16,0},{24,8},{1,17},{9,25},{17,1},{25,9},{2,18},{10... | collective-permute-start | bytes 1179656 | tf_op jit(solution)/shard_map/ppermute | solution.py:279
  132.3 2.4 %collective-permute-start.23 = (bf16[192,1024]{1,0:T(8,128)(2,1)S(1)}, bf16[192,1024]{1,0:T(8,128)(2,1)S(1)}, u32[]{:S(2)}, u32[]{:S(2)}) collective-permute-start(bf16[192,1024]{1,0:T(8,128)(2,1)S(1)} %get-tuple-element.191), channel_id=1, source_target_pairs={{0,8},{8,16},{16,24},{24,0},{1,9},{9,17},{17,25},{25,1},{2,10},{10... | collective-permute-start | bytes 1179656 | tf_op jit(solution)/shard_map/ppermute | solution.py:279
  134.7 22.1 %collective-permute-done.22.refs_2_ = bf16[192,1024]{1,0:T(8,128)(2,1)S(1)} collective-permute-done((bf16[192,1024]{1,0:T(8,128)(2,1)S(1)}, bf16[192,1024]{1,0:T(8,128)(2,1)S(1)}, u32[]{:S(2)}, u32[]{:S(2)}) %collective-permute-start.22) | collective-permute-done | bytes 393248 | tf_op jit(solution)/shard_map/ppermute | solution.py:279
  156.9 1.5 collective-permute-start.25
  158.5 0.6 collective-permute-start.24
  159.1 5.0 %shard_map.81 = (bf16[1024,1536]{1,0:T(8,128)(2,1)}, f32[8,128]{1,0:T(8,128)}) custom-call(s32[1]{0:T(128)} %bitcast.pos, bf16[192,1024]{1,0:T(8,128)(2,1)S(1)} %get-tuple-element.192.refs_0_, bf16[192,1024]{1,0:T(8,128)(2,1)S(1)} %collective-permute-done.19.refs_1_, bf16[192,1024]{1,0:T(8,128)(2,1)S(1)} %collective-permute-done.22.refs_2_, ...), custom_call_target="tpu_custom_call" | custom-call | bytes 25165824 | tf_op jit(solution)/shard_map/pallas_call | solution.py:458
  164.1 1.6 collective-permute-done.25.refs_11_
  165.7 1.3 collective-permute-done.24.refs_8_
  167.0 2.3 %shard_map.82 = f32[2,2,96,2048]{3,2,1,0:T(8,128)} custom-call(bf16[2,2,96,1024]{3,2,1,0:T(8,128)(2,1)S(1)} %get-tuple-element.199.refs_0_, bf16[2,2,96,1024]{3,2,1,0:T(8,128)(2,1)S(1)} %collective-permute-done.17.refs_1_, bf16[3,2,96,1024]{3,2,1,0:T(8,128)(2,1)S(1)} %collective-permute-done.21.refs_2_.refs_10_, ...), custom_call_target="tpu_custom_call" | custom-call | bytes 7864320 | tf_op jit(solution)/shard_map/pallas_call | solution.py:444
  (46 shorter events, 2.0 us)
Async XLA Ops:
  3.2 44.5 %collective-permute-start = (bf16[2,192,2048]{2,1,0:T(8,128)(2,1)}, bf16[2,192,2048]{2,1,0:T(8,128)(2,1)S(1)}, u32[]{:S(2)}, u32[]{:S(2)}) collective-permute-start(bf16[2,192,2048]{2,1,0:T(8,128)(2,1)} %refs_0_.2), channel_id=1, source_target_pairs={{0,2},{1,3},{2,0},{3,1},{4,6},{5,7},{6,4},{7,5},{8,10},{9,11},{10,... | collective-permute-start | bytes 4718600 | tf_op jit(solution)/shard_map/ppermute | solution.py:276
  6.1 41.5 %collective-permute-start.1 = (bf16[2,192,2048]{2,1,0:T(8,128)(2,1)}, bf16[2,192,2048]{2,1,0:T(8,128)(2,1)S(1)}, u32[]{:S(2)}, u32[]{:S(2)}) collective-permute-start(bf16[2,192,2048]{2,1,0:T(8,128)(2,1)} %refs_0_.2), channel_id=1, source_target_pairs={{0,4},{1,5},{2,6},{3,7},{4,0},{5,1},{6,2},{7,3},{8,12},{9,13},{10,... | collective-permute-start | bytes 4718600 | tf_op jit(solution)/shard_map/ppermute | solution.py:276
  7.7 17.8 %collective-permute-start.2 = (bf16[128,2176]{1,0:T(8,128)(2,1)}, bf16[128,2176]{1,0:T(8,128)(2,1)}, u32[]{:S(2)}, u32[]{:S(2)}) collective-permute-start(bf16[128,2176]{1,0:T(8,128)(2,1)} %fusion.1), channel_id=1, source_target_pairs={{0,8},{8,16},{16,24},{24,0},{1,9},{9,17},{17,25},{25,1},{2,10},{10... | collective-permute-start | bytes 1671176 | tf_op jit(solution)/shard_map/ppermute | solution.py:279
  9.2 38.4 %collective-permute-start.3 = (bf16[128,2176]{1,0:T(8,128)(2,1)}, bf16[128,2176]{1,0:T(8,128)(2,1)}, u32[]{:S(2)}, u32[]{:S(2)}) collective-permute-start(bf16[128,2176]{1,0:T(8,128)(2,1)} %fusion.1), channel_id=1, source_target_pairs={{0,16},{8,24},{16,0},{24,8},{1,17},{9,25},{17,1},{25,9},{2,18},{10... | collective-permute-start | bytes 1671176 | tf_op jit(solution)/shard_map/ppermute | solution.py:279
  11.8 35.8 %collective-permute-start.4 = (bf16[128,2176]{1,0:T(8,128)(2,1)}, bf16[128,2176]{1,0:T(8,128)(2,1)}, u32[]{:S(2)}, u32[]{:S(2)}) collective-permute-start(bf16[128,2176]{1,0:T(8,128)(2,1)} %fusion.1), channel_id=1, source_target_pairs={{0,24},{8,0},{16,8},{24,16},{1,25},{9,1},{17,9},{25,17},{2,26},{10... | collective-permute-start | bytes 1671176 | tf_op jit(solution)/shard_map/ppermute | solution.py:279
  13.3 1.9 %copy-start = (bf16[128,8,1536]{2,1,0:T(8,128)(2,1)S(1)}, bf16[128,8,1536]{2,1,0:T(8,128)(2,1)}, u32[]{:S(2)}) copy-start(bf16[128,8,1536]{2,1,0:T(8,128)(2,1)} %param.8) | copy-start | bytes 9437188
  15.2 0.7 copy-start.2
  48.8 26.7 %collective-permute-start.5 = (bf16[1,192,2048]{2,1,0:T(8,128)(2,1)S(1)}, bf16[1,192,2048]{2,1,0:T(8,128)(2,1)S(1)}, u32[]{:S(2)}, u32[]{:S(2)}) collective-permute-start(bf16[1,192,2048]{2,1,0:T(8,128)(2,1)S(1)} %slice.73), channel_id=1, source_target_pairs={{0,4},{1,5},{2,6},{3,7},{4,0},{5,1},{6,2},{7,3},{8,12},{9,13},{10,... | collective-permute-start | bytes 2359304 | tf_op jit(solution)/shard_map/ppermute | solution.py:276
  49.5 18.7 %copy-start.4 = (bf16[2,192,2048]{2,1,0:T(8,128)(2,1)S(1)}, bf16[2,192,2048]{2,1,0:T(8,128)(2,1)}, u32[]{:S(2)}) copy-start(bf16[2,192,2048]{2,1,0:T(8,128)(2,1)} %refs_0_.2) | copy-start | bytes 4718596
  49.5 26.0 %collective-permute-start.6 = (bf16[1,192,2048]{2,1,0:T(8,128)(2,1)S(1)}, bf16[1,192,2048]{2,1,0:T(8,128)(2,1)S(1)}, u32[]{:S(2)}, u32[]{:S(2)}) collective-permute-start(bf16[1,192,2048]{2,1,0:T(8,128)(2,1)S(1)} %slice.74), channel_id=1, source_target_pairs={{0,2},{1,3},{2,0},{3,1},{4,6},{5,7},{6,4},{7,5},{8,10},{9,11},{10,... | collective-permute-start | bytes 2359304 | tf_op jit(solution)/shard_map/ppermute | solution.py:276
  50.1 24.0 %collective-permute-start.7 = (bf16[1,96,1024]{2,1,0:T(8,128)(2,1)S(1)}, bf16[1,96,1024]{2,1,0:T(8,128)(2,1)S(1)}, u32[]{:S(2)}, u32[]{:S(2)}) collective-permute-start(bf16[1,96,1024]{2,1,0:T(8,128)(2,1)S(1)} %get-tuple-element.128), channel_id=1, source_target_pairs={{0,8},{8,16},{16,24},{24,0},{1,9},{9,17},{17,25},{25,1},{2,10},{10... | collective-permute-start | bytes 589832 | tf_op jit(solution)/shard_map/ppermute | solution.py:279
  62.5 13.0 %collective-permute-start.8 = (bf16[1,96,1024]{2,1,0:T(8,128)(2,1)S(1)}, bf16[1,96,1024]{2,1,0:T(8,128)(2,1)S(1)}, u32[]{:S(2)}, u32[]{:S(2)}) collective-permute-start(bf16[1,96,1024]{2,1,0:T(8,128)(2,1)S(1)} %get-tuple-element.129), channel_id=1, source_target_pairs={{0,16},{8,24},{16,0},{24,8},{1,17},{9,25},{17,1},{25,9},{2,18},{10... | collective-permute-start | bytes 589832 | tf_op jit(solution)/shard_map/ppermute | solution.py:279
  64.1 11.4 %collective-permute-start.9 = (bf16[1,96,1024]{2,1,0:T(8,128)(2,1)S(1)}, bf16[1,96,1024]{2,1,0:T(8,128)(2,1)S(1)}, u32[]{:S(2)}, u32[]{:S(2)}) collective-permute-start(bf16[1,96,1024]{2,1,0:T(8,128)(2,1)S(1)} %get-tuple-element.130), channel_id=1, source_target_pairs={{0,24},{8,0},{16,8},{24,16},{1,25},{9,1},{17,9},{25,17},{2,26},{10... | collective-permute-start | bytes 589832 | tf_op jit(solution)/shard_map/ppermute | solution.py:279
  75.5 8.7 %collective-permute-start.10 = (bf16[512,2176]{1,0:T(8,128)(2,1)S(1)}, bf16[512,2176]{1,0:T(8,128)(2,1)S(1)}, u32[]{:S(2)}, u32[]{:S(2)}) collective-permute-start(bf16[512,2176]{1,0:T(8,128)(2,1)S(1)} %constant_dynamic-update-slice_fusion.refs_3_.refs_5_.refs_0_), channel_id=1, source_target_pairs={{0,1},{1,0},{2,3},{3,2},{4,5},{5,4},{6,7},{7,6},{8,9},{9,8},{10,11... | collective-permute-start | bytes 6684680 | tf_op jit(solution)/shard_map/ppermute | solution.py:276
  75.7 20.8 %collective-permute-start.14 = (bf16[4,96,1024]{2,1,0:T(8,128)(2,1)S(1)}, bf16[4,96,1024]{2,1,0:T(8,128)(2,1)S(1)}, u32[]{:S(2)}, u32[]{:S(2)}) collective-permute-start(bf16[4,96,1024]{2,1,0:T(8,128)(2,1)S(1)} %constant_dynamic-update-slice_fusion.4.refs_2_), channel_id=1, source_target_pairs={{0,1},{1,0},{2,3},{3,2},{4,5},{5,4},{6,7},{7,6},{8,9},{9,8},{10,11... | collective-permute-start | bytes 2359304 | tf_op jit(solution)/shard_map/ppermute | solution.py:276
  76.2 18.6 %collective-permute-start.11 = (bf16[1,96,1024]{2,1,0:T(8,128)(2,1)S(1)}, bf16[1,96,1024]{2,1,0:T(8,128)(2,1)S(1)}, u32[]{:S(2)}, u32[]{:S(2)}) collective-permute-start(bf16[1,96,1024]{2,1,0:T(8,128)(2,1)S(1)} %get-tuple-element.141), channel_id=1, source_target_pairs={{0,8},{8,16},{16,24},{24,0},{1,9},{9,17},{17,25},{25,1},{2,10},{10... | collective-permute-start | bytes 589832 | tf_op jit(solution)/shard_map/ppermute | solution.py:279
  81.8 14.6 %collective-permute-start.12 = (bf16[1,96,1024]{2,1,0:T(8,128)(2,1)S(1)}, bf16[1,96,1024]{2,1,0:T(8,128)(2,1)S(1)}, u32[]{:S(2)}, u32[]{:S(2)}) collective-permute-start(bf16[1,96,1024]{2,1,0:T(8,128)(2,1)S(1)} %get-tuple-element.142), channel_id=1, source_target_pairs={{0,16},{8,24},{16,0},{24,8},{1,17},{9,25},{17,1},{25,9},{2,18},{10... | collective-permute-start | bytes 589832 | tf_op jit(solution)/shard_map/ppermute | solution.py:279
  83.3 13.1 %collective-permute-start.13 = (bf16[1,96,1024]{2,1,0:T(8,128)(2,1)S(1)}, bf16[1,96,1024]{2,1,0:T(8,128)(2,1)S(1)}, u32[]{:S(2)}, u32[]{:S(2)}) collective-permute-start(bf16[1,96,1024]{2,1,0:T(8,128)(2,1)S(1)} %get-tuple-element.143), channel_id=1, source_target_pairs={{0,24},{8,0},{16,8},{24,16},{1,25},{9,1},{17,9},{25,17},{2,26},{10... | collective-permute-start | bytes 589832 | tf_op jit(solution)/shard_map/ppermute | solution.py:279
  96.4 8.7 %collective-permute-start.16 = (bf16[4,192,1024]{2,1,0:T(8,128)(2,1)S(1)}, bf16[4,192,1024]{2,1,0:T(8,128)(2,1)S(1)}, u32[]{:S(2)}, u32[]{:S(2)}) collective-permute-start(bf16[4,192,1024]{2,1,0:T(8,128)(2,1)S(1)} %get-tuple-element.161), channel_id=1, source_target_pairs={{0,1},{1,0},{2,3},{3,2},{4,5},{5,4},{6,7},{7,6},{8,9},{9,8},{10,11... | collective-permute-start | bytes 4718600 | tf_op jit(solution)/shard_map/ppermute | solution.py:276
  96.5 8.6 %collective-permute-start.15 = (bf16[4,96,1024]{2,1,0:T(8,128)(2,1)S(1)}, bf16[4,96,1024]{2,1,0:T(8,128)(2,1)S(1)}, u32[]{:S(2)}, u32[]{:S(2)}) collective-permute-start(bf16[4,96,1024]{2,1,0:T(8,128)(2,1)S(1)} %constant_dynamic-update-slice_fusion.8.refs_2_), channel_id=1, source_target_pairs={{0,1},{1,0},{2,3},{3,2},{4,5},{5,4},{6,7},{7,6},{8,9},{9,8},{10,11... | collective-permute-start | bytes 2359304 | tf_op jit(solution)/shard_map/ppermute | solution.py:276
  105.2 19.5 %collective-permute-start.17 = (bf16[2,2,96,1024]{3,2,1,0:T(8,128)(2,1)S(1)}, bf16[2,2,96,1024]{3,2,1,0:T(8,128)(2,1)S(1)}, u32[]{:S(2)}, u32[]{:S(2)}) collective-permute-start(bf16[2,2,96,1024]{3,2,1,0:T(8,128)(2,1)S(1)} %get-tuple-element.166), channel_id=1, source_target_pairs={{0,2},{1,3},{2,0},{3,1},{4,6},{5,7},{6,4},{7,5},{8,10},{9,11},{10,... | collective-permute-start | bytes 2359304 | tf_op jit(solution)/shard_map/ppermute | solution.py:276
  106.7 19.2 %collective-permute-start.18 = (bf16[2,2,96,1024]{3,2,1,0:T(8,128)(2,1)S(1)}, bf16[2,2,96,1024]{3,2,1,0:T(8,128)(2,1)S(1)}, u32[]{:S(2)}, u32[]{:S(2)}) collective-permute-start(bf16[2,2,96,1024]{3,2,1,0:T(8,128)(2,1)S(1)} %get-tuple-element.168), channel_id=1, source_target_pairs={{0,4},{1,5},{2,6},{3,7},{4,0},{5,1},{6,2},{7,3},{8,12},{9,13},{10,... | collective-permute-start | bytes 2359304 | tf_op jit(solution)/shard_map/ppermute | solution.py:276
  108.5 13.5 %collective-permute-start.19 = (bf16[192,1024]{1,0:T(8,128)(2,1)S(1)}, bf16[192,1024]{1,0:T(8,128)(2,1)S(1)}, u32[]{:S(2)}, u32[]{:S(2)}) collective-permute-start(bf16[192,1024]{1,0:T(8,128)(2,1)S(1)} %get-tuple-element.209), channel_id=1, source_target_pairs={{0,24},{8,0},{16,8},{24,16},{1,25},{9,1},{17,9},{25,17},{2,26},{10... | collective-permute-start | bytes 1179656 | tf_op jit(solution)/shard_map/ppermute | solution.py:279
  126.2 30.6 %collective-permute-start.21 = (bf16[3,2,96,1024]{3,2,1,0:T(8,128)(2,1)S(1)}, bf16[3,2,96,1024]{3,2,1,0:T(8,128)(2,1)S(1)}, u32[]{:S(2)}, u32[]{:S(2)}) collective-permute-start(bf16[3,2,96,1024]{3,2,1,0:T(8,128)(2,1)S(1)} %pad_maximum_fusion.1), channel_id=1, source_target_pairs={{0,4},{1,5},{2,6},{3,7},{4,0},{5,1},{6,2},{7,3},{8,12},{9,13},{10,... | collective-permute-start | bytes 3538952 | tf_op jit(solution)/shard_map/ppermute | solution.py:276
  127.9 31.2 %copy-start.1 = (bf16[128,8,1536]{2,1,0:T(8,128)(2,1)S(1)}, bf16[128,8,1536]{2,1,0:T(8,128)(2,1)}, u32[]{:S(2)}) copy-start(bf16[128,8,1536]{2,1,0:T(8,128)(2,1)} %param.8) | copy-start | bytes 9437188
  128.0 31.1 %copy-start.3 = (f32[128,8]{0,1:T(8,128)S(1)}, f32[128,8]{0,1:T(8,128)}, u32[]{:S(2)}) copy-start(f32[128,8]{0,1:T(8,128)} %param.10) | copy-start | bytes 12292
  128.0 28.8 %collective-permute-start.20 = (bf16[3,2,96,1024]{3,2,1,0:T(8,128)(2,1)S(1)}, bf16[3,2,96,1024]{3,2,1,0:T(8,128)(2,1)S(1)}, u32[]{:S(2)}, u32[]{:S(2)}) collective-permute-start(bf16[3,2,96,1024]{3,2,1,0:T(8,128)(2,1)S(1)} %pad_maximum_fusion), channel_id=1, source_target_pairs={{0,2},{1,3},{2,0},{3,1},{4,6},{5,7},{6,4},{7,5},{8,10},{9,11},{10,... | collective-permute-start | bytes 3538952 | tf_op jit(solution)/shard_map/ppermute | solution.py:276
  128.6 28.1 %collective-permute-start.22 = (bf16[192,1024]{1,0:T(8,128)(2,1)S(1)}, bf16[192,1024]{1,0:T(8,128)(2,1)S(1)}, u32[]{:S(2)}, u32[]{:S(2)}) collective-permute-start(bf16[192,1024]{1,0:T(8,128)(2,1)S(1)} %get-tuple-element.190), channel_id=1, source_target_pairs={{0,16},{8,24},{16,0},{24,8},{1,17},{9,25},{17,1},{25,9},{2,18},{10... | collective-permute-start | bytes 1179656 | tf_op jit(solution)/shard_map/ppermute | solution.py:279
  132.3 24.5 %collective-permute-start.23 = (bf16[192,1024]{1,0:T(8,128)(2,1)S(1)}, bf16[192,1024]{1,0:T(8,128)(2,1)S(1)}, u32[]{:S(2)}, u32[]{:S(2)}) collective-permute-start(bf16[192,1024]{1,0:T(8,128)(2,1)S(1)} %get-tuple-element.191), channel_id=1, source_target_pairs={{0,8},{8,16},{16,24},{24,0},{1,9},{9,17},{17,25},{25,1},{2,10},{10... | collective-permute-start | bytes 1179656 | tf_op jit(solution)/shard_map/ppermute | solution.py:279
  156.9 8.8 %collective-permute-start.25 = (bf16[1,2,96,1024]{3,2,1,0:T(8,128)(2,1)S(1)}, bf16[1,2,96,1024]{3,2,1,0:T(8,128)(2,1)S(1)}, u32[]{:S(2)}, u32[]{:S(2)}) collective-permute-start(bf16[1,2,96,1024]{3,2,1,0:T(8,128)(2,1)S(1)} %add_convert_fusion), channel_id=1, source_target_pairs={{0,2},{1,3},{2,0},{3,1},{4,6},{5,7},{6,4},{7,5},{8,10},{9,11},{10,... | collective-permute-start | bytes 1179656 | tf_op jit(solution)/shard_map/ppermute | solution.py:276
  158.5 8.4 %collective-permute-start.24 = (bf16[1,2,96,1024]{3,2,1,0:T(8,128)(2,1)S(1)}, bf16[1,2,96,1024]{3,2,1,0:T(8,128)(2,1)S(1)}, u32[]{:S(2)}, u32[]{:S(2)}) collective-permute-start(bf16[1,2,96,1024]{3,2,1,0:T(8,128)(2,1)S(1)} %add_convert_fusion.1), channel_id=1, source_target_pairs={{0,4},{1,5},{2,6},{3,7},{4,0},{5,1},{6,2},{7,3},{8,12},{9,13},{10,... | collective-permute-start | bytes 1179656 | tf_op jit(solution)/shard_map/ppermute | solution.py:276

commit v5 on v4

--- a/solution.py
+++ b/solution.py
@@ -68,33 +68,53 @@
             idv[b, k] = jnp.broadcast_to(rows[k : k + 1, :], idv.shape[2:]).astype(BF16)
 
 
-def tagged(eids, tokens):
-    return [jnp.full((ROWS, tokens), eids[e], F32).astype(BF16) for e in range(eids.shape[0])]
-
-
-def back_body(nw, groups, top, eids, *refs):
-    ng = len(groups)
-    ws, cots, refs = refs[:nw], refs[nw : nw + ng], refs[nw + ng :]
-    earlier = sum(begun for _, begun in groups)
-    befores, outs = refs[:earlier], refs[earlier : earlier + ng]
-    wv, cv, nv, idv, grads, pv, sem = refs[earlier + ng :]
+def step_of(units):
+    return 2 * ROWS if units % (2 * ROWS) == 0 else ROWS
+
+
+def tagged(eids, tokens, step=ROWS):
+    return [jnp.full((step, tokens), eids[e], F32).astype(BF16) for e in range(eids.shape[0])]
+
+
+def pack_body(counts, *refs):
+    ins, outs, sem = refs[: sum(counts)], refs[sum(counts) : -1], refs[-1]
+    copies = []
+    for count, out in zip(counts, outs):
+        at = 0
+        for a in ins[len(copies) : len(copies) + count]:
+            dst = out.at[pl.ds(at, a.shape[0])]
+            copies.append(pltpu.make_async_copy(a, dst, sem.at[len(copies)]))
+            at += a.shape[0]
+    for c in copies:
+        c.start()
+    for c in copies:
+        c.wait()
+
+
+def back_body(nw, nc, ng, known, top, eids, *refs):
+    ws, cots, refs = refs[:nw], refs[nw : nw + nc], refs[nw + nc :]
+    befores, refs = refs[: known > 0], refs[known > 0 :]
+    outs, (wv, cv, nv, idv, grads, pv, sem) = refs[:ng], refs[ng:]
     units, width = wv.shape[1:]
     blocks, tokens = idv.shape[0], idv.shape[3]
     per = blocks // ng
-    ready, copies = [], []
-    for g in range(ng):
-        rows = pl.ds(g * per * tokens, per * tokens)
-        ready.append(pltpu.make_async_copy(cots[g].at[:, pl.ds(0, width)], cv.at[rows, :], sem.at[g]))
-        for b in range(per):
-            src = cots[g].at[pl.ds(b * tokens, ROWS), pl.ds(width, tokens)]
-            ready.append(pltpu.make_async_copy(src, nv.at[g * per + b], sem.at[ng + g * per + b]))
+    done = befores[0].shape[0] if known else 0
+    ready, copies, block = [], [], 0
+    for i, cot in enumerate(cots):
+        count = cot.shape[0] // tokens
+        rows = pl.ds(block * tokens, count * tokens)
+        ready.append(pltpu.make_async_copy(cot.at[:, pl.ds(0, width)], cv.at[rows, :], sem.at[i]))
+        for b in range(count):
+            src = cot.at[pl.ds(b * tokens, ROWS), pl.ds(width, tokens)]
+            ready.append(pltpu.make_async_copy(src, nv.at[block + b], sem.at[nc + block + b]))
+        block += count
     at, places = 0, []
     for i, w in enumerate(ws):
         places.append((at, w.shape[0]))
-        copies.append(pltpu.make_async_copy(w, wv.at[pl.ds(at, w.shape[0])], sem.at[ng + blocks + i]))
+        copies.append(pltpu.make_async_copy(w, wv.at[pl.ds(at, w.shape[0])], sem.at[nc + blocks + i]))
         at += w.shape[0]
-    for i in range(earlier):
-        copies.append(pltpu.make_async_copy(befores[i], pv.at[i], sem.at[ng + blocks + nw + i]))
+    for a in befores:
+        copies.append(pltpu.make_async_copy(a, pv, sem.at[nc + blocks + nw]))
     for c in ready + copies:
         c.start()
     for c in ready:
@@ -103,33 +123,30 @@
     tags = tagged(eids, tokens)
     for i, (start, count) in enumerate(places):
         copies[i].wait()
-        meets = [g for g in range(ng) if groups[g][0] <= i]
-        low, high = meets[0] * per * tokens, (meets[-1] + 1) * per * tokens
+        low = done * tokens if i < known else 0
         w = wv[start : start + count].reshape(count * units, width)
-        got = lax.dot_general(w, cv[low:high, :], (((1,), (1,)), ((), ())), preferred_element_type=F32)
-        grads[start : start + count, :, low:high] = got.astype(BF16).reshape(count, units, high - low)
+        got = lax.dot_general(w, cv[low:, :], (((1,), (1,)), ((), ())), preferred_element_type=F32)
+        grads[start : start + count, :, low:] = got.astype(BF16).reshape(count, units, blocks * tokens - low)
     for c in copies[nw:]:
         c.wait()
-    source = 0
-    for g, (first, begun) in enumerate(groups):
-        for s in range(per):
-            block = g * per + s
-            cols = slice(block * tokens, (block + 1) * tokens)
-
-            def body(j, _, g=g, s=s, block=block, cols=cols, begin=places[first][0], begun=begun, source=source):
-                f = pl.multiple_of(j * ROWS, ROWS)
-                held = {e: grads[e, pl.ds(f, ROWS), cols] for e in range(begin, at)}
-                for k in range(top):
-                    span = slice(k * tokens, (k + 1) * tokens)
-                    row = idv[block, k]
-                    acc = pv[source, s, pl.ds(f, ROWS), span] if begun else jnp.zeros((ROWS, tokens), BF16)
-                    for e in held:
-                        acc = jnp.where(row == tags[e], held[e], acc)
-                    outs[g][s, pl.ds(f, ROWS), span] = acc
-                return 0
-
-            lax.fori_loop(0, units // ROWS, body, 0)
-        source += begun
+    for block in range(blocks):
+        cols = slice(block * tokens, (block + 1) * tokens)
+        begun = block < done
+        begin = places[known][0] if begun else 0
+
+        def body(j, _, block=block, cols=cols, begun=begun, begin=begin):
+            f = pl.multiple_of(j * ROWS, ROWS)
+            held = {e: grads[e, pl.ds(f, ROWS), cols] for e in range(begin, at)}
+            for k in range(top):
+                span = slice(k * tokens, (k + 1) * tokens)
+                row = idv[block, k]
+                acc = pv[block, pl.ds(f, ROWS), span] if begun else jnp.zeros((ROWS, tokens), BF16)
+                for e in held:
+                    acc = jnp.where(row == tags[e], held[e], acc)
+                outs[block // per][block % per, pl.ds(f, ROWS), span] = acc
+            return 0
+
+        lax.fori_loop(0, units // ROWS, body, 0)
 
 
 def down_body(top, plan, columns, eids, *refs):
@@ -154,22 +171,23 @@
     for c in late:
         c.start()
     spread(nv, idv, top)
-    tags = tagged(eids, tokens)
+    step = idv.shape[2]
+    tags = tagged(eids, tokens, step)
     for b in range(nb):
         cols = slice(b * tokens, (b + 1) * tokens)
 
         def body(j, _, b=b, cols=cols):
-            f = pl.multiple_of(j * ROWS, ROWS)
-            held = [hv[b, pl.ds(f, ROWS), k * tokens : (k + 1) * tokens] for k in range(top)]
+            f = pl.multiple_of(j * step, ROWS)
+            held = [hv[b, pl.ds(f, step), k * tokens : (k + 1) * tokens] for k in range(top)]
             rows = [idv[b, k] for k in range(top)]
             for e in range(experts):
-                acc = jnp.zeros((ROWS, tokens), BF16)
+                acc = jnp.zeros((step, tokens), BF16)
                 for k in range(top):
                     acc = jnp.where(rows[k] == tags[e], held[k], acc)
-                dense[e, pl.ds(f, ROWS), cols] = acc
+                dense[e, pl.ds(f, step), cols] = acc
             return 0
 
-        lax.fori_loop(0, units // ROWS, body, 0)
+        lax.fori_loop(0, units // step, body, 0)
     for c in late:
         c.wait()
     lhs = dense[...].reshape(experts * units, nb * tokens)
@@ -309,32 +327,50 @@
     keep = made[-1]
     hs = [[made[s * chunks + c] for s in range(nd)] for c in range(chunks)]
 
-    def back(weights, groups, cots, befores):
-        nw, ng, count = len(weights), len(cots), sum(w.shape[0] for w in weights)
-        n = ng * nd * tokens
+    def back(weights, cots, ng, known, befores):
+        nw, nc, count = len(weights), len(cots), sum(w.shape[0] for w in weights)
+        n = sum(a.shape[0] for a in cots)
+        blocks = n // tokens
         return call(
-            functools.partial(back_body, nw, groups, top),
+            functools.partial(back_body, nw, nc, ng, known, top),
             2 * count * size * width * n,
             2 * (count * size * width + n * width + n * top * size),
-            2 * 2 * ng * nd * size * routes,
-            in_specs=[SMEM] + [ANY] * (nw + ng + len(befores)),
+            2 * 2 * blocks * size * routes,
+            in_specs=[SMEM] + [ANY] * (nw + nc + len(befores)),
             out_specs=[VMEM] * ng,
-            out_shape=[jax.ShapeDtypeStruct((nd, size, routes), BF16)] * ng,
+            out_shape=[jax.ShapeDtypeStruct((blocks // ng, size, routes), BF16)] * ng,
             scratch_shapes=[
                 pltpu.VMEM((count, size, width), BF16),
                 pltpu.VMEM((n, width), BF16),
-                pltpu.VMEM((ng * nd, ROWS, tokens), BF16),
-                pltpu.VMEM((ng * nd, top, ROWS, tokens), BF16),
+                pltpu.VMEM((blocks, ROWS, tokens), BF16),
+                pltpu.VMEM((blocks, top, ROWS, tokens), BF16),
                 pltpu.VMEM((count, size, n), BF16),
-                pltpu.VMEM((max(1, len(befores)), nd, size, routes), BF16),
-                pltpu.SemaphoreType.DMA((nw + ng + ng * nd + len(befores),)),
+                pltpu.VMEM((befores[0].shape[0] if befores else 1, size, routes), BF16),
+                pltpu.SemaphoreType.DMA((nc + blocks + nw + 1,)),
             ],
         )(eids[:count], *weights, *cots, *befores)
 
+    def pack(*lists):
+        flat = [a for arrays in lists for a in arrays]
+        shapes = [(sum(a.shape[0] for a in arrays),) + arrays[0].shape[1:] for arrays in lists]
+        return call(
+            functools.partial(pack_body, tuple(len(arrays) for arrays in lists)),
+            0,
+            4 * sum(a.size for a in flat),
+            0,
+            in_specs=[ANY] * len(flat),
+            out_specs=[ANY] * len(lists),
+            out_shape=[jax.ShapeDtypeStruct(shape, BF16) for shape in shapes],
+            scratch_shapes=[pltpu.SemaphoreType.DMA((len(flat),))],
+        )(*flat)
+
+    far_step = nd // 2
+    order = [0] + [s for s in range(1, nd) if s != far_step] + [far_step]
     first = after(w_down, sent)
     near = [swap(first, 2), swap(first, 4)] if bits == 3 else []
-    far = [shift(sent, s) for s in range(1, nd)]
-    near, far, hs, keep, sent = lax.optimization_barrier((near, far, hs, keep, sent))
+    far = {s: shift(sent, s) for s in range(1, nd) if s != far_step}
+    moved = {far_step: shift(hs[0][far_step], far_step)}
+    near, far, moved, hs, keep, sent = lax.optimization_barrier((near, far, moved, hs, keep, sent))
 
     if bits == 3:
         corner = [swap(near[0][: per // 2], 4), swap(near[1][per // 2 :], 2)]
@@ -344,14 +380,19 @@
         for b in range(1, bits):
             weights = jnp.concatenate([weights, swap(weights, 1 << b)], 0)
         weights = [weights]
-    cots = jnp.concatenate([sent] + far, 0)
+    far[far_step] = shift(far[far_step - 1], 1)
+    for s in range(1, nd):
+        if s != far_step:
+            moved[s] = shift(hs[0][s], s)
+    early = jnp.concatenate([sent] + [far[s] for s in order[1:-1]], 0)
+    known = 3 if bits == 3 else 0
+    begun = back(weights[:3], [early], 1, 0, []) if known else []
+    weights, far, moved, hs, early, begun = lax.optimization_barrier((weights, far, moved, hs, early, begun))
+    cots, packed = pack([early, far[far_step]], [hs[0][0]] + [moved[s] for s in order[1:]])
+    mine = [packed]
 
     def send(c):
-        return [hs[c][0]] + [shift(hs[c][s], s) for s in range(1, nd)]
-
-    mine = [send(0)]
-    begun = back(weights[:3], ((0, False),), [cots], []) if bits == 3 else []
-    weights, cots, mine, hs, begun = lax.optimization_barrier((weights, cots, mine, hs, begun))
+        return [hs[c][0]] + [shift(hs[c][s], s) for s in order[1:]]
 
     half = width // 2
     if bits == 3:
@@ -374,7 +415,7 @@
                 pltpu.VMEM((nb * tokens, width), BF16),
                 pltpu.VMEM((nb, part, routes), BF16),
                 pltpu.VMEM((nb, ROWS, tokens), BF16),
-                pltpu.VMEM((nb, top, ROWS, tokens), BF16),
+                pltpu.VMEM((nb, top, step_of(part), tokens), BF16),
                 pltpu.VMEM((held, part, nb * tokens), BF16),
                 pltpu.VMEM((width // columns, held, part, columns), BF16),
                 pltpu.SemaphoreType.DMA((4 + nb + width // columns * groups,)),
@@ -382,12 +423,10 @@
         )(eids, cots, cots_theirs, mine[c], theirs[c])
 
     cots_theirs = swap(cots, 1)
-    mine[0] = jnp.concatenate(mine[0], 0)
     theirs = [swap(mine[0], 1)]
     for c in range(1, chunks):
         mine.append(send(c))
-    groups_met = ((3 if bits == 3 else 0, bits == 3), (0, False))
-    own, other = back(weights, groups_met, [cots, cots_theirs], begun)
+    own, other = back(weights, [cots, cots_theirs], 2, known, begun)
     cots, cots_theirs, mine, theirs, own, other = lax.optimization_barrier(
         (cots, cots_theirs, mine, theirs, own, other)
     )
@@ -406,7 +445,7 @@
 
     plane = bits == 3
     got = [[swap(sums[0][0], 2), swap(sums[0][2], 4)]] if plane else []
-    backs = [own[s] + other[s] for s in range(nd)]
+    backs = [own[order.index(s)] + other[order.index(s)] for s in range(nd)]
     backs[1] = shift(backs[1], nd - 1)
     for c in range(1, chunks):
         sums.append(down(eids, c))

time: 171 us -> 165 us (0.965); the launches traced: 169 us -> 165 us
  starting transfers between devices: 53 us -> 30.2 us
  waiting for transfers between devices: 62.4 us -> 72.5 us
  Pallas kernels: 42.1 us -> 46.4 us
  local copies, waits for them, and re-layouts: 7.33 us -> 11.4 us
    ppermute x12, starting transfers between devices: 38.9 us -> 16.4 us  [shift(): return lax.ppermute(a, 'dp', [(i, (i + s) % nd) for i in range(nd)])]
    ppermute x14, waiting for transfers between devices: 6.84 us -> 12.2 us  [swap(): return lax.ppermute(a, 'expert', [(i, i ^ mask) for i in range(ne)])]
    ppermute x12, waiting for transfers between devices: 55.5 us -> 60.3 us  [shift(): return lax.ppermute(a, 'dp', [(i, (i + s) % nd) for i in range(nd)])]
    pallas_call x2 -> x3, Pallas kernels: 16.5 us -> 20.8 us  [the longest x2 19.4 us: back(): call(functools.partial(back_body, nw, nc, ng, known, top), 2 * count * si...]
    unnamed x19 -> x43, local copies, waits for them, and re-layouts: 6 us -> 10.1 us
  transfers between devices with their start and end apart: 26 -> 26, of which waited for: 10 -> 11; matrix products, arithmetic and copies ran while one was open for 2% -> 2% of each run, Pallas kernels for 24% -> 26%
where the time goes in v5:
time: 165 us
  waiting for transfers between devices  72.5 us (44%)
  Pallas kernels  46.4 us (28%)
  starting transfers between devices  30.2 us (18%)
  local copies, waits for them, and re-layouts  11.4 us (7%)
  other arithmetic  3.56 us (2%)
    ppermute x12, waiting for transfers between devices, shift(): return lax.ppermute(a, 'dp', [(i, (i + s) % nd) for i in range(nd)])  60.3 us
    pallas_call x2, Pallas kernels, back(): call(functools.partial(back_body, nw, nc, ng, known, top), 2 * count * si...  19.4 us
    ppermute x12, starting transfers between devices, shift(): return lax.ppermute(a, 'dp', [(i, (i + s) % nd) for i in range(nd)])  16.4 us
    pallas_call x2, Pallas kernels, down(): call(functools.partial(down_body, top, plan, columns), 2 * held * part *...  15.3 us
    ppermute x14, starting transfers between devices, swap(): return lax.ppermute(a, 'expert', [(i, i ^ mask) for i in range(ne)])  13.8 us
    ppermute x14, waiting for transfers between devices, swap(): return lax.ppermute(a, 'expert', [(i, i ^ mask) for i in range(ne)])  12.2 us
    unnamed x43, local copies, waits for them, and re-layouts  10.1 us
    pallas_call x1, Pallas kernels, local(): call(functools.partial(final_body, nd, top), 0, 8 * units * routes * 4, 2...  5.01 us
  transfers between devices with their start and end apart: 26, of which 11 were waited for; matrix products, arithmetic and copies ran while one was open for 2% of the time, Pallas kernels for 26%

profile of v5, /device:TPU:0, one launch (start us, length us, event | category | flops | bytes accessed | tf_op | source)
XLA Modules:
  0.0 165.1 jit_solution(4613471000705747591)
XLA Ops:
  0.6 0.7 convert_bitcast_fusion
  1.3 1.9 %fusion.1 = bf16[128,2176]{1,0:T(8,128)(2,1)} fusion(bf16[8,128]{1,0:T(8,128)(2,1)S(1)} %convert_bitcast_fusion, bf16[128,2048]{1,0:T(8,128)(2,1)} %param.7), kind=kLoop, calls=%fused_computation.8 | loop fusion | flops 1671168 | bytes 1083392 | tf_op jit(solution)/shard_map/concatenate | solution.py:305
  3.2 2.9 %collective-permute-start = (bf16[2,192,2048]{2,1,0:T(8,128)(2,1)}, bf16[2,192,2048]{2,1,0:T(8,128)(2,1)S(1)}, u32[]{:S(2)}, u32[]{:S(2)}) collective-permute-start(bf16[2,192,2048]{2,1,0:T(8,128)(2,1)} %refs_0_.2), channel_id=1, source_target_pairs={{0,2},{1,3},{2,0},{3,1},{4,6},{5,7},{6,4},{7,5},{8,10},{9,11},{10,... | collective-permute-start | bytes 4718600 | tf_op jit(solution)/shard_map/ppermute | solution.py:294
  6.1 1.5 collective-permute-start.1
  7.7 1.6 collective-permute-start.2
  9.2 2.2 %collective-permute-start.3 = (bf16[128,2176]{1,0:T(8,128)(2,1)}, bf16[128,2176]{1,0:T(8,128)(2,1)}, u32[]{:S(2)}, u32[]{:S(2)}) collective-permute-start(bf16[128,2176]{1,0:T(8,128)(2,1)} %fusion.1), channel_id=1, source_target_pairs={{0,24},{8,0},{16,8},{24,16},{1,25},{9,1},{17,9},{25,17},{2,26},{10... | collective-permute-start | bytes 1671176 | tf_op jit(solution)/shard_map/ppermute | solution.py:297
  11.5 1.9 %copy-done = bf16[128,8,1536]{2,1,0:T(8,128)(2,1)S(1)} copy-done((bf16[128,8,1536]{2,1,0:T(8,128)(2,1)S(1)}, bf16[128,8,1536]{2,1,0:T(8,128)(2,1)}, u32[]{:S(2)}) %copy-start) | copy-done | bytes 3145752
  13.4 0.7 copy-done.7
  14.1 2.9 %shard_map.76 = (bf16[1,96,1024]{2,1,0:T(8,128)(2,1)S(1)}, bf16[1,96,1024]{2,1,0:T(8,128)(2,1)S(1)}, bf16[1,96,1024]{2,1,0:T(8,128)(2,1)S(1)}, bf16[1,96,1024]{2...) custom-call(s32[1]{0:T(128)} %bitcast.pos, ...), custom_call_target="tpu_custom_call" | custom-call | bytes 18874368 | tf_op jit(solution)/shard_map/pallas_call | solution.py:316
  17.0 1.1 copy-done.3
  18.1 0.7 copy-done.5
  18.8 0.7 copy-done.9
  19.5 0.7 copy-done.11
  20.2 0.7 copy-done.13
  20.8 0.7 copy-done.15
  21.5 0.7 copy-done.17
  22.2 0.8 collective-permute-start.4
  23.1 20.8 %collective-permute-done.4.refs_5_ = bf16[1,96,1024]{2,1,0:T(8,128)(2,1)S(1)} collective-permute-done((bf16[1,96,1024]{2,1,0:T(8,128)(2,1)}, bf16[1,96,1024]{2,1,0:T(8,128)(2,1)S(1)}, u32[]{:S(2)}, u32[]{:S(2)}) %collective-permute-start.4) | collective-permute-done | bytes 196640 | tf_op jit(solution)/shard_map/ppermute | solution.py:297
  43.9 1.1 constant_dynamic-update-slice_fusion.2
  46.3 0.9 collective-permute-start.7
  47.2 1.1 constant_dynamic-update-slice_fusion.1
  48.4 1.6 collective-permute-start.8
  50.0 2.2 %collective-permute-start.9 = (bf16[1,96,1024]{2,1,0:T(8,128)(2,1)S(1)}, bf16[1,96,1024]{2,1,0:T(8,128)(2,1)S(1)}, u32[]{:S(2)}, u32[]{:S(2)}) collective-permute-start(bf16[1,96,1024]{2,1,0:T(8,128)(2,1)S(1)} %copy-done.16), channel_id=1, source_target_pairs={{0,24},{8,0},{16,8},{24,16},{1,25},{9,1},{17,9},{25,17},{2,26},{10... | collective-permute-start | bytes 589832 | tf_op jit(solution)/shard_map/ppermute | solution.py:297
  52.3 1.1 constant_dynamic-update-slice_fusion.refs_3_.refs_0_
  53.4 5.4 %shard_map.77.refs_7_ = bf16[3,192,1024]{2,1,0:T(8,128)(2,1)S(1)} custom-call(f32[6]{0:T(128)S(1)} %bitcast.30, bf16[2,192,2048]{2,1,0:T(8,128)(2,1)S(1)} %copy-done.2, bf16[2,192,2048]{2,1,0:T(8,128)(2,1)S(1)} %collective-permute-done.refs_1_, bf16[2,192,2048]{2,1,0:T(8,128)(2,1)S(1)} %collective-permute-done.1.refs_2_, ...), custom_call_target="tpu_custom_call" | custom-call | flops 1811939328 | bytes 7471104 | tf_op jit(solution)/shard_map/pallas_call | solution.py:334
  58.8 9.4 %collective-permute-done.8.refs_3_ = bf16[1,96,1024]{2,1,0:T(8,128)(2,1)S(1)} collective-permute-done((bf16[1,96,1024]{2,1,0:T(8,128)(2,1)S(1)}, bf16[1,96,1024]{2,1,0:T(8,128)(2,1)S(1)}, u32[]{:S(2)}, u32[]{:S(2)}) %collective-permute-start.8) | collective-permute-done | bytes 196640 | tf_op jit(solution)/shard_map/ppermute | solution.py:297
  68.2 2.3 %collective-permute-done.9.refs_4_ = bf16[1,96,1024]{2,1,0:T(8,128)(2,1)S(1)} collective-permute-done((bf16[1,96,1024]{2,1,0:T(8,128)(2,1)S(1)}, bf16[1,96,1024]{2,1,0:T(8,128)(2,1)S(1)}, u32[]{:S(2)}, u32[]{:S(2)}) %collective-permute-start.9) | collective-permute-done | bytes 196640 | tf_op jit(solution)/shard_map/ppermute | solution.py:297
  70.6 1.4 shard_map.78
  72.5 0.8 collective-permute-start.11
  73.4 3.0 %collective-permute-start.12 = (bf16[1,96,1024]{2,1,0:T(8,128)(2,1)S(1)}, bf16[1,96,1024]{2,1,0:T(8,128)(2,1)S(1)}, u32[]{:S(2)}, u32[]{:S(2)}) collective-permute-start(bf16[1,96,1024]{2,1,0:T(8,128)(2,1)S(1)} %copy-done.12), channel_id=1, source_target_pairs={{0,24},{8,0},{16,8},{24,16},{1,25},{9,1},{17,9},{25,17},{2,26},{10... | collective-permute-start | bytes 589832 | tf_op jit(solution)/shard_map/ppermute | solution.py:297
  76.4 14.1 %shard_map.79 = (bf16[4,192,1024]{2,1,0:T(8,128)(2,1)S(1)}, bf16[4,192,1024]{2,1,0:T(8,128)(2,1)S(1)}) custom-call(f32[8]{0:T(128)S(1)} %convert_element_type.47.eids, bf16[2,192,2048]{2,1,0:T(8,128)(2,1)S(1)} %copy-done.2, bf16[2,192,2048]{2,1,0:T(8,128)(2,1)S(1)} %collective-permute-done.refs_1_, bf16[2,192,2048]{2,1,0:T(8,128)(2,1)S(1)} %collective-permute-done.1.refs_2_, ...), custom_call_target="tpu_custom_call" | custom-call | flops 6442450944 | bytes 13631488 | tf_op jit(solution)/shard_map/pallas_call | solution.py:334
  90.5 2.2 %collective-permute-done.13 = bf16[1,96,1024]{2,1,0:T(8,128)(2,1)S(1)} collective-permute-done((bf16[1,96,1024]{2,1,0:T(8,128)(2,1)S(1)}, bf16[1,96,1024]{2,1,0:T(8,128)(2,1)S(1)}, u32[]{:S(2)}, u32[]{:S(2)}) %collective-permute-start.13) | collective-permute-done | bytes 196640 | tf_op jit(solution)/shard_map/ppermute | solution.py:297
  93.3 7.7 %shard_map.80 = (bf16[2,2,96,1024]{3,2,1,0:T(8,128)(2,1)S(1)}, bf16[2,2,96,1024]{3,2,1,0:T(8,128)(2,1)S(1)}, bf16[2,2,96,1024]{3,2,1,0:T(8,128)(2,1)S(1)}, bf16[2,2,96,1024]{3,2,1,0:T(8,128)(2,1)S(1)}) custom-call(f32[8]{0:T(128)S(1)} %convert_element_type.47.eids, bf16[512,2176]{1,0:T(8,128)(2,1)S(1)} %get-tuple-element.174.refs_5_.refs_0_, ...), custom_call_target="tpu_custom_call" | custom-call | flops 3221225472 | bytes 8912896 | tf_op jit(solution)/shard_map/pallas_call | solution.py:406
  101.0 1.6 collective-permute-start.17
  102.6 1.5 collective-permute-start.18
  104.4 1.4 collective-permute-start.19
  105.8 7.7 %shard_map.81 = (bf16[2,2,96,1024]{3,2,1,0:T(8,128)(2,1)S(1)}, bf16[2,2,96,1024]{3,2,1,0:T(8,128)(2,1)S(1)}, bf16[2,2,96,1024]{3,2,1,0:T(8,128)(2,1)S(1)}, bf16[2,2,96,1024]{3,2,1,0:T(8,128)(2,1)S(1)}) custom-call(f32[8]{0:T(128)S(1)} %convert_element_type.47.eids, bf16[512,2176]{1,0:T(8,128)(2,1)S(1)} %get-tuple-element.174.refs_5_.refs_0_, ...), custom_call_target="tpu_custom_call" | custom-call | flops 3221225472 | bytes 8912896 | tf_op jit(solution)/shard_map/pallas_call | solution.py:406
  113.5 1.6 collective-permute-done.19.refs_1_
  115.1 5.5 %collective-permute-done.17.refs_1_ = bf16[2,2,96,1024]{3,2,1,0:T(8,128)(2,1)S(1)} collective-permute-done((bf16[2,2,96,1024]{3,2,1,0:T(8,128)(2,1)S(1)}, bf16[2,2,96,1024]{3,2,1,0:T(8,128)(2,1)S(1)}, u32[]{:S(2)}, u32[]{:S(2)}) %collective-permute-start.17) | collective-permute-done | bytes 786464 | tf_op jit(solution)/shard_map/ppermute | solution.py:294
  120.6 1.2 collective-permute-done.18.refs_4_
  122.0 1.6 collective-permute-start.21
  125.1 1.2 collective-permute-start.23
  126.2 23.9 %collective-permute-done.22.refs_2_ = bf16[192,1024]{1,0:T(8,128)(2,1)S(1)} collective-permute-done((bf16[192,1024]{1,0:T(8,128)(2,1)S(1)}, bf16[192,1024]{1,0:T(8,128)(2,1)S(1)}, u32[]{:S(2)}, u32[]{:S(2)}) %collective-permute-start.22) | collective-permute-done | bytes 393248 | tf_op jit(solution)/shard_map/ppermute | solution.py:297
  150.6 1.2 collective-permute-start.25
  152.5 5.0 %shard_map.82 = (bf16[1024,1536]{1,0:T(8,128)(2,1)}, f32[8,128]{1,0:T(8,128)}) custom-call(s32[1]{0:T(128)} %bitcast.pos, bf16[192,1024]{1,0:T(8,128)(2,1)S(1)} %get-tuple-element.196.refs_0_, bf16[192,1024]{1,0:T(8,128)(2,1)S(1)} %collective-permute-done.19.refs_1_, bf16[192,1024]{1,0:T(8,128)(2,1)S(1)} %collective-permute-done.22.refs_2_, ...), custom_call_target="tpu_custom_call" | custom-call | bytes 25165824 | tf_op jit(solution)/shard_map/pallas_call | solution.py:497
  157.5 3.9 %collective-permute-done.25.refs_11_ = bf16[1,2,96,1024]{3,2,1,0:T(8,128)(2,1)S(1)} collective-permute-done((bf16[1,2,96,1024]{3,2,1,0:T(8,128)(2,1)S(1)}, bf16[1,2,96,1024]{3,2,1,0:T(8,128)(2,1)S(1)}, u32[]{:S(2)}, u32[]{:S(2)}) %collective-permute-start.25) | collective-permute-done | bytes 393248 | tf_op jit(solution)/shard_map/ppermute | solution.py:294
  161.4 1.3 collective-permute-done.24.refs_8_
  162.8 2.3 %shard_map.83 = f32[2,2,96,2048]{3,2,1,0:T(8,128)} custom-call(bf16[2,2,96,1024]{3,2,1,0:T(8,128)(2,1)S(1)} %get-tuple-element.203.refs_0_, bf16[2,2,96,1024]{3,2,1,0:T(8,128)(2,1)S(1)} %collective-permute-done.17.refs_1_, bf16[3,2,96,1024]{3,2,1,0:T(8,128)(2,1)S(1)} %collective-permute-done.21.refs_2_.refs_10_, ...), custom_call_target="tpu_custom_call" | custom-call | bytes 7864320 | tf_op jit(solution)/shard_map/pallas_call | solution.py:483
  (70 shorter events, 5.6 us)
Async XLA Ops:
  3.2 40.7 %collective-permute-start = (bf16[2,192,2048]{2,1,0:T(8,128)(2,1)}, bf16[2,192,2048]{2,1,0:T(8,128)(2,1)S(1)}, u32[]{:S(2)}, u32[]{:S(2)}) collective-permute-start(bf16[2,192,2048]{2,1,0:T(8,128)(2,1)} %refs_0_.2), channel_id=1, source_target_pairs={{0,2},{1,3},{2,0},{3,1},{4,6},{5,7},{6,4},{7,5},{8,10},{9,11},{10,... | collective-permute-start | bytes 4718600 | tf_op jit(solution)/shard_map/ppermute | solution.py:294
  6.1 37.8 %collective-permute-start.1 = (bf16[2,192,2048]{2,1,0:T(8,128)(2,1)}, bf16[2,192,2048]{2,1,0:T(8,128)(2,1)S(1)}, u32[]{:S(2)}, u32[]{:S(2)}) collective-permute-start(bf16[2,192,2048]{2,1,0:T(8,128)(2,1)} %refs_0_.2), channel_id=1, source_target_pairs={{0,4},{1,5},{2,6},{3,7},{4,0},{5,1},{6,2},{7,3},{8,12},{9,13},{10,... | collective-permute-start | bytes 4718600 | tf_op jit(solution)/shard_map/ppermute | solution.py:294
  7.7 36.2 %collective-permute-start.2 = (bf16[128,2176]{1,0:T(8,128)(2,1)}, bf16[128,2176]{1,0:T(8,128)(2,1)}, u32[]{:S(2)}, u32[]{:S(2)}) collective-permute-start(bf16[128,2176]{1,0:T(8,128)(2,1)} %fusion.1), channel_id=1, source_target_pairs={{0,8},{8,16},{16,24},{24,0},{1,9},{9,17},{17,25},{25,1},{2,10},{10... | collective-permute-start | bytes 1671176 | tf_op jit(solution)/shard_map/ppermute | solution.py:297
  9.2 34.7 %collective-permute-start.3 = (bf16[128,2176]{1,0:T(8,128)(2,1)}, bf16[128,2176]{1,0:T(8,128)(2,1)}, u32[]{:S(2)}, u32[]{:S(2)}) collective-permute-start(bf16[128,2176]{1,0:T(8,128)(2,1)} %fusion.1), channel_id=1, source_target_pairs={{0,24},{8,0},{16,8},{24,16},{1,25},{9,1},{17,9},{25,17},{2,26},{10... | collective-permute-start | bytes 1671176 | tf_op jit(solution)/shard_map/ppermute | solution.py:297
  11.5 1.9 %copy-start = (bf16[128,8,1536]{2,1,0:T(8,128)(2,1)S(1)}, bf16[128,8,1536]{2,1,0:T(8,128)(2,1)}, u32[]{:S(2)}) copy-start(bf16[128,8,1536]{2,1,0:T(8,128)(2,1)} %param.8) | copy-start | bytes 9437188
  13.4 0.7 copy-start.7
  17.0 1.1 copy-start.3
  18.1 0.7 copy-start.5
  18.8 0.7 copy-start.9
  19.5 0.7 copy-start.11
  20.1 0.7 copy-start.13
  20.8 0.7 copy-start.15
  21.5 0.7 copy-start.17
  22.2 21.7 %collective-permute-start.4 = (bf16[1,96,1024]{2,1,0:T(8,128)(2,1)}, bf16[1,96,1024]{2,1,0:T(8,128)(2,1)S(1)}, u32[]{:S(2)}, u32[]{:S(2)}) collective-permute-start(bf16[1,96,1024]{2,1,0:T(8,128)(2,1)} %get-tuple-element.114), channel_id=1, source_target_pairs={{0,16},{8,24},{16,0},{24,8},{1,17},{9,25},{17,1},{25,9},{2,18},{10... | collective-permute-start | bytes 589832 | tf_op jit(solution)/shard_map/ppermute | solution.py:297
  45.1 3.3 %copy-start.18 = (bf16[1,96,1024]{2,1,0:T(8,128)(2,1)S(1)}, bf16[1,96,1024]{2,1,0:T(8,128)(2,1)}, u32[]{:S(2)}) copy-start(bf16[1,96,1024]{2,1,0:T(8,128)(2,1)} %copy-done.17) | copy-start | bytes 589828
  45.1 4.9 %copy-start.16 = (bf16[1,96,1024]{2,1,0:T(8,128)(2,1)S(1)}, bf16[1,96,1024]{2,1,0:T(8,128)(2,1)}, u32[]{:S(2)}) copy-start(bf16[1,96,1024]{2,1,0:T(8,128)(2,1)} %copy-done.15) | copy-start | bytes 589828
  45.1 8.3 %copy-start.2 = (bf16[2,192,2048]{2,1,0:T(8,128)(2,1)S(1)}, bf16[2,192,2048]{2,1,0:T(8,128)(2,1)}, u32[]{:S(2)}) copy-start(bf16[2,192,2048]{2,1,0:T(8,128)(2,1)} %refs_0_.2) | copy-start | bytes 4718596
  45.1 25.4 %collective-permute-start.5 = (bf16[1,192,2048]{2,1,0:T(8,128)(2,1)S(1)}, bf16[1,192,2048]{2,1,0:T(8,128)(2,1)S(1)}, u32[]{:S(2)}, u32[]{:S(2)}) collective-permute-start(bf16[1,192,2048]{2,1,0:T(8,128)(2,1)S(1)} %slice.73), channel_id=1, source_target_pairs={{0,4},{1,5},{2,6},{3,7},{4,0},{5,1},{6,2},{7,3},{8,12},{9,13},{10,... | collective-permute-start | bytes 2359304 | tf_op jit(solution)/shard_map/ppermute | solution.py:294
  45.7 24.8 %collective-permute-start.6 = (bf16[1,192,2048]{2,1,0:T(8,128)(2,1)S(1)}, bf16[1,192,2048]{2,1,0:T(8,128)(2,1)S(1)}, u32[]{:S(2)}, u32[]{:S(2)}) collective-permute-start(bf16[1,192,2048]{2,1,0:T(8,128)(2,1)S(1)} %slice.74), channel_id=1, source_target_pairs={{0,2},{1,3},{2,0},{3,1},{4,6},{5,7},{6,4},{7,5},{8,10},{9,11},{10,... | collective-permute-start | bytes 2359304 | tf_op jit(solution)/shard_map/ppermute | solution.py:294
  46.3 24.2 %collective-permute-start.7 = (bf16[128,2176]{1,0:T(8,128)(2,1)}, bf16[128,2176]{1,0:T(8,128)(2,1)S(1)}, u32[]{:S(2)}, u32[]{:S(2)}) collective-permute-start(bf16[128,2176]{1,0:T(8,128)(2,1)} %collective-permute-done.2), channel_id=1, source_target_pairs={{0,8},{8,16},{16,24},{24,0},{1,9},{9,17},{17,25},{25,1},{2,10},{10... | collective-permute-start | bytes 1671176 | tf_op jit(solution)/shard_map/ppermute | solution.py:297
  48.4 19.9 %collective-permute-start.8 = (bf16[1,96,1024]{2,1,0:T(8,128)(2,1)S(1)}, bf16[1,96,1024]{2,1,0:T(8,128)(2,1)S(1)}, u32[]{:S(2)}, u32[]{:S(2)}) collective-permute-start(bf16[1,96,1024]{2,1,0:T(8,128)(2,1)S(1)} %copy-done.18), channel_id=1, source_target_pairs={{0,8},{8,16},{16,24},{24,0},{1,9},{9,17},{17,25},{25,1},{2,10},{10... | collective-permute-start | bytes 589832 | tf_op jit(solution)/shard_map/ppermute | solution.py:297
  50.0 20.5 %collective-permute-start.9 = (bf16[1,96,1024]{2,1,0:T(8,128)(2,1)S(1)}, bf16[1,96,1024]{2,1,0:T(8,128)(2,1)S(1)}, u32[]{:S(2)}, u32[]{:S(2)}) collective-permute-start(bf16[1,96,1024]{2,1,0:T(8,128)(2,1)S(1)} %copy-done.16), channel_id=1, source_target_pairs={{0,24},{8,0},{16,8},{24,16},{1,25},{9,1},{17,9},{25,17},{2,26},{10... | collective-permute-start | bytes 589832 | tf_op jit(solution)/shard_map/ppermute | solution.py:297
  58.8 13.8 %copy-start.14 = (bf16[1,96,1024]{2,1,0:T(8,128)(2,1)S(1)}, bf16[1,96,1024]{2,1,0:T(8,128)(2,1)}, u32[]{:S(2)}) copy-start(bf16[1,96,1024]{2,1,0:T(8,128)(2,1)} %copy-done.13) | copy-start | bytes 589828
  58.8 14.6 %copy-start.12 = (bf16[1,96,1024]{2,1,0:T(8,128)(2,1)S(1)}, bf16[1,96,1024]{2,1,0:T(8,128)(2,1)}, u32[]{:S(2)}) copy-start(bf16[1,96,1024]{2,1,0:T(8,128)(2,1)} %copy-done.11) | copy-start | bytes 589828
  58.8 17.6 %copy-start.10 = (bf16[1,96,1024]{2,1,0:T(8,128)(2,1)S(1)}, bf16[1,96,1024]{2,1,0:T(8,128)(2,1)}, u32[]{:S(2)}) copy-start(bf16[1,96,1024]{2,1,0:T(8,128)(2,1)} %copy-done.9) | copy-start | bytes 589828
  72.0 4.4 %collective-permute-start.10 = (bf16[512,2176]{1,0:T(8,128)(2,1)S(1)}, bf16[512,2176]{1,0:T(8,128)(2,1)S(1)}, u32[]{:S(2)}, u32[]{:S(2)}) collective-permute-start(bf16[512,2176]{1,0:T(8,128)(2,1)S(1)} %get-tuple-element.174.refs_5_.refs_0_), channel_id=1, source_target_pairs={{0,1},{1,0},{2,3},{3,2},{4,5},{5,4},{6,7},{7,6},{8,9},{9,8},{10,11... | collective-permute-start | bytes 6684680 | tf_op jit(solution)/shard_map/ppermute | solution.py:294
  72.0 20.6 %copy-start.6 = (bf16[1,96,1024]{2,1,0:T(8,128)(2,1)S(1)}, bf16[1,96,1024]{2,1,0:T(8,128)(2,1)}, u32[]{:S(2)}) copy-start(bf16[1,96,1024]{2,1,0:T(8,128)(2,1)} %copy-done.5) | copy-start | bytes 589828
  72.1 20.6 %collective-permute-start.14 = (bf16[4,96,1024]{2,1,0:T(8,128)(2,1)S(1)}, bf16[4,96,1024]{2,1,0:T(8,128)(2,1)S(1)}, u32[]{:S(2)}, u32[]{:S(2)}) collective-permute-start(bf16[4,96,1024]{2,1,0:T(8,128)(2,1)S(1)} %get-tuple-element.158.refs_2_), channel_id=1, source_target_pairs={{0,1},{1,0},{2,3},{3,2},{4,5},{5,4},{6,7},{7,6},{8,9},{9,8},{10,11... | collective-permute-start | bytes 2359304 | tf_op jit(solution)/shard_map/ppermute | solution.py:294
  72.5 17.9 %collective-permute-start.11 = (bf16[1,96,1024]{2,1,0:T(8,128)(2,1)S(1)}, bf16[1,96,1024]{2,1,0:T(8,128)(2,1)S(1)}, u32[]{:S(2)}, u32[]{:S(2)}) collective-permute-start(bf16[1,96,1024]{2,1,0:T(8,128)(2,1)S(1)} %copy-done.14), channel_id=1, source_target_pairs={{0,8},{8,16},{16,24},{24,0},{1,9},{9,17},{17,25},{25,1},{2,10},{10... | collective-permute-start | bytes 589832 | tf_op jit(solution)/shard_map/ppermute | solution.py:297
  73.4 17.1 %collective-permute-start.12 = (bf16[1,96,1024]{2,1,0:T(8,128)(2,1)S(1)}, bf16[1,96,1024]{2,1,0:T(8,128)(2,1)S(1)}, u32[]{:S(2)}, u32[]{:S(2)}) collective-permute-start(bf16[1,96,1024]{2,1,0:T(8,128)(2,1)S(1)} %copy-done.12), channel_id=1, source_target_pairs={{0,24},{8,0},{16,8},{24,16},{1,25},{9,1},{17,9},{25,17},{2,26},{10... | collective-permute-start | bytes 589832 | tf_op jit(solution)/shard_map/ppermute | solution.py:297
  76.4 16.3 %collective-permute-start.13 = (bf16[1,96,1024]{2,1,0:T(8,128)(2,1)S(1)}, bf16[1,96,1024]{2,1,0:T(8,128)(2,1)S(1)}, u32[]{:S(2)}, u32[]{:S(2)}) collective-permute-start(bf16[1,96,1024]{2,1,0:T(8,128)(2,1)S(1)} %copy-done.10), channel_id=1, source_target_pairs={{0,16},{8,24},{16,0},{24,8},{1,17},{9,25},{17,1},{25,9},{2,18},{10... | collective-permute-start | bytes 589832 | tf_op jit(solution)/shard_map/ppermute | solution.py:297
  92.7 8.4 %collective-permute-start.16 = (bf16[4,192,1024]{2,1,0:T(8,128)(2,1)S(1)}, bf16[4,192,1024]{2,1,0:T(8,128)(2,1)S(1)}, u32[]{:S(2)}, u32[]{:S(2)}) collective-permute-start(bf16[4,192,1024]{2,1,0:T(8,128)(2,1)S(1)} %get-tuple-element.165), channel_id=1, source_target_pairs={{0,1},{1,0},{2,3},{3,2},{4,5},{5,4},{6,7},{7,6},{8,9},{9,8},{10,11... | collective-permute-start | bytes 4718600 | tf_op jit(solution)/shard_map/ppermute | solution.py:294
  92.8 8.3 %collective-permute-start.15 = (bf16[4,96,1024]{2,1,0:T(8,128)(2,1)S(1)}, bf16[4,96,1024]{2,1,0:T(8,128)(2,1)S(1)}, u32[]{:S(2)}, u32[]{:S(2)}) collective-permute-start(bf16[4,96,1024]{2,1,0:T(8,128)(2,1)S(1)} %constant_dynamic-update-slice_fusion.3.refs_2_), channel_id=1, source_target_pairs={{0,1},{1,0},{2,3},{3,2},{4,5},{5,4},{6,7},{7,6},{8,9},{9,8},{10,11... | collective-permute-start | bytes 2359304 | tf_op jit(solution)/shard_map/ppermute | solution.py:294
  101.0 19.5 %collective-permute-start.17 = (bf16[2,2,96,1024]{3,2,1,0:T(8,128)(2,1)S(1)}, bf16[2,2,96,1024]{3,2,1,0:T(8,128)(2,1)S(1)}, u32[]{:S(2)}, u32[]{:S(2)}) collective-permute-start(bf16[2,2,96,1024]{3,2,1,0:T(8,128)(2,1)S(1)} %get-tuple-element.170), channel_id=1, source_target_pairs={{0,2},{1,3},{2,0},{3,1},{4,6},{5,7},{6,4},{7,5},{8,10},{9,11},{10,... | collective-permute-start | bytes 2359304 | tf_op jit(solution)/shard_map/ppermute | solution.py:294
  102.6 19.2 %collective-permute-start.18 = (bf16[2,2,96,1024]{3,2,1,0:T(8,128)(2,1)S(1)}, bf16[2,2,96,1024]{3,2,1,0:T(8,128)(2,1)S(1)}, u32[]{:S(2)}, u32[]{:S(2)}) collective-permute-start(bf16[2,2,96,1024]{3,2,1,0:T(8,128)(2,1)S(1)} %get-tuple-element.172), channel_id=1, source_target_pairs={{0,4},{1,5},{2,6},{3,7},{4,0},{5,1},{6,2},{7,3},{8,12},{9,13},{10,... | collective-permute-start | bytes 2359304 | tf_op jit(solution)/shard_map/ppermute | solution.py:294
  104.4 10.8 %collective-permute-start.19 = (bf16[192,1024]{1,0:T(8,128)(2,1)S(1)}, bf16[192,1024]{1,0:T(8,128)(2,1)S(1)}, u32[]{:S(2)}, u32[]{:S(2)}) collective-permute-start(bf16[192,1024]{1,0:T(8,128)(2,1)S(1)} %get-tuple-element.213), channel_id=1, source_target_pairs={{0,24},{8,0},{16,8},{24,16},{1,25},{9,1},{17,9},{25,17},{2,26},{10... | collective-permute-start | bytes 1179656 | tf_op jit(solution)/shard_map/ppermute | solution.py:297
  122.0 28.1 %collective-permute-start.21 = (bf16[3,2,96,1024]{3,2,1,0:T(8,128)(2,1)S(1)}, bf16[3,2,96,1024]{3,2,1,0:T(8,128)(2,1)S(1)}, u32[]{:S(2)}, u32[]{:S(2)}) collective-permute-start(bf16[3,2,96,1024]{3,2,1,0:T(8,128)(2,1)S(1)} %pad_maximum_fusion.1), channel_id=1, source_target_pairs={{0,4},{1,5},{2,6},{3,7},{4,0},{5,1},{6,2},{7,3},{8,12},{9,13},{10,... | collective-permute-start | bytes 3538952 | tf_op jit(solution)/shard_map/ppermute | solution.py:294
  123.6 28.9 %copy-start.4 = (bf16[768,1024]{1,0:T(8,128)(2,1)S(1)}, bf16[768,1024]{1,0:T(8,128)(2,1)}, u32[]{:S(2)}) copy-start(bf16[768,1024]{1,0:T(8,128)(2,1)} %copy-done.3) | copy-start | bytes 4718596
  123.8 28.7 %copy-start.1 = (bf16[128,8,1536]{2,1,0:T(8,128)(2,1)S(1)}, bf16[128,8,1536]{2,1,0:T(8,128)(2,1)}, u32[]{:S(2)}) copy-start(bf16[128,8,1536]{2,1,0:T(8,128)(2,1)} %param.8) | copy-start | bytes 9437188
  123.9 28.6 %copy-start.8 = (f32[128,8]{0,1:T(8,128)S(1)}, f32[128,8]{0,1:T(8,128)}, u32[]{:S(2)}) copy-start(f32[128,8]{0,1:T(8,128)} %param.10) | copy-start | bytes 12292
  123.9 26.5 %collective-permute-start.20 = (bf16[3,2,96,1024]{3,2,1,0:T(8,128)(2,1)S(1)}, bf16[3,2,96,1024]{3,2,1,0:T(8,128)(2,1)S(1)}, u32[]{:S(2)}, u32[]{:S(2)}) collective-permute-start(bf16[3,2,96,1024]{3,2,1,0:T(8,128)(2,1)S(1)} %pad_maximum_fusion), channel_id=1, source_target_pairs={{0,2},{1,3},{2,0},{3,1},{4,6},{5,7},{6,4},{7,5},{8,10},{9,11},{10,... | collective-permute-start | bytes 3538952 | tf_op jit(solution)/shard_map/ppermute | solution.py:294
  124.5 25.7 %collective-permute-start.22 = (bf16[192,1024]{1,0:T(8,128)(2,1)S(1)}, bf16[192,1024]{1,0:T(8,128)(2,1)S(1)}, u32[]{:S(2)}, u32[]{:S(2)}) collective-permute-start(bf16[192,1024]{1,0:T(8,128)(2,1)S(1)} %get-tuple-element.194), channel_id=1, source_target_pairs={{0,16},{8,24},{16,0},{24,8},{1,17},{9,25},{17,1},{25,9},{2,18},{10... | collective-permute-start | bytes 1179656 | tf_op jit(solution)/shard_map/ppermute | solution.py:297
  125.1 25.1 %collective-permute-start.23 = (bf16[192,1024]{1,0:T(8,128)(2,1)S(1)}, bf16[192,1024]{1,0:T(8,128)(2,1)S(1)}, u32[]{:S(2)}, u32[]{:S(2)}) collective-permute-start(bf16[192,1024]{1,0:T(8,128)(2,1)S(1)} %get-tuple-element.195), channel_id=1, source_target_pairs={{0,8},{8,16},{16,24},{24,0},{1,9},{9,17},{17,25},{25,1},{2,10},{10... | collective-permute-start | bytes 1179656 | tf_op jit(solution)/shard_map/ppermute | solution.py:297
  150.6 10.9 %collective-permute-start.25 = (bf16[1,2,96,1024]{3,2,1,0:T(8,128)(2,1)S(1)}, bf16[1,2,96,1024]{3,2,1,0:T(8,128)(2,1)S(1)}, u32[]{:S(2)}, u32[]{:S(2)}) collective-permute-start(bf16[1,2,96,1024]{3,2,1,0:T(8,128)(2,1)S(1)} %add_convert_fusion), channel_id=1, source_target_pairs={{0,2},{1,3},{2,0},{3,1},{4,6},{5,7},{6,4},{7,5},{8,10},{9,11},{10,... | collective-permute-start | bytes 1179656 | tf_op jit(solution)/shard_map/ppermute | solution.py:294
  151.9 10.8 %collective-permute-start.24 = (bf16[1,2,96,1024]{3,2,1,0:T(8,128)(2,1)S(1)}, bf16[1,2,96,1024]{3,2,1,0:T(8,128)(2,1)S(1)}, u32[]{:S(2)}, u32[]{:S(2)}) collective-permute-start(bf16[1,2,96,1024]{3,2,1,0:T(8,128)(2,1)S(1)} %add_convert_fusion.1), channel_id=1, source_target_pairs={{0,4},{1,5},{2,6},{3,7},{4,0},{5,1},{6,2},{7,3},{8,12},{9,13},{10,... | collective-permute-start | bytes 1179656 | tf_op jit(solution)/shard_map/ppermute | solution.py:294

commit v6 on v5

--- a/solution.py
+++ b/solution.py
@@ -446,12 +446,12 @@
     plane = bits == 3
     got = [[swap(sums[0][0], 2), swap(sums[0][2], 4)]] if plane else []
     backs = [own[order.index(s)] + other[order.index(s)] for s in range(nd)]
-    backs[1] = shift(backs[1], nd - 1)
+    backs = [a if s in (0, far_step) else shift(a, nd - s) for s, a in enumerate(backs)]
     for c in range(1, chunks):
         sums.append(down(eids, c))
     sums, got, backs = lax.optimization_barrier((sums, got, backs))
 
-    backs = [a if s < 2 else shift(a, nd - s) for s, a in enumerate(backs)]
+    backs[far_step] = shift(backs[far_step], nd - far_step)
     mids = []
     for c in range(1, chunks if plane else 1):
         mids = middle(sums[c - 1], got[c - 1])

time: 165 us -> 163 us (0.988)
  waiting for transfers between devices: 72.5 us -> 70.2 us
    ppermute x14, waiting for transfers between devices: 12.2 us -> 9.04 us  [swap(): return lax.ppermute(a, 'expert', [(i, i ^ mask) for i in range(ne)])]
where the time goes in v6:
time: 163 us; the launch traced here: 162 us
  waiting for transfers between devices  70.2 us (43%)
  Pallas kernels  46.4 us (28%)
  starting transfers between devices  29.7 us (18%)
  local copies, waits for them, and re-layouts  11.4 us (7%)
  other arithmetic  3.56 us (2%)
    ppermute x12, waiting for transfers between devices, shift(): return lax.ppermute(a, 'dp', [(i, (i + s) % nd) for i in range(nd)])  61.1 us
    pallas_call x2, Pallas kernels, back(): call(functools.partial(back_body, nw, nc, ng, known, top), 2 * count * si...  19.4 us
    ppermute x12, starting transfers between devices, shift(): return lax.ppermute(a, 'dp', [(i, (i + s) % nd) for i in range(nd)])  16.5 us
    pallas_call x2, Pallas kernels, down(): call(functools.partial(down_body, top, plan, columns), 2 * held * part *...  15.3 us
    ppermute x14, starting transfers between devices, swap(): return lax.ppermute(a, 'expert', [(i, i ^ mask) for i in range(ne)])  13.2 us
    unnamed x43, local copies, waits for them, and re-layouts  10.1 us
    ppermute x14, waiting for transfers between devices, swap(): return lax.ppermute(a, 'expert', [(i, i ^ mask) for i in range(ne)])  9.04 us
    pallas_call x1, Pallas kernels, local(): call(functools.partial(final_body, nd, top), 0, 8 * units * routes * 4, 2...  5.01 us
  transfers between devices with their start and end apart: 26, of which 11 were waited for; matrix products, arithmetic and copies ran while one was open for 2% of the time, Pallas kernels for 26%

profile of v6, /device:TPU:0, one launch (start us, length us, event | category | flops | bytes accessed | tf_op | source)
XLA Modules:
  0.0 162.2 jit_solution(3748539262923916907)
XLA Ops:
  0.6 0.7 convert_bitcast_fusion
  1.3 1.9 %fusion.1 = bf16[128,2176]{1,0:T(8,128)(2,1)} fusion(bf16[8,128]{1,0:T(8,128)(2,1)S(1)} %convert_bitcast_fusion, bf16[128,2048]{1,0:T(8,128)(2,1)} %param.7), kind=kLoop, calls=%fused_computation.8 | loop fusion | flops 1671168 | bytes 1083392 | tf_op jit(solution)/shard_map/concatenate | solution.py:305
  3.2 2.9 %collective-permute-start = (bf16[2,192,2048]{2,1,0:T(8,128)(2,1)}, bf16[2,192,2048]{2,1,0:T(8,128)(2,1)S(1)}, u32[]{:S(2)}, u32[]{:S(2)}) collective-permute-start(bf16[2,192,2048]{2,1,0:T(8,128)(2,1)} %refs_0_.2), channel_id=1, source_target_pairs={{0,2},{1,3},{2,0},{3,1},{4,6},{5,7},{6,4},{7,5},{8,10},{9,11},{10,... | collective-permute-start | bytes 4718600 | tf_op jit(solution)/shard_map/ppermute | solution.py:294
  6.1 1.5 collective-permute-start.1
  7.7 1.6 collective-permute-start.2
  9.2 2.2 %collective-permute-start.3 = (bf16[128,2176]{1,0:T(8,128)(2,1)}, bf16[128,2176]{1,0:T(8,128)(2,1)}, u32[]{:S(2)}, u32[]{:S(2)}) collective-permute-start(bf16[128,2176]{1,0:T(8,128)(2,1)} %fusion.1), channel_id=1, source_target_pairs={{0,24},{8,0},{16,8},{24,16},{1,25},{9,1},{17,9},{25,17},{2,26},{10... | collective-permute-start | bytes 1671176 | tf_op jit(solution)/shard_map/ppermute | solution.py:297
  11.5 1.9 %copy-done = bf16[128,8,1536]{2,1,0:T(8,128)(2,1)S(1)} copy-done((bf16[128,8,1536]{2,1,0:T(8,128)(2,1)S(1)}, bf16[128,8,1536]{2,1,0:T(8,128)(2,1)}, u32[]{:S(2)}) %copy-start) | copy-done | bytes 3145752
  13.4 0.7 copy-done.7
  14.1 2.9 %shard_map.76 = (bf16[1,96,1024]{2,1,0:T(8,128)(2,1)S(1)}, bf16[1,96,1024]{2,1,0:T(8,128)(2,1)S(1)}, bf16[1,96,1024]{2,1,0:T(8,128)(2,1)S(1)}, bf16[1,96,1024]{2...) custom-call(s32[1]{0:T(128)} %bitcast.pos, ...), custom_call_target="tpu_custom_call" | custom-call | bytes 18874368 | tf_op jit(solution)/shard_map/pallas_call | solution.py:316
  17.0 1.1 copy-done.3
  18.8 0.7 copy-done.9
  20.2 0.7 copy-done.13
  20.8 0.7 copy-done.15
  21.5 0.7 copy-done.17
  22.2 0.8 collective-permute-start.4
  23.1 20.8 %collective-permute-done.4.refs_5_ = bf16[1,96,1024]{2,1,0:T(8,128)(2,1)S(1)} collective-permute-done((bf16[1,96,1024]{2,1,0:T(8,128)(2,1)}, bf16[1,96,1024]{2,1,0:T(8,128)(2,1)S(1)}, u32[]{:S(2)}, u32[]{:S(2)}) %collective-permute-start.4) | collective-permute-done | bytes 196640 | tf_op jit(solution)/shard_map/ppermute | solution.py:297
  43.9 1.1 constant_dynamic-update-slice_fusion.2
  46.3 0.9 collective-permute-start.7
  47.2 1.1 constant_dynamic-update-slice_fusion.1
  48.4 1.6 %collective-permute-start.8 = (bf16[1,96,1024]{2,1,0:T(8,128)(2,1)S(1)}, bf16[1,96,1024]{2,1,0:T(8,128)(2,1)S(1)}, u32[]{:S(2)}, u32[]{:S(2)}) collective-permute-start(bf16[1,96,1024]{2,1,0:T(8,128)(2,1)S(1)} %copy-done.18), channel_id=1, source_target_pairs={{0,8},{8,16},{16,24},{24,0},{1,9},{9,17},{17,25},{25,1},{2,10},{10... | collective-permute-start | bytes 589832 | tf_op jit(solution)/shard_map/ppermute | solution.py:297
  50.0 2.2 %collective-permute-start.9 = (bf16[1,96,1024]{2,1,0:T(8,128)(2,1)S(1)}, bf16[1,96,1024]{2,1,0:T(8,128)(2,1)S(1)}, u32[]{:S(2)}, u32[]{:S(2)}) collective-permute-start(bf16[1,96,1024]{2,1,0:T(8,128)(2,1)S(1)} %copy-done.16), channel_id=1, source_target_pairs={{0,24},{8,0},{16,8},{24,16},{1,25},{9,1},{17,9},{25,17},{2,26},{10... | collective-permute-start | bytes 589832 | tf_op jit(solution)/shard_map/ppermute | solution.py:297
  52.3 1.1 constant_dynamic-update-slice_fusion.refs_3_.refs_0_
  53.4 5.4 %shard_map.77.refs_7_ = bf16[3,192,1024]{2,1,0:T(8,128)(2,1)S(1)} custom-call(f32[6]{0:T(128)S(1)} %bitcast.30, bf16[2,192,2048]{2,1,0:T(8,128)(2,1)S(1)} %copy-done.2, bf16[2,192,2048]{2,1,0:T(8,128)(2,1)S(1)} %collective-permute-done.refs_1_, bf16[2,192,2048]{2,1,0:T(8,128)(2,1)S(1)} %collective-permute-done.1.refs_2_, ...), custom_call_target="tpu_custom_call" | custom-call | flops 1811939328 | bytes 7471104 | tf_op jit(solution)/shard_map/pallas_call | solution.py:334
  58.8 9.4 %collective-permute-done.8.refs_3_ = bf16[1,96,1024]{2,1,0:T(8,128)(2,1)S(1)} collective-permute-done((bf16[1,96,1024]{2,1,0:T(8,128)(2,1)S(1)}, bf16[1,96,1024]{2,1,0:T(8,128)(2,1)S(1)}, u32[]{:S(2)}, u32[]{:S(2)}) %collective-permute-start.8) | collective-permute-done | bytes 196640 | tf_op jit(solution)/shard_map/ppermute | solution.py:297
  68.2 2.3 %collective-permute-done.9.refs_4_ = bf16[1,96,1024]{2,1,0:T(8,128)(2,1)S(1)} collective-permute-done((bf16[1,96,1024]{2,1,0:T(8,128)(2,1)S(1)}, bf16[1,96,1024]{2,1,0:T(8,128)(2,1)S(1)}, u32[]{:S(2)}, u32[]{:S(2)}) %collective-permute-start.9) | collective-permute-done | bytes 196640 | tf_op jit(solution)/shard_map/ppermute | solution.py:297
  70.6 1.4 shard_map.78
  72.5 0.8 collective-permute-start.11
  73.4 3.0 %collective-permute-start.12 = (bf16[1,96,1024]{2,1,0:T(8,128)(2,1)S(1)}, bf16[1,96,1024]{2,1,0:T(8,128)(2,1)S(1)}, u32[]{:S(2)}, u32[]{:S(2)}) collective-permute-start(bf16[1,96,1024]{2,1,0:T(8,128)(2,1)S(1)} %copy-done.12), channel_id=1, source_target_pairs={{0,24},{8,0},{16,8},{24,16},{1,25},{9,1},{17,9},{25,17},{2,26},{10... | collective-permute-start | bytes 589832 | tf_op jit(solution)/shard_map/ppermute | solution.py:297
  76.4 14.1 %shard_map.79 = (bf16[4,192,1024]{2,1,0:T(8,128)(2,1)S(1)}, bf16[4,192,1024]{2,1,0:T(8,128)(2,1)S(1)}) custom-call(f32[8]{0:T(128)S(1)} %convert_element_type.47.eids, bf16[2,192,2048]{2,1,0:T(8,128)(2,1)S(1)} %copy-done.2, bf16[2,192,2048]{2,1,0:T(8,128)(2,1)S(1)} %collective-permute-done.refs_1_, bf16[2,192,2048]{2,1,0:T(8,128)(2,1)S(1)} %collective-permute-done.1.refs_2_, ...), custom_call_target="tpu_custom_call" | custom-call | flops 6442450944 | bytes 13631488 | tf_op jit(solution)/shard_map/pallas_call | solution.py:334
  90.5 2.2 %collective-permute-done.13 = bf16[1,96,1024]{2,1,0:T(8,128)(2,1)S(1)} collective-permute-done((bf16[1,96,1024]{2,1,0:T(8,128)(2,1)S(1)}, bf16[1,96,1024]{2,1,0:T(8,128)(2,1)S(1)}, u32[]{:S(2)}, u32[]{:S(2)}) %collective-permute-start.13) | collective-permute-done | bytes 196640 | tf_op jit(solution)/shard_map/ppermute | solution.py:297
  93.3 7.7 %shard_map.80 = (bf16[2,2,96,1024]{3,2,1,0:T(8,128)(2,1)S(1)}, bf16[2,2,96,1024]{3,2,1,0:T(8,128)(2,1)S(1)}, bf16[2,2,96,1024]{3,2,1,0:T(8,128)(2,1)S(1)}, bf16[2,2,96,1024]{3,2,1,0:T(8,128)(2,1)S(1)}) custom-call(f32[8]{0:T(128)S(1)} %convert_element_type.47.eids, bf16[512,2176]{1,0:T(8,128)(2,1)S(1)} %get-tuple-element.174.refs_5_.refs_0_, ...), custom_call_target="tpu_custom_call" | custom-call | flops 3221225472 | bytes 8912896 | tf_op jit(solution)/shard_map/pallas_call | solution.py:406
  101.0 1.6 collective-permute-start.17
  102.6 1.5 collective-permute-start.18
  104.4 1.2 collective-permute-start.19
  105.6 0.8 collective-permute-start.20
  106.4 7.7 %shard_map.81 = (bf16[2,2,96,1024]{3,2,1,0:T(8,128)(2,1)S(1)}, bf16[2,2,96,1024]{3,2,1,0:T(8,128)(2,1)S(1)}, bf16[2,2,96,1024]{3,2,1,0:T(8,128)(2,1)S(1)}, bf16[2,2,96,1024]{3,2,1,0:T(8,128)(2,1)S(1)}) custom-call(f32[8]{0:T(128)S(1)} %convert_element_type.47.eids, bf16[512,2176]{1,0:T(8,128)(2,1)S(1)} %get-tuple-element.174.refs_5_.refs_0_, ...), custom_call_target="tpu_custom_call" | custom-call | flops 3221225472 | bytes 8912896 | tf_op jit(solution)/shard_map/pallas_call | solution.py:406
  114.1 2.5 %collective-permute-done.19.refs_1_ = bf16[192,1024]{1,0:T(8,128)(2,1)S(1)} collective-permute-done((bf16[192,1024]{1,0:T(8,128)(2,1)S(1)}, bf16[192,1024]{1,0:T(8,128)(2,1)S(1)}, u32[]{:S(2)}, u32[]{:S(2)}) %collective-permute-start.19) | collective-permute-done | bytes 393248 | tf_op jit(solution)/shard_map/ppermute | solution.py:297
  116.6 6.7 %collective-permute-done.20.refs_3_ = bf16[192,1024]{1,0:T(8,128)(2,1)S(1)} collective-permute-done((bf16[192,1024]{1,0:T(8,128)(2,1)S(1)}, bf16[192,1024]{1,0:T(8,128)(2,1)S(1)}, u32[]{:S(2)}, u32[]{:S(2)}) %collective-permute-start.20) | collective-permute-done | bytes 393248 | tf_op jit(solution)/shard_map/ppermute | solution.py:297
  123.6 0.8 collective-permute-start.22
  124.6 0.7 collective-permute-start.21
  125.3 1.2 collective-permute-start.23
  126.5 17.1 %collective-permute-done.23.refs_2_ = bf16[192,1024]{1,0:T(8,128)(2,1)S(1)} collective-permute-done((bf16[192,1024]{1,0:T(8,128)(2,1)S(1)}, bf16[192,1024]{1,0:T(8,128)(2,1)S(1)}, u32[]{:S(2)}, u32[]{:S(2)}) %collective-permute-start.23) | collective-permute-done | bytes 393248 | tf_op jit(solution)/shard_map/ppermute | solution.py:297
  143.6 6.4 %collective-permute-done.22.refs_2_.refs_10_ = bf16[3,2,96,1024]{3,2,1,0:T(8,128)(2,1)S(1)} collective-permute-done((bf16[3,2,96,1024]{3,2,1,0:T(8,128)(2,1)S(1)}, bf16[3,2,96,1024]{3,2,1,0:T(8,128)(2,1)S(1)}, u32[]{:S(2)}, u32[]{:S(2)}) %collective-permute-start.22) | collective-permute-done | bytes 1179680 | tf_op jit(solution)/shard_map/ppermute | solution.py:294
  150.0 0.8 collective-permute-done.21.refs_5_.refs_7_
  151.8 1.3 collective-permute-start.24
  153.1 5.0 %shard_map.82 = (bf16[1024,1536]{1,0:T(8,128)(2,1)}, f32[8,128]{1,0:T(8,128)}) custom-call(s32[1]{0:T(128)} %bitcast.pos, bf16[192,1024]{1,0:T(8,128)(2,1)S(1)} %get-tuple-element.196.refs_0_, bf16[192,1024]{1,0:T(8,128)(2,1)S(1)} %collective-permute-done.19.refs_1_, bf16[192,1024]{1,0:T(8,128)(2,1)S(1)} %collective-permute-done.23.refs_2_, ...), custom_call_target="tpu_custom_call" | custom-call | bytes 25165824 | tf_op jit(solution)/shard_map/pallas_call | solution.py:497
  158.1 1.3 collective-permute-done.25.refs_11_
  159.9 2.3 %shard_map.83 = f32[2,2,96,2048]{3,2,1,0:T(8,128)} custom-call(bf16[2,2,96,1024]{3,2,1,0:T(8,128)(2,1)S(1)} %get-tuple-element.203.refs_0_, bf16[2,2,96,1024]{3,2,1,0:T(8,128)(2,1)S(1)} %collective-permute-done.17.refs_1_, bf16[3,2,96,1024]{3,2,1,0:T(8,128)(2,1)S(1)} %collective-permute-done.22.refs_2_.refs_10_, ...), custom_call_target="tpu_custom_call" | custom-call | bytes 7864320 | tf_op jit(solution)/shard_map/pallas_call | solution.py:483
  (70 shorter events, 6.2 us)
Async XLA Ops:
  3.2 40.7 %collective-permute-start = (bf16[2,192,2048]{2,1,0:T(8,128)(2,1)}, bf16[2,192,2048]{2,1,0:T(8,128)(2,1)S(1)}, u32[]{:S(2)}, u32[]{:S(2)}) collective-permute-start(bf16[2,192,2048]{2,1,0:T(8,128)(2,1)} %refs_0_.2), channel_id=1, source_target_pairs={{0,2},{1,3},{2,0},{3,1},{4,6},{5,7},{6,4},{7,5},{8,10},{9,11},{10,... | collective-permute-start | bytes 4718600 | tf_op jit(solution)/shard_map/ppermute | solution.py:294
  6.1 37.8 %collective-permute-start.1 = (bf16[2,192,2048]{2,1,0:T(8,128)(2,1)}, bf16[2,192,2048]{2,1,0:T(8,128)(2,1)S(1)}, u32[]{:S(2)}, u32[]{:S(2)}) collective-permute-start(bf16[2,192,2048]{2,1,0:T(8,128)(2,1)} %refs_0_.2), channel_id=1, source_target_pairs={{0,4},{1,5},{2,6},{3,7},{4,0},{5,1},{6,2},{7,3},{8,12},{9,13},{10,... | collective-permute-start | bytes 4718600 | tf_op jit(solution)/shard_map/ppermute | solution.py:294
  7.7 36.2 %collective-permute-start.2 = (bf16[128,2176]{1,0:T(8,128)(2,1)}, bf16[128,2176]{1,0:T(8,128)(2,1)}, u32[]{:S(2)}, u32[]{:S(2)}) collective-permute-start(bf16[128,2176]{1,0:T(8,128)(2,1)} %fusion.1), channel_id=1, source_target_pairs={{0,8},{8,16},{16,24},{24,0},{1,9},{9,17},{17,25},{25,1},{2,10},{10... | collective-permute-start | bytes 1671176 | tf_op jit(solution)/shard_map/ppermute | solution.py:297
  9.2 34.7 %collective-permute-start.3 = (bf16[128,2176]{1,0:T(8,128)(2,1)}, bf16[128,2176]{1,0:T(8,128)(2,1)}, u32[]{:S(2)}, u32[]{:S(2)}) collective-permute-start(bf16[128,2176]{1,0:T(8,128)(2,1)} %fusion.1), channel_id=1, source_target_pairs={{0,24},{8,0},{16,8},{24,16},{1,25},{9,1},{17,9},{25,17},{2,26},{10... | collective-permute-start | bytes 1671176 | tf_op jit(solution)/shard_map/ppermute | solution.py:297
  11.5 1.9 %copy-start = (bf16[128,8,1536]{2,1,0:T(8,128)(2,1)S(1)}, bf16[128,8,1536]{2,1,0:T(8,128)(2,1)}, u32[]{:S(2)}) copy-start(bf16[128,8,1536]{2,1,0:T(8,128)(2,1)} %param.8) | copy-start | bytes 9437188
  13.4 0.7 copy-start.7
  17.0 1.1 copy-start.3
  18.1 0.7 copy-start.5
  18.8 0.7 copy-start.9
  19.5 0.7 copy-start.11
  20.1 0.7 copy-start.13
  20.8 0.7 copy-start.15
  21.5 0.7 copy-start.17
  22.2 21.7 %collective-permute-start.4 = (bf16[1,96,1024]{2,1,0:T(8,128)(2,1)}, bf16[1,96,1024]{2,1,0:T(8,128)(2,1)S(1)}, u32[]{:S(2)}, u32[]{:S(2)}) collective-permute-start(bf16[1,96,1024]{2,1,0:T(8,128)(2,1)} %get-tuple-element.114), channel_id=1, source_target_pairs={{0,16},{8,24},{16,0},{24,8},{1,17},{9,25},{17,1},{25,9},{2,18},{10... | collective-permute-start | bytes 589832 | tf_op jit(solution)/shard_map/ppermute | solution.py:297
  45.1 3.3 %copy-start.18 = (bf16[1,96,1024]{2,1,0:T(8,128)(2,1)S(1)}, bf16[1,96,1024]{2,1,0:T(8,128)(2,1)}, u32[]{:S(2)}) copy-start(bf16[1,96,1024]{2,1,0:T(8,128)(2,1)} %copy-done.17) | copy-start | bytes 589828
  45.1 4.9 %copy-start.16 = (bf16[1,96,1024]{2,1,0:T(8,128)(2,1)S(1)}, bf16[1,96,1024]{2,1,0:T(8,128)(2,1)}, u32[]{:S(2)}) copy-start(bf16[1,96,1024]{2,1,0:T(8,128)(2,1)} %copy-done.15) | copy-start | bytes 589828
  45.1 8.3 %copy-start.2 = (bf16[2,192,2048]{2,1,0:T(8,128)(2,1)S(1)}, bf16[2,192,2048]{2,1,0:T(8,128)(2,1)}, u32[]{:S(2)}) copy-start(bf16[2,192,2048]{2,1,0:T(8,128)(2,1)} %refs_0_.2) | copy-start | bytes 4718596
  45.1 25.4 %collective-permute-start.5 = (bf16[1,192,2048]{2,1,0:T(8,128)(2,1)S(1)}, bf16[1,192,2048]{2,1,0:T(8,128)(2,1)S(1)}, u32[]{:S(2)}, u32[]{:S(2)}) collective-permute-start(bf16[1,192,2048]{2,1,0:T(8,128)(2,1)S(1)} %slice.73), channel_id=1, source_target_pairs={{0,4},{1,5},{2,6},{3,7},{4,0},{5,1},{6,2},{7,3},{8,12},{9,13},{10,... | collective-permute-start | bytes 2359304 | tf_op jit(solution)/shard_map/ppermute | solution.py:294
  45.7 24.8 %collective-permute-start.6 = (bf16[1,192,2048]{2,1,0:T(8,128)(2,1)S(1)}, bf16[1,192,2048]{2,1,0:T(8,128)(2,1)S(1)}, u32[]{:S(2)}, u32[]{:S(2)}) collective-permute-start(bf16[1,192,2048]{2,1,0:T(8,128)(2,1)S(1)} %slice.74), channel_id=1, source_target_pairs={{0,2},{1,3},{2,0},{3,1},{4,6},{5,7},{6,4},{7,5},{8,10},{9,11},{10,... | collective-permute-start | bytes 2359304 | tf_op jit(solution)/shard_map/ppermute | solution.py:294
  46.3 24.2 %collective-permute-start.7 = (bf16[128,2176]{1,0:T(8,128)(2,1)}, bf16[128,2176]{1,0:T(8,128)(2,1)S(1)}, u32[]{:S(2)}, u32[]{:S(2)}) collective-permute-start(bf16[128,2176]{1,0:T(8,128)(2,1)} %collective-permute-done.2), channel_id=1, source_target_pairs={{0,8},{8,16},{16,24},{24,0},{1,9},{9,17},{17,25},{25,1},{2,10},{10... | collective-permute-start | bytes 1671176 | tf_op jit(solution)/shard_map/ppermute | solution.py:297
  48.4 19.9 %collective-permute-start.8 = (bf16[1,96,1024]{2,1,0:T(8,128)(2,1)S(1)}, bf16[1,96,1024]{2,1,0:T(8,128)(2,1)S(1)}, u32[]{:S(2)}, u32[]{:S(2)}) collective-permute-start(bf16[1,96,1024]{2,1,0:T(8,128)(2,1)S(1)} %copy-done.18), channel_id=1, source_target_pairs={{0,8},{8,16},{16,24},{24,0},{1,9},{9,17},{17,25},{25,1},{2,10},{10... | collective-permute-start | bytes 589832 | tf_op jit(solution)/shard_map/ppermute | solution.py:297
  50.0 20.5 %collective-permute-start.9 = (bf16[1,96,1024]{2,1,0:T(8,128)(2,1)S(1)}, bf16[1,96,1024]{2,1,0:T(8,128)(2,1)S(1)}, u32[]{:S(2)}, u32[]{:S(2)}) collective-permute-start(bf16[1,96,1024]{2,1,0:T(8,128)(2,1)S(1)} %copy-done.16), channel_id=1, source_target_pairs={{0,24},{8,0},{16,8},{24,16},{1,25},{9,1},{17,9},{25,17},{2,26},{10... | collective-permute-start | bytes 589832 | tf_op jit(solution)/shard_map/ppermute | solution.py:297
  58.8 13.8 %copy-start.14 = (bf16[1,96,1024]{2,1,0:T(8,128)(2,1)S(1)}, bf16[1,96,1024]{2,1,0:T(8,128)(2,1)}, u32[]{:S(2)}) copy-start(bf16[1,96,1024]{2,1,0:T(8,128)(2,1)} %copy-done.13) | copy-start | bytes 589828
  58.8 14.6 %copy-start.12 = (bf16[1,96,1024]{2,1,0:T(8,128)(2,1)S(1)}, bf16[1,96,1024]{2,1,0:T(8,128)(2,1)}, u32[]{:S(2)}) copy-start(bf16[1,96,1024]{2,1,0:T(8,128)(2,1)} %copy-done.11) | copy-start | bytes 589828
  58.8 17.6 %copy-start.10 = (bf16[1,96,1024]{2,1,0:T(8,128)(2,1)S(1)}, bf16[1,96,1024]{2,1,0:T(8,128)(2,1)}, u32[]{:S(2)}) copy-start(bf16[1,96,1024]{2,1,0:T(8,128)(2,1)} %copy-done.9) | copy-start | bytes 589828
  72.0 4.4 %collective-permute-start.10 = (bf16[512,2176]{1,0:T(8,128)(2,1)S(1)}, bf16[512,2176]{1,0:T(8,128)(2,1)S(1)}, u32[]{:S(2)}, u32[]{:S(2)}) collective-permute-start(bf16[512,2176]{1,0:T(8,128)(2,1)S(1)} %get-tuple-element.174.refs_5_.refs_0_), channel_id=1, source_target_pairs={{0,1},{1,0},{2,3},{3,2},{4,5},{5,4},{6,7},{7,6},{8,9},{9,8},{10,11... | collective-permute-start | bytes 6684680 | tf_op jit(solution)/shard_map/ppermute | solution.py:294
  72.0 20.6 %copy-start.6 = (bf16[1,96,1024]{2,1,0:T(8,128)(2,1)S(1)}, bf16[1,96,1024]{2,1,0:T(8,128)(2,1)}, u32[]{:S(2)}) copy-start(bf16[1,96,1024]{2,1,0:T(8,128)(2,1)} %copy-done.5) | copy-start | bytes 589828
  72.1 20.6 %collective-permute-start.14 = (bf16[4,96,1024]{2,1,0:T(8,128)(2,1)S(1)}, bf16[4,96,1024]{2,1,0:T(8,128)(2,1)S(1)}, u32[]{:S(2)}, u32[]{:S(2)}) collective-permute-start(bf16[4,96,1024]{2,1,0:T(8,128)(2,1)S(1)} %get-tuple-element.158.refs_2_), channel_id=1, source_target_pairs={{0,1},{1,0},{2,3},{3,2},{4,5},{5,4},{6,7},{7,6},{8,9},{9,8},{10,11... | collective-permute-start | bytes 2359304 | tf_op jit(solution)/shard_map/ppermute | solution.py:294
  72.5 17.9 %collective-permute-start.11 = (bf16[1,96,1024]{2,1,0:T(8,128)(2,1)S(1)}, bf16[1,96,1024]{2,1,0:T(8,128)(2,1)S(1)}, u32[]{:S(2)}, u32[]{:S(2)}) collective-permute-start(bf16[1,96,1024]{2,1,0:T(8,128)(2,1)S(1)} %copy-done.14), channel_id=1, source_target_pairs={{0,8},{8,16},{16,24},{24,0},{1,9},{9,17},{17,25},{25,1},{2,10},{10... | collective-permute-start | bytes 589832 | tf_op jit(solution)/shard_map/ppermute | solution.py:297
  73.4 17.1 %collective-permute-start.12 = (bf16[1,96,1024]{2,1,0:T(8,128)(2,1)S(1)}, bf16[1,96,1024]{2,1,0:T(8,128)(2,1)S(1)}, u32[]{:S(2)}, u32[]{:S(2)}) collective-permute-start(bf16[1,96,1024]{2,1,0:T(8,128)(2,1)S(1)} %copy-done.12), channel_id=1, source_target_pairs={{0,24},{8,0},{16,8},{24,16},{1,25},{9,1},{17,9},{25,17},{2,26},{10... | collective-permute-start | bytes 589832 | tf_op jit(solution)/shard_map/ppermute | solution.py:297
  76.4 16.3 %collective-permute-start.13 = (bf16[1,96,1024]{2,1,0:T(8,128)(2,1)S(1)}, bf16[1,96,1024]{2,1,0:T(8,128)(2,1)S(1)}, u32[]{:S(2)}, u32[]{:S(2)}) collective-permute-start(bf16[1,96,1024]{2,1,0:T(8,128)(2,1)S(1)} %copy-done.10), channel_id=1, source_target_pairs={{0,16},{8,24},{16,0},{24,8},{1,17},{9,25},{17,1},{25,9},{2,18},{10... | collective-permute-start | bytes 589832 | tf_op jit(solution)/shard_map/ppermute | solution.py:297
  92.7 8.4 %collective-permute-start.16 = (bf16[4,192,1024]{2,1,0:T(8,128)(2,1)S(1)}, bf16[4,192,1024]{2,1,0:T(8,128)(2,1)S(1)}, u32[]{:S(2)}, u32[]{:S(2)}) collective-permute-start(bf16[4,192,1024]{2,1,0:T(8,128)(2,1)S(1)} %get-tuple-element.165), channel_id=1, source_target_pairs={{0,1},{1,0},{2,3},{3,2},{4,5},{5,4},{6,7},{7,6},{8,9},{9,8},{10,11... | collective-permute-start | bytes 4718600 | tf_op jit(solution)/shard_map/ppermute | solution.py:294
  92.8 8.3 %collective-permute-start.15 = (bf16[4,96,1024]{2,1,0:T(8,128)(2,1)S(1)}, bf16[4,96,1024]{2,1,0:T(8,128)(2,1)S(1)}, u32[]{:S(2)}, u32[]{:S(2)}) collective-permute-start(bf16[4,96,1024]{2,1,0:T(8,128)(2,1)S(1)} %constant_dynamic-update-slice_fusion.3.refs_2_), channel_id=1, source_target_pairs={{0,1},{1,0},{2,3},{3,2},{4,5},{5,4},{6,7},{7,6},{8,9},{9,8},{10,11... | collective-permute-start | bytes 2359304 | tf_op jit(solution)/shard_map/ppermute | solution.py:294
  101.0 22.3 %collective-permute-start.17 = (bf16[2,2,96,1024]{3,2,1,0:T(8,128)(2,1)S(1)}, bf16[2,2,96,1024]{3,2,1,0:T(8,128)(2,1)S(1)}, u32[]{:S(2)}, u32[]{:S(2)}) collective-permute-start(bf16[2,2,96,1024]{3,2,1,0:T(8,128)(2,1)S(1)} %get-tuple-element.170), channel_id=1, source_target_pairs={{0,2},{1,3},{2,0},{3,1},{4,6},{5,7},{6,4},{7,5},{8,10},{9,11},{10,... | collective-permute-start | bytes 2359304 | tf_op jit(solution)/shard_map/ppermute | solution.py:294
  102.6 20.7 %collective-permute-start.18 = (bf16[2,2,96,1024]{3,2,1,0:T(8,128)(2,1)S(1)}, bf16[2,2,96,1024]{3,2,1,0:T(8,128)(2,1)S(1)}, u32[]{:S(2)}, u32[]{:S(2)}) collective-permute-start(bf16[2,2,96,1024]{3,2,1,0:T(8,128)(2,1)S(1)} %get-tuple-element.172), channel_id=1, source_target_pairs={{0,4},{1,5},{2,6},{3,7},{4,0},{5,1},{6,2},{7,3},{8,12},{9,13},{10,... | collective-permute-start | bytes 2359304 | tf_op jit(solution)/shard_map/ppermute | solution.py:294
  104.4 12.3 %collective-permute-start.19 = (bf16[192,1024]{1,0:T(8,128)(2,1)S(1)}, bf16[192,1024]{1,0:T(8,128)(2,1)S(1)}, u32[]{:S(2)}, u32[]{:S(2)}) collective-permute-start(bf16[192,1024]{1,0:T(8,128)(2,1)S(1)} %get-tuple-element.213), channel_id=1, source_target_pairs={{0,24},{8,0},{16,8},{24,16},{1,25},{9,1},{17,9},{25,17},{2,26},{10... | collective-permute-start | bytes 1179656 | tf_op jit(solution)/shard_map/ppermute | solution.py:297
  105.6 17.7 %collective-permute-start.20 = (bf16[192,1024]{1,0:T(8,128)(2,1)S(1)}, bf16[192,1024]{1,0:T(8,128)(2,1)S(1)}, u32[]{:S(2)}, u32[]{:S(2)}) collective-permute-start(bf16[192,1024]{1,0:T(8,128)(2,1)S(1)} %get-tuple-element.211), channel_id=1, source_target_pairs={{0,8},{8,16},{16,24},{24,0},{1,9},{9,17},{17,25},{25,1},{2,10},{10... | collective-permute-start | bytes 1179656 | tf_op jit(solution)/shard_map/ppermute | solution.py:297
  123.6 26.5 %collective-permute-start.22 = (bf16[3,2,96,1024]{3,2,1,0:T(8,128)(2,1)S(1)}, bf16[3,2,96,1024]{3,2,1,0:T(8,128)(2,1)S(1)}, u32[]{:S(2)}, u32[]{:S(2)}) collective-permute-start(bf16[3,2,96,1024]{3,2,1,0:T(8,128)(2,1)S(1)} %pad_maximum_fusion.1), channel_id=1, source_target_pairs={{0,4},{1,5},{2,6},{3,7},{4,0},{5,1},{6,2},{7,3},{8,12},{9,13},{10,... | collective-permute-start | bytes 3538952 | tf_op jit(solution)/shard_map/ppermute | solution.py:294
  124.3 28.7 %copy-start.4 = (bf16[768,1024]{1,0:T(8,128)(2,1)S(1)}, bf16[768,1024]{1,0:T(8,128)(2,1)}, u32[]{:S(2)}) copy-start(bf16[768,1024]{1,0:T(8,128)(2,1)} %copy-done.3) | copy-start | bytes 4718596
  124.5 28.6 %copy-start.1 = (bf16[128,8,1536]{2,1,0:T(8,128)(2,1)S(1)}, bf16[128,8,1536]{2,1,0:T(8,128)(2,1)}, u32[]{:S(2)}) copy-start(bf16[128,8,1536]{2,1,0:T(8,128)(2,1)} %param.8) | copy-start | bytes 9437188
  124.6 28.5 %copy-start.8 = (f32[128,8]{0,1:T(8,128)S(1)}, f32[128,8]{0,1:T(8,128)}, u32[]{:S(2)}) copy-start(f32[128,8]{0,1:T(8,128)} %param.10) | copy-start | bytes 12292
  124.6 26.2 %collective-permute-start.21 = (bf16[3,2,96,1024]{3,2,1,0:T(8,128)(2,1)S(1)}, bf16[3,2,96,1024]{3,2,1,0:T(8,128)(2,1)S(1)}, u32[]{:S(2)}, u32[]{:S(2)}) collective-permute-start(bf16[3,2,96,1024]{3,2,1,0:T(8,128)(2,1)S(1)} %pad_maximum_fusion), channel_id=1, source_target_pairs={{0,2},{1,3},{2,0},{3,1},{4,6},{5,7},{6,4},{7,5},{8,10},{9,11},{10,... | collective-permute-start | bytes 3538952 | tf_op jit(solution)/shard_map/ppermute | solution.py:294
  125.3 18.3 %collective-permute-start.23 = (bf16[192,1024]{1,0:T(8,128)(2,1)S(1)}, bf16[192,1024]{1,0:T(8,128)(2,1)S(1)}, u32[]{:S(2)}, u32[]{:S(2)}) collective-permute-start(bf16[192,1024]{1,0:T(8,128)(2,1)S(1)} %get-tuple-element.194), channel_id=1, source_target_pairs={{0,16},{8,24},{16,0},{24,8},{1,17},{9,25},{17,1},{25,9},{2,18},{10... | collective-permute-start | bytes 1179656 | tf_op jit(solution)/shard_map/ppermute | solution.py:297
  151.0 8.4 %collective-permute-start.25 = (bf16[1,2,96,1024]{3,2,1,0:T(8,128)(2,1)S(1)}, bf16[1,2,96,1024]{3,2,1,0:T(8,128)(2,1)S(1)}, u32[]{:S(2)}, u32[]{:S(2)}) collective-permute-start(bf16[1,2,96,1024]{3,2,1,0:T(8,128)(2,1)S(1)} %add_convert_fusion), channel_id=1, source_target_pairs={{0,2},{1,3},{2,0},{3,1},{4,6},{5,7},{6,4},{7,5},{8,10},{9,11},{10,... | collective-permute-start | bytes 1179656 | tf_op jit(solution)/shard_map/ppermute | solution.py:294
  151.8 8.1 %collective-permute-start.24 = (bf16[1,2,96,1024]{3,2,1,0:T(8,128)(2,1)S(1)}, bf16[1,2,96,1024]{3,2,1,0:T(8,128)(2,1)S(1)}, u32[]{:S(2)}, u32[]{:S(2)}) collective-permute-start(bf16[1,2,96,1024]{3,2,1,0:T(8,128)(2,1)S(1)} %add_convert_fusion.1), channel_id=1, source_target_pairs={{0,4},{1,5},{2,6},{3,7},{4,0},{5,1},{6,2},{7,3},{8,12},{9,13},{10,... | collective-permute-start | bytes 1179656 | tf_op jit(solution)/shard_map/ppermute | solution.py:294
